TPU v7x, 512 devices: a whole 4x4x16 slice. The times are simulated.
512 devices in a mesh: dp: 16 (over z), ctx: 32 (over y, x, core).
Axes of the slice: x: 4, y: 4, z: 16, core: 2. Of those that a mesh axis runs over, the one named last changes fastest.
Arguments:
- query_matrix: bfloat16 [65536, 1280], P(('dp', 'ctx')), parts along dimension 0, may hold values from -6 to 6
- address_matrix: bfloat16 [65536, 1280], P(('dp', 'ctx')), parts along dimension 0, may hold values from -6 to 6
- content_matrix: bfloat16 [65536, 1280], P(('dp', 'ctx')), parts along dimension 0, may hold values from -24 to 24
- erasure_vector_raw: bfloat16 [65536, 1280], P(('dp', 'ctx')), parts along dimension 0, may hold values from -16 to 16
- erasure_strength: bfloat16 [65536, 1280], P(('dp', 'ctx')), parts along dimension 0, may hold values from 0 to 1
- forgetting_exponent: bfloat16 [65536, 1280], P(('dp', 'ctx')), parts along dimension 0, may hold values from -0.5 to 0
- initial_memory_matrix: float32 [1024, 1280], P('dp', 'ctx'), parts along dimension 0, may hold values from -384 to 384
- diagonal_boost_vector: float32 [1280], replicated, may hold values from -0.5 to 0.5
- layernorm_multiplier: float32 [1280], replicated, may hold values from 0.1 to 1.9
- layernorm_shift_vector: float32 [1280], replicated, may hold values from -2 to 2
Outputs:
- ungated_result: bfloat16 [65536, 1280], P(('dp', 'ctx')), parts along dimension 0
- exit_state: float32 [1024, 1280], P('dp', 'ctx'), parts along dimension 0
There are 16 independent parts, one for each index of `dp`. A program takes and returns all parts, laid end to end along the dimension named above; an argument that names none is the same for every part. Nothing has to cross between parts.
All inputs are finite; a program needn't handle non-finite values.
Results may differ from a plain program's by a relative error of at most 0.001.
Values sent between devices are 32-bit elements; how exact they have to be, the bound alone decides.
No kernel may reach another device: no remote copies, remote signals or barrier semaphores. Data moves between devices by JAX's collectives and lax.ppermute only.
A program may use at most 128 MiB of HBM per device.

v0:
```python
import functools

import jax
import jax.numpy as jnp
from jax import lax
from jax.experimental import pallas as pl
from jax.experimental.pallas import tpu as pltpu
from jax.sharding import PartitionSpec as P

HEADS = 20
CH = 64
PAIR = 2 * CH
PAIRS = HEADS // 2
WIDTH = HEADS * CH
GROUP = 5
INTERPRET = False
F32 = jnp.float32
BF16 = jnp.bfloat16
NN = (((1,), (0,)), ((), ()))
NT = (((1,), (1,)), ((), ()))


def mxu(a, b, dims=NN):
    return lax.dot_general(a, b, dims, preferred_element_type=F32)


def split(x):
    hi = x.astype(BF16)
    return hi, (x - hi.astype(F32)).astype(BF16)


def lanes(*xs):
    return jnp.concatenate(xs, axis=1)


def rows(*xs):
    return jnp.concatenate(xs, axis=0)


def square(a, b):
    both = lanes(*b)
    out = mxu(lanes(*a), rows(both, both))
    return out[:, :PAIR] + out[:, PAIR:]


def wide(a, b):
    return mxu(lanes(*a), rows(b[0], b[0])) + mxu(a[0], b[1])


def exact_right(a, b):
    return mxu(lanes(*a), rows(b, b))


def iota(shape, dim):
    return lax.broadcasted_iota(jnp.int32, shape, dim)


def low_half(n):
    return iota((n, PAIR), 1) < CH


def block_ones():
    same = (iota((PAIR, PAIR), 0) < CH) == (iota((PAIR, PAIR), 1) < CH)
    return jnp.where(same, 1.0, 0.0).astype(BF16)


def head_sum(x, ones):
    return exact_right(split(x), ones)


def decays(logs, tril):
    return mxu(tril, logs)


def units(raw, ones):
    raw = raw.astype(F32)
    return raw * lax.rsqrt(head_sum(raw * raw, ones) + CH * 1e-05)


def tril_ones(n):
    return jnp.where(iota((n, n), 0) >= iota((n, n), 1), 1.0, 0.0).astype(BF16)


def grams(left, right, low):
    zero = jnp.zeros_like(left)
    stacked = split(rows(jnp.where(low, left, zero), jnp.where(low, zero, left)))
    b = split(right)
    return mxu(lanes(*stacked), lanes(b[0], b[0]), NT) + mxu(stacked[0], b[1], NT)


def local_kernel(
    k_ref, v_ref, raw_ref, rate_ref, log_ref, slots_ref, w_ref, u_ref, moves, ends, *, owners, columns
):
    n = k_ref.shape[0]
    step = pl.program_id(0)
    low = low_half(n)
    ones = block_ones()
    tril = tril_ones(n)
    t_id, s_id = iota((n, n), 0), iota((n, n), 1)
    strict = t_id > s_id
    apart = t_id ^ s_id
    pairs = range(GROUP)
    cut = [slice(p * PAIR, (p + 1) * PAIR) for p in pairs]

    cumul = [decays(log_ref[:, c], tril) for c in cut]
    unit = [units(raw_ref[:, c], ones) for c in cut]
    alpha = [-unit[p] * jnp.exp(cumul[p] - log_ref[:, cut[p]].astype(F32)) for p in pairs]
    fall = [jnp.exp(-cumul[p]) for p in pairs]
    beta = [rate_ref[:, cut[p]].astype(F32) * unit[p] * fall[p] for p in pairs]
    key = [k_ref[:, cut[p]].astype(F32) * fall[p] for p in pairs]
    gram = [grams(alpha[p], rows(beta[p], key[p]), low) for p in pairs]

    heads = range(2 * GROUP)
    inner, cross = [], []
    for h in heads:
        part = gram[h // 2][(h % 2) * n : (h % 2 + 1) * n]
        inner.append(jnp.where(strict, part[:, :n], 0.0))
        cross.append(jnp.where(strict, part[:, n:], 0.0))
    akv = [exact_right(split(cross[h]), v_ref[:, cut[h // 2]]) for h in heads]
    akv = [jnp.where(low, akv[2 * p], akv[2 * p + 1]) for p in pairs]
    right = [split(lanes(alpha[p], akv[p])) for p in pairs]

    eye = jnp.where(t_id == s_id, 1.0, 0.0)
    solver = [eye + jnp.where(apart == 1, inner[h], 0.0) for h in heads]
    size = 2
    while size < n:
        joins = (apart >= size) & (apart < 2 * size)
        halves = [split(solver[h]) for h in heads]
        mid = [square(split(jnp.where(joins, inner[h], 0.0)), halves[h]) for h in heads]
        solver = [solver[h] + square(halves[h], split(mid[h])) for h in heads]
        size *= 2
    solved = [wide(split(solver[h]), right[h // 2]) for h in heads]
    for p in pairs:
        first, second = solved[2 * p], solved[2 * p + 1]
        w = jnp.where(low, first[:, :PAIR], second[:, :PAIR])
        u = jnp.where(low, first[:, PAIR:], second[:, PAIR:])
        w_ref[:, cut[p]] = w
        u_ref[:, cut[p]] = u
        scale = jnp.exp(cumul[p][n - 1 :, :])
        end_b = beta[p] * scale
        end_k = key[p] * scale
        moved = square(split(end_b.T), split(w))
        row, lane = iota((CH, PAIR), 0), iota((CH, PAIR), 1)
        diagonal = jnp.where(row == lane % CH, scale, 0.0)
        moves[step * GROUP + p] = jnp.where(low_half(CH), moved[:CH], moved[CH:]) + diagonal
        content = v_ref[:, cut[p]].astype(F32).T.astype(BF16)
        by_key = mxu(content, lanes(*split(end_k)))
        fresh = square(split(u.T), split(end_b)) + by_key[:, :PAIR] + by_key[:, PAIR:]
        own = (iota((PAIR, PAIR), 0) < CH) == low_half(PAIR)
        fresh = jnp.where(own, fresh, 0.0)
        ends[pl.ds(pl.multiple_of((step * GROUP + p) * PAIR, PAIR), PAIR), :] = fresh + pltpu.roll(
            fresh, CH, 1
        )

    @pl.when(step == pl.num_programs(0) - 1)
    def _():
        ends[WIDTH:, :] = jnp.zeros((ends.shape[0] - WIDTH, PAIR), F32)
        short = (columns + 15) // 16 * 8
        for owner in range(owners):
            first = owner * columns // CH
            if first % 2 == 0 or first == HEADS - 1:
                slot = moves[first // 2]
            else:
                slot = jnp.where(low_half(CH), moves[first // 2 + 1], moves[first // 2])
            slots_ref[owner, :CH, :] = slot
            at = owner * columns
            slots_ref[owner, CH:, :] = jnp.where(
                low_half(short), ends[at : at + short, :], ends[at + short : at + 2 * short, :]
            )


def read_kernel(
    q_ref, k_ref, v_ref, raw_ref, rate_ref, log_ref, w_ref, u_ref, boost_ref, shift_ref,
    read_ref, local_ref, base_ref,
):
    n = k_ref.shape[0]
    low = low_half(n)
    ones = block_ones()
    tril = tril_ones(n)
    weak = iota((n, n), 0) >= iota((n, n), 1)
    pairs = range(GROUP)
    cut = [slice(p * PAIR, (p + 1) * PAIR) for p in pairs]

    cumul = [decays(log_ref[:, c], tril) for c in cut]
    unit = [units(raw_ref[:, c], ones) for c in cut]
    fall = [jnp.exp(-cumul[p]) for p in pairs]
    beta = [rate_ref[:, cut[p]].astype(F32) * unit[p] * fall[p] for p in pairs]
    key = [k_ref[:, cut[p]].astype(F32) * fall[p] for p in pairs]
    read = [q_ref[:, cut[p]].astype(F32) * jnp.exp(cumul[p]) for p in pairs]
    gram = [grams(read[p], rows(beta[p], key[p]), low) for p in pairs]
    for p in pairs:
        c = cut[p]
        solved = split(lanes(w_ref[:, c], u_ref[:, c]))
        v = v_ref[:, c]
        reads, locals_ = [], []
        for h in range(2):
            part = gram[p][h * n : (h + 1) * n]
            both = wide(split(jnp.where(weak, part[:, :n], 0.0)), solved)
            direct = exact_right(split(jnp.where(weak, part[:, n:], 0.0)), v)
            reads.append(both[:, :PAIR])
            locals_.append(both[:, PAIR:] + direct)
        read_ref[:, c] = read[p] + jnp.where(low, *reads)
        local_ref[:, c] = jnp.where(low, *locals_)
        product = q_ref[:, c].astype(F32) * k_ref[:, c].astype(F32) * boost_ref[:, c]
        base_ref[:, c] = head_sum(product, ones) * v.astype(F32) + shift_ref[:, c]


def scan_kernel(slots_ref, entry_ref, mask_ref, starts_ref, exit_ref):
    short = starts_ref.shape[1]
    low = low_half(short)
    mask = mask_ref[...]
    state = entry_ref[...]
    for d in range(slots_ref.shape[0]):
        starts_ref[d] = jnp.where(low, state[:short], state[short:])
        hi, lo = split(slots_ref[d, :CH, :])
        weights = rows(lanes(hi, hi), lanes(hi, hi), lanes(lo, lo), lanes(lo, lo))
        end = slots_ref[d, CH:, :]
        turned = pltpu.roll(end, CH, 1)
        fresh = rows(jnp.where(low, end, turned), jnp.where(low, turned, end))
        out = mxu(lanes(*split(state * mask)), weights, NT)
        state = out[:, :PAIR] + out[:, PAIR:] + fresh
    exit_ref[...] = state


def final_kernel(starts_ref, read_ref, local_ref, base_ref, gain_ref, out_ref, begins, *, columns):
    short = starts_ref.shape[1]
    low = low_half(short)
    for owner in range(starts_ref.shape[0]):
        part = starts_ref[owner]
        turned = pltpu.roll(part, CH, 1)
        at = owner * columns
        begins[at : at + short, :] = jnp.where(low, part, turned)
        begins[at + short : at + columns, :] = jnp.where(low, turned, part)[: columns - short]
    own = (iota((PAIR, PAIR), 0) < CH) == low_half(PAIR)
    ones = block_ones()
    for p in range(PAIRS):
        c = slice(p * PAIR, (p + 1) * PAIR)
        a = split(read_ref[:, c])
        b = split(jnp.where(own, begins[c, :], 0.0))
        carried = mxu(lanes(*a), lanes(b[0], b[0]), NT) + mxu(a[0], b[1], NT)
        readout = carried + local_ref[:, c]
        centred = readout - head_sum(readout, ones) * (1.0 / CH)
        variance = head_sum(centred * centred, ones) * (1.0 / CH)
        scaled = centred * lax.rsqrt(variance + 1e-05) * gain_ref[:, c]
        out_ref[:, c] = (scaled + base_ref[:, c]).astype(BF16)


def call(kernel, **kwargs):
    params = pltpu.CompilerParams(vmem_limit_bytes=48 * 1024 * 1024)
    return pl.pallas_call(kernel, interpret=INTERPRET, compiler_params=params, **kwargs)


def shards(q, k, v, raw, rates, logs, memory, boost, gain, shift):
    n = q.shape[0]
    owners = lax.axis_size("ctx")
    columns = memory.shape[1]
    short = (columns + 15) // 16 * 8
    block = GROUP * PAIR
    tokens = pl.BlockSpec((n, block), lambda i: (0, i))
    vector = pl.BlockSpec((1, block), lambda i: (0, i))
    steps = WIDTH // block
    plane = jax.ShapeDtypeStruct((n, WIDTH), F32)

    slots, w, u = call(
        functools.partial(local_kernel, owners=owners, columns=columns),
        grid=(steps,),
        in_specs=[tokens] * 5,
        out_specs=[
            pl.BlockSpec((owners, CH + short, PAIR), lambda i: (0, 0, 0)),
            tokens,
            tokens,
        ],
        out_shape=[jax.ShapeDtypeStruct((owners, CH + short, PAIR), F32), plane, plane],
        scratch_shapes=[
            pltpu.VMEM((PAIRS, CH, PAIR), F32),
            pltpu.VMEM((WIDTH + 8, PAIR), F32),
        ],
    )(k, v, raw, rates, logs)
    slots = lax.all_to_all(slots, "ctx", 0, 0)

    read, local, base = call(
        read_kernel,
        grid=(steps,),
        in_specs=[tokens] * 8 + [vector] * 2,
        out_specs=[tokens] * 3,
        out_shape=[plane] * 3,
    )(q, k, v, raw, rates, logs, w, u, boost.reshape(1, WIDTH), shift.reshape(1, WIDTH))

    place = lax.axis_index("ctx")
    own = lax.broadcasted_iota(jnp.int32, (2 * short, PAIR), 0)
    half = lax.broadcasted_iota(jnp.int32, (2 * short, PAIR), 1) // CH
    mask = ((place * columns + own) // CH % 2 == half) & (own < columns)
    entry = jnp.pad(memory.T, ((0, 2 * short - columns), (0, 0)))
    starts, final = call(
        scan_kernel,
        out_shape=[
            jax.ShapeDtypeStruct((owners, short, PAIR), F32),
            jax.ShapeDtypeStruct((2 * short, PAIR), F32),
        ],
    )(slots, jnp.concatenate([entry, entry], axis=1), mask.astype(F32))
    starts = lax.all_to_all(starts, "ctx", 0, 0)
    exit_state = final[:columns, :CH].T

    out = call(
        functools.partial(final_kernel, columns=columns),
        out_shape=jax.ShapeDtypeStruct((n, WIDTH), BF16),
        scratch_shapes=[pltpu.VMEM((WIDTH, PAIR), F32)],
    )(starts, read, local, base, gain.reshape(1, WIDTH))
    return out, exit_state


def solution(mesh):
    rows_spec = P(("dp", "ctx"), None)
    return jax.shard_map(
        shards,
        mesh=mesh,
        in_specs=(rows_spec,) * 6 + (P("dp", "ctx"), P(), P(), P()),
        out_specs=(rows_spec, P("dp", "ctx")),
        check_vma=False,
    )
```

profile of v0, /device:TPU:1, one launch (start us, length us, event | category | flops | bytes accessed | tf_op | source)
XLA Modules:
  0.0 75.4 jit_solution(11500953617010347491)
XLA Ops:
  0.6 0.0 copy-start
  0.6 1.0 %copy-done = bf16[128,1280]{1,0:T(8,128)(2,1)S(1)} copy-done((bf16[128,1280]{1,0:T(8,128)(2,1)S(1)}, bf16[128,1280]{1,0:T(8,128)(2,1)}, u32[]{:S(2)}) %copy-start) | copy-done | bytes 327704
  1.6 1.0 %copy-done.2 = bf16[128,1280]{1,0:T(8,128)(2,1)S(1)} copy-done((bf16[128,1280]{1,0:T(8,128)(2,1)S(1)}, bf16[128,1280]{1,0:T(8,128)(2,1)}, u32[]{:S(2)}) %copy-start.2) | copy-done | bytes 327704
  2.6 1.0 %copy-done.4 = bf16[128,1280]{1,0:T(8,128)(2,1)S(1)} copy-done((bf16[128,1280]{1,0:T(8,128)(2,1)S(1)}, bf16[128,1280]{1,0:T(8,128)(2,1)}, u32[]{:S(2)}) %copy-start.4) | copy-done | bytes 327704
  3.6 1.0 %copy-done.6 = bf16[128,1280]{1,0:T(8,128)(2,1)S(1)} copy-done((bf16[128,1280]{1,0:T(8,128)(2,1)S(1)}, bf16[128,1280]{1,0:T(8,128)(2,1)}, u32[]{:S(2)}) %copy-start.6) | copy-done | bytes 327704
  4.5 1.0 %copy-done.8 = bf16[128,1280]{1,0:T(8,128)(2,1)S(1)} copy-done((bf16[128,1280]{1,0:T(8,128)(2,1)S(1)}, bf16[128,1280]{1,0:T(8,128)(2,1)}, u32[]{:S(2)}) %copy-start.8) | copy-done | bytes 327704
  5.5 9.3 %shard_map.113 = (f32[32,88,128]{2,1,0:T(8,128)}, f32[128,1280]{1,0:T(8,128)S(1)}, f32[128,1280]{1,0:T(8,128)S(1)}) custom-call(bf16[128,1280]{1,0:T(8,128)(2,1)S(1)} %copy-done, bf16[128,1280]{1,0:T(8,128)(2,1)S(1)} %copy-done.2, bf16[128,1280]{1,0:T(8,128)(2,1)S(1)} %copy-done.4, bf16[128,1280]{1,0:T(8,128)(2,1)S(1)} %copy-done.6, ...), custom_call_target="tpu_custom_call" | custom-call | tf_op jit(solution)/shard_map/pallas_call | solution.py:264
  14.8 0.8 %copy-done.10 = f32[128,1280]{1,0:T(8,128)} copy-done((f32[128,1280]{1,0:T(8,128)}, f32[128,1280]{1,0:T(8,128)S(1)}, u32[]{:S(2)}) %copy-start.10) | copy-done | bytes 655384
  15.7 0.9 %copy-done.12 = f32[128,1280]{1,0:T(8,128)} copy-done((f32[128,1280]{1,0:T(8,128)}, f32[128,1280]{1,0:T(8,128)S(1)}, u32[]{:S(2)}) %copy-start.12) | copy-done | bytes 655384
  16.5 10.6 %all-to-all-start = ((f32[32,88,128]{2,1,0:T(8,128)}), f32[32,88,128]{2,1,0:T(8,128)S(1)}, u32[]{:S(2)}, u32[]{:S(2)}) async-start(f32[32,88,128]{2,1,0:T(8,128)} %get-tuple-element.10), calls=%async_computation | async-start | bytes 2883584 | tf_op jit(solution)/shard_map/all_to_all | solution.py:279
  27.2 0.0 copy-start.22
  27.2 0.0 copy-start.23
  27.2 0.0 copy-start.24
  27.2 0.0 copy-start.1
  27.2 0.0 copy-start.3
  27.2 0.0 copy-start.5
  27.2 0.0 copy-start.7
  27.3 0.0 copy-start.9
  27.3 0.0 copy-start.20
  27.3 0.0 copy-done.21
  27.4 0.1 pad_maximum_fusion.entry_ref
  27.4 0.1 fusion.3.mask_ref
  27.5 20.3 %all-to-all-done.slots_ref = f32[32,88,128]{2,1,0:T(8,128)S(1)} async-done(((f32[32,88,128]{2,1,0:T(8,128)}), f32[32,88,128]{2,1,0:T(8,128)S(1)}, u32[]{:S(2)}, u32[]{:S(2)}) %all-to-all-start) | async-done | bytes 1441824 | tf_op jit(solution)/shard_map/all_to_all | solution.py:279
  47.8 4.6 %shard_map.114 = (f32[32,24,128]{2,1,0:T(8,128)}, f32[48,128]{1,0:T(8,128)S(1)}) custom-call(f32[32,88,128]{2,1,0:T(8,128)S(1)} %all-to-all-done.slots_ref, f32[48,128]{1,0:T(8,128)S(1)} %pad_maximum_fusion.entry_ref, f32[48,128]{1,0:T(8,128)S(1)} %fusion.3.mask_ref), custom_call_target="tpu_custom_call" | custom-call | tf_op jit(solution)/shard_map/pallas_call | solution.py:294
  52.5 5.6 %all-to-all-start.1 = ((f32[32,24,128]{2,1,0:T(8,128)}), f32[32,24,128]{2,1,0:T(8,128)S(1)}, u32[]{:S(2)}, u32[]{:S(2)}) async-start(f32[32,24,128]{2,1,0:T(8,128)} %get-tuple-element.11), calls=%async_computation.1 | async-start | bytes 786432 | tf_op jit(solution)/shard_map/all_to_all | solution.py:301
  58.0 0.0 copy-done.22
  58.0 0.0 copy-done.23
  58.1 0.0 copy-done.24
  58.1 0.0 copy-done.1
  58.1 0.0 copy-done.3
  58.1 0.0 copy-done.5
  58.1 0.0 copy-done.7
  58.1 0.0 copy-done.9
  58.1 0.0 copy-done.20
  58.2 0.0 copy-start.11
  58.2 1.1 %copy-done.11 = f32[128,1280]{1,0:T(8,128)S(1)} copy-done((f32[128,1280]{1,0:T(8,128)S(1)}, f32[128,1280]{1,0:T(8,128)}, u32[]{:S(2)}) %copy-start.11) | copy-done | bytes 655384
  59.2 1.1 %copy-done.13 = f32[128,1280]{1,0:T(8,128)S(1)} copy-done((f32[128,1280]{1,0:T(8,128)S(1)}, f32[128,1280]{1,0:T(8,128)}, u32[]{:S(2)}) %copy-start.13) | copy-done | bytes 655384
  60.3 3.3 %shard_map.115 = (f32[128,1280]{1,0:T(8,128)S(1)}, f32[128,1280]{1,0:T(8,128)S(1)}, f32[128,1280]{1,0:T(8,128)S(1)}) custom-call(bf16[128,1280]{1,0:T(8,128)(2,1)S(1)} %copy-done.20, bf16[128,1280]{1,0:T(8,128)(2,1)S(1)} %copy-done.1, bf16[128,1280]{1,0:T(8,128)(2,1)S(1)} %copy-done.3, bf16[128,1280]{1,0:T(8,128)(2,1)S(1)} %copy-done.5, ...), custom_call_target="tpu_custom_call" | custom-call | tf_op jit(solution)/shard_map/pallas_call | solution.py:281
  63.7 0.0 copy-start.14
  63.7 0.8 %copy-done.14 = f32[128,1280]{1,0:T(8,128)} copy-done((f32[128,1280]{1,0:T(8,128)}, f32[128,1280]{1,0:T(8,128)S(1)}, u32[]{:S(2)}) %copy-start.14) | copy-done | bytes 655384
  64.5 0.9 %copy-done.16 = f32[128,1280]{1,0:T(8,128)} copy-done((f32[128,1280]{1,0:T(8,128)}, f32[128,1280]{1,0:T(8,128)S(1)}, u32[]{:S(2)}) %copy-start.16) | copy-done | bytes 655384
  65.4 0.8 %copy-done.18 = f32[128,1280]{1,0:T(8,128)} copy-done((f32[128,1280]{1,0:T(8,128)}, f32[128,1280]{1,0:T(8,128)S(1)}, u32[]{:S(2)}) %copy-start.18) | copy-done | bytes 655384
  66.2 0.6 slice_bitcast_fusion
  66.8 1.5 %all-to-all-done.1.starts_ref = f32[32,24,128]{2,1,0:T(8,128)S(1)} async-done(((f32[32,24,128]{2,1,0:T(8,128)}), f32[32,24,128]{2,1,0:T(8,128)S(1)}, u32[]{:S(2)}, u32[]{:S(2)}) %all-to-all-start.1) | async-done | bytes 393248 | tf_op jit(solution)/shard_map/all_to_all | solution.py:301
  68.3 1.1 %copy-done.15 = f32[128,1280]{1,0:T(8,128)S(1)} copy-done((f32[128,1280]{1,0:T(8,128)S(1)}, f32[128,1280]{1,0:T(8,128)}, u32[]{:S(2)}) %copy-start.15) | copy-done | bytes 655384
  69.4 1.1 %copy-done.17 = f32[128,1280]{1,0:T(8,128)S(1)} copy-done((f32[128,1280]{1,0:T(8,128)S(1)}, f32[128,1280]{1,0:T(8,128)}, u32[]{:S(2)}) %copy-start.17) | copy-done | bytes 655384
  70.5 1.1 %copy-done.19 = f32[128,1280]{1,0:T(8,128)S(1)} copy-done((f32[128,1280]{1,0:T(8,128)S(1)}, f32[128,1280]{1,0:T(8,128)}, u32[]{:S(2)}) %copy-start.19) | copy-done | bytes 655384
  71.6 3.8 %shard_map.116 = bf16[128,1280]{1,0:T(8,128)(2,1)} custom-call(f32[32,24,128]{2,1,0:T(8,128)S(1)} %all-to-all-done.1.starts_ref, f32[128,1280]{1,0:T(8,128)S(1)} %copy-done.15, f32[128,1280]{1,0:T(8,128)S(1)} %copy-done.17, f32[128,1280]{1,0:T(8,128)S(1)} %copy-done.19, f32[1,1280]{1,0:T(1,128)S(1)} %reshape.15.gain_ref), custom_call_target="tpu_custom_call" | custom-call | tf_op jit(solution)/shard_map/pallas_call | solution.py:304
  (21 shorter events, 0.1 us)
Async XLA Ops:
  0.6 1.0 %copy-start = (bf16[128,1280]{1,0:T(8,128)(2,1)S(1)}, bf16[128,1280]{1,0:T(8,128)(2,1)}, u32[]{:S(2)}) copy-start(bf16[128,1280]{1,0:T(8,128)(2,1)} %k_ref.3) | copy-start | bytes 983044
  1.6 1.0 %copy-start.2 = (bf16[128,1280]{1,0:T(8,128)(2,1)S(1)}, bf16[128,1280]{1,0:T(8,128)(2,1)}, u32[]{:S(2)}) copy-start(bf16[128,1280]{1,0:T(8,128)(2,1)} %v_ref.3) | copy-start | bytes 983044
  2.6 1.0 %copy-start.4 = (bf16[128,1280]{1,0:T(8,128)(2,1)S(1)}, bf16[128,1280]{1,0:T(8,128)(2,1)}, u32[]{:S(2)}) copy-start(bf16[128,1280]{1,0:T(8,128)(2,1)} %raw_ref.3) | copy-start | bytes 983044
  3.6 1.0 %copy-start.6 = (bf16[128,1280]{1,0:T(8,128)(2,1)S(1)}, bf16[128,1280]{1,0:T(8,128)(2,1)}, u32[]{:S(2)}) copy-start(bf16[128,1280]{1,0:T(8,128)(2,1)} %rate_ref.3) | copy-start | bytes 983044
  4.5 1.0 %copy-start.8 = (bf16[128,1280]{1,0:T(8,128)(2,1)S(1)}, bf16[128,1280]{1,0:T(8,128)(2,1)}, u32[]{:S(2)}) copy-start(bf16[128,1280]{1,0:T(8,128)(2,1)} %log_ref.3) | copy-start | bytes 983044
  14.8 0.8 %copy-start.10 = (f32[128,1280]{1,0:T(8,128)}, f32[128,1280]{1,0:T(8,128)S(1)}, u32[]{:S(2)}) copy-start(f32[128,1280]{1,0:T(8,128)S(1)} %get-tuple-element.12.w_ref) | copy-start | bytes 1966084
  15.7 0.9 %copy-start.12 = (f32[128,1280]{1,0:T(8,128)}, f32[128,1280]{1,0:T(8,128)S(1)}, u32[]{:S(2)}) copy-start(f32[128,1280]{1,0:T(8,128)S(1)} %get-tuple-element.13.u_ref) | copy-start | bytes 1966084
  16.5 10.7 %copy-start.21 = (f32[64,40]{0,1:T(8,128)S(1)}, f32[64,40]{0,1:T(8,128)}, u32[]{:S(2)}) copy-start(f32[64,40]{0,1:T(8,128)} %param.16) | copy-start | bytes 30724
  16.5 31.3 %all-to-all-start = ((f32[32,88,128]{2,1,0:T(8,128)}), f32[32,88,128]{2,1,0:T(8,128)S(1)}, u32[]{:S(2)}, u32[]{:S(2)}) async-start(f32[32,88,128]{2,1,0:T(8,128)} %get-tuple-element.10), calls=%async_computation | async-start | bytes 2883584 | tf_op jit(solution)/shard_map/all_to_all | solution.py:279
  27.2 30.9 %copy-start.22 = (f32[1280]{0:T(1024)S(1)}, f32[1280]{0:T(1024)}, u32[]{:S(2)}) copy-start(f32[1280]{0:T(1024)} %param.17) | copy-start | bytes 15364
  27.2 30.9 %copy-start.23 = (f32[1280]{0:T(1024)S(1)}, f32[1280]{0:T(1024)}, u32[]{:S(2)}) copy-start(f32[1280]{0:T(1024)} %param.19) | copy-start | bytes 15364
  27.2 30.9 %copy-start.24 = (f32[1280]{0:T(1024)S(1)}, f32[1280]{0:T(1024)}, u32[]{:S(2)}) copy-start(f32[1280]{0:T(1024)} %param.18) | copy-start | bytes 15364
  27.2 30.9 %copy-start.1 = (bf16[128,1280]{1,0:T(8,128)(2,1)S(1)}, bf16[128,1280]{1,0:T(8,128)(2,1)}, u32[]{:S(2)}) copy-start(bf16[128,1280]{1,0:T(8,128)(2,1)} %k_ref.3) | copy-start | bytes 983044
  27.2 30.9 %copy-start.3 = (bf16[128,1280]{1,0:T(8,128)(2,1)S(1)}, bf16[128,1280]{1,0:T(8,128)(2,1)}, u32[]{:S(2)}) copy-start(bf16[128,1280]{1,0:T(8,128)(2,1)} %v_ref.3) | copy-start | bytes 983044
  27.2 30.9 %copy-start.5 = (bf16[128,1280]{1,0:T(8,128)(2,1)S(1)}, bf16[128,1280]{1,0:T(8,128)(2,1)}, u32[]{:S(2)}) copy-start(bf16[128,1280]{1,0:T(8,128)(2,1)} %raw_ref.3) | copy-start | bytes 983044
  27.2 30.9 %copy-start.7 = (bf16[128,1280]{1,0:T(8,128)(2,1)S(1)}, bf16[128,1280]{1,0:T(8,128)(2,1)}, u32[]{:S(2)}) copy-start(bf16[128,1280]{1,0:T(8,128)(2,1)} %rate_ref.3) | copy-start | bytes 983044
  27.3 30.9 %copy-start.9 = (bf16[128,1280]{1,0:T(8,128)(2,1)S(1)}, bf16[128,1280]{1,0:T(8,128)(2,1)}, u32[]{:S(2)}) copy-start(bf16[128,1280]{1,0:T(8,128)(2,1)} %log_ref.3) | copy-start | bytes 983044
  27.3 30.9 %copy-start.20 = (bf16[128,1280]{1,0:T(8,128)(2,1)S(1)}, bf16[128,1280]{1,0:T(8,128)(2,1)}, u32[]{:S(2)}) copy-start(bf16[128,1280]{1,0:T(8,128)(2,1)} %q_ref.1) | copy-start | bytes 983044
  52.5 15.8 %all-to-all-start.1 = ((f32[32,24,128]{2,1,0:T(8,128)}), f32[32,24,128]{2,1,0:T(8,128)S(1)}, u32[]{:S(2)}, u32[]{:S(2)}) async-start(f32[32,24,128]{2,1,0:T(8,128)} %get-tuple-element.11), calls=%async_computation.1 | async-start | bytes 786432 | tf_op jit(solution)/shard_map/all_to_all | solution.py:301
  58.2 1.1 %copy-start.11 = (f32[128,1280]{1,0:T(8,128)S(1)}, f32[128,1280]{1,0:T(8,128)}, u32[]{:S(2)}) copy-start(f32[128,1280]{1,0:T(8,128)} %copy-done.10) | copy-start | bytes 1966084
  59.2 1.1 %copy-start.13 = (f32[128,1280]{1,0:T(8,128)S(1)}, f32[128,1280]{1,0:T(8,128)}, u32[]{:S(2)}) copy-start(f32[128,1280]{1,0:T(8,128)} %copy-done.12) | copy-start | bytes 1966084
  63.7 0.8 %copy-start.14 = (f32[128,1280]{1,0:T(8,128)}, f32[128,1280]{1,0:T(8,128)S(1)}, u32[]{:S(2)}) copy-start(f32[128,1280]{1,0:T(8,128)S(1)} %get-tuple-element.14.read_ref) | copy-start | bytes 1966084
  64.5 0.9 %copy-start.16 = (f32[128,1280]{1,0:T(8,128)}, f32[128,1280]{1,0:T(8,128)S(1)}, u32[]{:S(2)}) copy-start(f32[128,1280]{1,0:T(8,128)S(1)} %get-tuple-element.15.local_ref) | copy-start | bytes 1966084
  65.4 0.8 %copy-start.18 = (f32[128,1280]{1,0:T(8,128)}, f32[128,1280]{1,0:T(8,128)S(1)}, u32[]{:S(2)}) copy-start(f32[128,1280]{1,0:T(8,128)S(1)} %get-tuple-element.16.base_ref) | copy-start | bytes 1966084
  68.3 1.1 %copy-start.15 = (f32[128,1280]{1,0:T(8,128)S(1)}, f32[128,1280]{1,0:T(8,128)}, u32[]{:S(2)}) copy-start(f32[128,1280]{1,0:T(8,128)} %copy-done.14) | copy-start | bytes 1966084
  69.4 1.1 %copy-start.17 = (f32[128,1280]{1,0:T(8,128)S(1)}, f32[128,1280]{1,0:T(8,128)}, u32[]{:S(2)}) copy-start(f32[128,1280]{1,0:T(8,128)} %copy-done.16) | copy-start | bytes 1966084
  70.5 1.1 %copy-start.19 = (f32[128,1280]{1,0:T(8,128)S(1)}, f32[128,1280]{1,0:T(8,128)}, u32[]{:S(2)}) copy-start(f32[128,1280]{1,0:T(8,128)} %copy-done.18) | copy-start | bytes 1966084
where the time goes:
time: 76.1 us; the launch traced here: 75.4 us
  waiting for transfers between devices  21.8 us (29%)
  Pallas kernels  21.1 us (28%)
  starting transfers between devices  16.2 us (21%)
  local copies, waits for them, and re-layouts  15.2 us (20%)
  between operations  0.91 us (1%)
    all_to_all x1, waiting for transfers between devices, shards(): slots = lax.all_to_all(slots, 'ctx', 0, 0)  20.3 us
    unnamed x50, local copies, waits for them, and re-layouts  14.6 us
    all_to_all x1, starting transfers between devices, shards(): slots = lax.all_to_all(slots, 'ctx', 0, 0)  10.6 us
    pallas_call x1, Pallas kernels, shards(): call(functools.partial(local_kernel, owners=owners, columns=columns), gri...  9.35 us
    all_to_all x1, starting transfers between devices, shards(): starts = lax.all_to_all(starts, 'ctx', 0, 0)  5.55 us
    pallas_call x1, Pallas kernels, shards(): call(scan_kernel, out_shape=[jax.ShapeDtypeStruct((owners, short, PAIR),...  4.63 us
    pallas_call x1, Pallas kernels, shards(): call(functools.partial(final_kernel, columns=columns), out_shape=jax.Shap...  3.8 us
    pallas_call x1, Pallas kernels, shards(): call(read_kernel, grid=(steps,), in_specs=[tokens] * 8 + [vector] * 2, ou...  3.33 us
  transfers between devices with their start and end apart: 2, of which 2 were waited for; matrix products, arithmetic and copies ran while one was open for 1% of the time, Pallas kernels for 4%

commit v1 on v0

v1 whole, which is shorter than its diff:
```python
import functools

import jax
import jax.numpy as jnp
from jax import lax
from jax.experimental import pallas as pl
from jax.experimental.pallas import tpu as pltpu
from jax.sharding import PartitionSpec as P

HEADS = 20
CH = 64
PAIR = 2 * CH
PAIRS = HEADS // 2
WIDTH = HEADS * CH
GROUP = 5
INTERPRET = False
F32 = jnp.float32
BF16 = jnp.bfloat16
NN = (((1,), (0,)), ((), ()))
NT = (((1,), (1,)), ((), ()))


def mxu(a, b, dims=NN):
    return lax.dot_general(a, b, dims, preferred_element_type=F32)


def split(x):
    hi = x.astype(BF16)
    return hi, (x - hi.astype(F32)).astype(BF16)


def lanes(*xs):
    return jnp.concatenate(xs, axis=1)


def rows(*xs):
    return jnp.concatenate(xs, axis=0)


def square(a, b):
    both = lanes(*b)
    out = mxu(lanes(*a), rows(both, both))
    return out[:, :PAIR] + out[:, PAIR:]


def wide(a, b):
    return mxu(lanes(*a), rows(b[0], b[0])) + mxu(a[0], b[1])


def exact_right(a, b):
    return mxu(lanes(*a), rows(b, b))


def iota(shape, dim):
    return lax.broadcasted_iota(jnp.int32, shape, dim)


def low_half(n):
    return iota((n, PAIR), 1) < CH


def block_ones():
    same = (iota((PAIR, PAIR), 0) < CH) == (iota((PAIR, PAIR), 1) < CH)
    return jnp.where(same, 1.0, 0.0).astype(BF16)


def head_sum(x, ones):
    return exact_right(split(x), ones)


def decays(logs, tril):
    return mxu(tril, logs)


def units(raw, ones):
    raw = raw.astype(F32)
    return raw * lax.rsqrt(head_sum(raw * raw, ones) + CH * 1e-05)


def tril_ones(n):
    return jnp.where(iota((n, n), 0) >= iota((n, n), 1), 1.0, 0.0).astype(BF16)


def grams(left, right, low):
    zero = jnp.zeros_like(left)
    stacked = split(rows(jnp.where(low, left, zero), jnp.where(low, zero, left)))
    b = split(right)
    return mxu(lanes(*stacked), lanes(b[0], b[0]), NT) + mxu(stacked[0], b[1], NT)


def inverse(inner):
    n = inner[0].shape[0]
    slab = 16
    count = n // slab
    row, lane = iota((slab, n), 0), iota((slab, n), 1)
    apart = row ^ (lane % slab)
    same = jnp.where(iota((n, n), 0) // slab == iota((n, n), 1) // slab, 1.0, 0.0)
    same_short = same.astype(BF16)

    def spread(pair):
        return tuple(rows(*[x] * count) * same_short for x in pair)

    small = [sum(jnp.where(lane // slab == i, x[i * slab : (i + 1) * slab], 0.0) for i in range(count)) for x in inner]
    solver = [jnp.where(apart == 0, 1.0, 0.0) + jnp.where(apart == 1, x, 0.0) for x in small]
    size = 2
    while size < slab:
        joins = (apart >= size) & (apart < 2 * size)
        halves = [split(x) for x in solver]
        mid = [square(split(jnp.where(joins, x, 0.0)), spread(t)) for x, t in zip(small, halves)]
        solver = [x + square(t, spread(split(m))) for x, t, m in zip(solver, halves, mid)]
        size *= 2
    halves = [spread(split(x)) for x in solver]
    solver = [rows(*[x] * count) * same for x in solver]

    while size < n:
        odd = lambda x: rows(*[x[i : i + size] for i in range(size, n, 2 * size)])

        def joined(even_of, new):
            parts = []
            for i in range(0, n // 2, size):
                parts += [even_of(2 * i), new[i : i + size]]
            return rows(*parts)

        apart = odd(iota((n, n), 0) ^ iota((n, n), 1))
        joins = (apart >= size) & (apart < 2 * size)
        gap = jnp.zeros((size, n), BF16)
        mid = [square(split(jnp.where(joins, odd(x), 0.0)), t) for x, t in zip(inner, halves)]
        mid = [tuple(joined(lambda i: gap, m) for m in split(x)) for x in mid]
        later = [
            odd(x) + square((odd(t[0]), odd(t[1])), m) for x, t, m in zip(solver, halves, mid)
        ]
        halves = [
            tuple(joined(lambda i: old[i : i + size], new) for old, new in zip(t, split(x)))
            for x, t in zip(later, halves)
        ]
        solver = [joined(lambda i: x[i : i + size], y) for x, y in zip(solver, later)]
        size *= 2
    return halves


def local_kernel(*refs, owners, columns):
    inputs, (slots_out, w_out, u_out) = refs[:5], refs[5:8]
    buffers = refs[8:13]
    slots, w_all, u_all, ends, in_sems, out_sems = refs[13:]
    n, width = w_all.shape
    block = GROUP * PAIR
    groups = width // block
    loads = [
        [
            pltpu.make_async_copy(src.at[:, pl.ds(g * block, block)], dst.at[:, pl.ds(g * block, block)], in_sems.at[g, i])
            for i, (src, dst) in enumerate(zip(inputs, buffers))
        ]
        for g in range(groups)
    ]
    for group in loads:
        for copy in group:
            copy.start()
    k_ref, v_ref, raw_ref, rate_ref, log_ref = buffers
    low = low_half(n)
    ones = block_ones()
    tril = tril_ones(n)
    strict = iota((n, n), 0) > iota((n, n), 1)
    own = (iota((PAIR, PAIR), 0) < CH) == low_half(PAIR)
    short = (columns + 15) // 16 * 8
    row, lane = iota((CH, PAIR), 0), iota((CH, PAIR), 1)
    moves, stores, owner = [], [], 0
    pairs = range(GROUP)
    heads = range(2 * GROUP)
    for g in range(groups):
        for copy in loads[g]:
            copy.wait()
        cut = [slice(g * block + p * PAIR, g * block + (p + 1) * PAIR) for p in pairs]
        cumul = [decays(log_ref[:, c], tril) for c in cut]
        unit = [units(raw_ref[:, c], ones) for c in cut]
        alpha = [-unit[p] * jnp.exp(cumul[p] - log_ref[:, cut[p]].astype(F32)) for p in pairs]
        fall = [jnp.exp(-cumul[p]) for p in pairs]
        beta = [rate_ref[:, cut[p]].astype(F32) * unit[p] * fall[p] for p in pairs]
        key = [k_ref[:, cut[p]].astype(F32) * fall[p] for p in pairs]
        gram = [grams(alpha[p], rows(beta[p], key[p]), low) for p in pairs]

        inner, cross = [], []
        for h in heads:
            part = gram[h // 2][(h % 2) * n : (h % 2 + 1) * n]
            inner.append(jnp.where(strict, part[:, :n], 0.0))
            cross.append(jnp.where(strict, part[:, n:], 0.0))
        akv = [exact_right(split(cross[h]), v_ref[:, cut[h // 2]]) for h in heads]
        akv = [jnp.where(low, akv[2 * p], akv[2 * p + 1]) for p in pairs]
        right = [split(lanes(alpha[p], akv[p])) for p in pairs]
        solver = inverse(inner)
        solved = [wide(solver[h], right[h // 2]) for h in heads]
        for p in pairs:
            first, second = solved[2 * p], solved[2 * p + 1]
            w = jnp.where(low, first[:, :PAIR], second[:, :PAIR])
            u = jnp.where(low, first[:, PAIR:], second[:, PAIR:])
            w_all[:, cut[p]] = w
            u_all[:, cut[p]] = u
            scale = jnp.exp(cumul[p][n - 1 :, :])
            end_b = beta[p] * scale
            end_k = key[p] * scale
            moved = square(split(end_b.T), split(w))
            diagonal = jnp.where(row == lane % CH, scale, 0.0)
            moves.append(jnp.where(low_half(CH), moved[:CH], moved[CH:]) + diagonal)
            content = v_ref[:, cut[p]].astype(F32).T.astype(BF16)
            by_key = mxu(content, lanes(*split(end_k)))
            fresh = square(split(u.T), split(end_b)) + by_key[:, :PAIR] + by_key[:, PAIR:]
            fresh = jnp.where(own, fresh, 0.0)
            ends[cut[p], :] = fresh + pltpu.roll(fresh, CH, 1)

        begin = owner
        while owner < owners and (owner + 1) * columns <= (g + 1) * block:
            at = owner * columns
            first, last = at // CH, (at + columns - 1) // CH
            slot = moves[first // 2]
            if first // 2 != last // 2:
                slot = jnp.where(low_half(CH), moves[last // 2], slot)
            slots[owner, :CH, :] = slot
            tail = rows(ends[at + short : at + columns, :], jnp.zeros((2 * short - columns, PAIR), F32))
            slots[owner, CH:, :] = jnp.where(low_half(short), ends[at : at + short, :], tail)
            owner += 1
        here = pl.ds(g * block, block)
        ready = pl.ds(begin, owner - begin)
        stores += [
            pltpu.make_async_copy(slots.at[ready], slots_out.at[ready], out_sems.at[g, 0]),
            pltpu.make_async_copy(w_all.at[:, here], w_out.at[:, here], out_sems.at[g, 1]),
            pltpu.make_async_copy(u_all.at[:, here], u_out.at[:, here], out_sems.at[g, 2]),
        ]
        for copy in stores[-3:]:
            copy.start()
    for copy in stores:
        copy.wait()


def read_kernel(*refs):
    inputs, (boost_ref, shift_ref) = refs[:8], refs[8:10]
    outputs = refs[10:13]
    buffers = refs[13:21]
    results, in_sems, out_sems = refs[21:24], refs[24], refs[25]
    n, width = results[0].shape
    block = GROUP * PAIR
    groups = width // block

    def moved(sources, targets, sems, g):
        here = pl.ds(g * block, block)
        return [
            pltpu.make_async_copy(src.at[:, here], dst.at[:, here], sems.at[g, i])
            for i, (src, dst) in enumerate(zip(sources, targets))
        ]

    loads = [moved(inputs, buffers, in_sems, g) for g in range(groups)]
    for group in loads:
        for copy in group:
            copy.start()
    q_ref, k_ref, v_ref, raw_ref, rate_ref, log_ref, w_ref, u_ref = buffers
    read_ref, local_ref, base_ref = results
    low = low_half(n)
    ones = block_ones()
    tril = tril_ones(n)
    weak = iota((n, n), 0) >= iota((n, n), 1)
    pairs = range(GROUP)
    stores = []
    for g in range(groups):
        for copy in loads[g]:
            copy.wait()
        cut = [slice(g * block + p * PAIR, g * block + (p + 1) * PAIR) for p in pairs]
        cumul = [decays(log_ref[:, c], tril) for c in cut]
        unit = [units(raw_ref[:, c], ones) for c in cut]
        fall = [jnp.exp(-cumul[p]) for p in pairs]
        beta = [rate_ref[:, cut[p]].astype(F32) * unit[p] * fall[p] for p in pairs]
        key = [k_ref[:, cut[p]].astype(F32) * fall[p] for p in pairs]
        read = [q_ref[:, cut[p]].astype(F32) * jnp.exp(cumul[p]) for p in pairs]
        gram = [grams(read[p], rows(beta[p], key[p]), low) for p in pairs]
        for p in pairs:
            c = cut[p]
            solved = split(lanes(w_ref[:, c], u_ref[:, c]))
            v = v_ref[:, c]
            reads, locals_ = [], []
            for h in range(2):
                part = gram[p][h * n : (h + 1) * n]
                both = wide(split(jnp.where(weak, part[:, :n], 0.0)), solved)
                direct = exact_right(split(jnp.where(weak, part[:, n:], 0.0)), v)
                reads.append(both[:, :PAIR])
                locals_.append(both[:, PAIR:] + direct)
            read_ref[:, c] = read[p] + jnp.where(low, *reads)
            local_ref[:, c] = jnp.where(low, *locals_)
            product = q_ref[:, c].astype(F32) * k_ref[:, c].astype(F32) * boost_ref[:, c]
            base_ref[:, c] = head_sum(product, ones) * v.astype(F32) + shift_ref[:, c]
        stores += moved(results, outputs, out_sems, g)
        for copy in stores[-3:]:
            copy.start()
    for copy in stores:
        copy.wait()


def scan_kernel(slots_ref, entry_ref, mask_ref, after_ref, starts_out, exit_ref, starts, sems):
    del after_ref
    count, short = starts.shape[:2]
    low = low_half(short)
    mask = mask_ref[...]
    state = entry_ref[...]
    chunk = count // sems.shape[0]
    stores = []
    for d in range(count):
        starts[d] = jnp.where(low, state[:short], state[short:])
        if d % chunk == chunk - 1:
            part = pl.ds(d + 1 - chunk, chunk)
            stores.append(pltpu.make_async_copy(starts.at[part], starts_out.at[part], sems.at[d // chunk]))
            stores[-1].start()
        hi, lo = split(slots_ref[d, :CH, :])
        weights = rows(lanes(hi, hi), lanes(hi, hi), lanes(lo, lo), lanes(lo, lo))
        end = slots_ref[d, CH:, :]
        turned = pltpu.roll(end, CH, 1)
        fresh = rows(jnp.where(low, end, turned), jnp.where(low, turned, end))
        out = mxu(lanes(*split(state * mask)), weights, NT)
        state = out[:, :PAIR] + out[:, PAIR:] + fresh
    exit_ref[...] = state
    for copy in stores:
        copy.wait()


def final_kernel(starts_ref, read_in, local_in, base_in, gain_ref, out, *scratch, columns):
    buffers, (begins, result, in_sems, out_sems) = scratch[:3], scratch[3:]
    read_ref, local_ref, base_ref = buffers
    cut = [slice(p * PAIR, (p + 1) * PAIR) for p in range(PAIRS)]
    place = [pl.ds(p * PAIR, PAIR) for p in range(PAIRS)]
    block = GROUP * PAIR
    loads = []
    for g in range(WIDTH // block):
        here = pl.ds(g * block, block)
        for i, (src, dst) in enumerate(zip((read_in, local_in, base_in), buffers)):
            loads.append(pltpu.make_async_copy(src.at[:, here], dst.at[:, here], in_sems.at[g, i]))
    for copy in loads:
        copy.start()
    short = starts_ref.shape[1]
    low = low_half(short)
    for owner in range(starts_ref.shape[0]):
        part = starts_ref[owner]
        turned = pltpu.roll(part, CH, 1)
        at = owner * columns
        begins[at : at + short, :] = jnp.where(low, part, turned)
        begins[at + short : at + columns, :] = jnp.where(low, turned, part)[: columns - short]
    own = (iota((PAIR, PAIR), 0) < CH) == low_half(PAIR)
    ones = block_ones()
    right = [split(jnp.where(own, begins[c, :], 0.0)) for c in cut]
    stores = []
    for g in range(PAIRS // GROUP):
        for copy in loads[3 * g : 3 * g + 3]:
            copy.wait()
        pairs = range(g * GROUP, (g + 1) * GROUP)
        left = [split(read_ref[:, cut[p]]) for p in pairs]
        carried = [
            mxu(lanes(*a), lanes(right[p][0], right[p][0]), NT) + mxu(a[0], right[p][1], NT)
            for p, a in zip(pairs, left)
        ]
        readout = [x + local_ref[:, cut[p]] for p, x in zip(pairs, carried)]
        centred = [x - head_sum(x, ones) * (1.0 / CH) for x in readout]
        variance = [head_sum(x * x, ones) * (1.0 / CH) for x in centred]
        for p, x, y in zip(pairs, centred, variance):
            scaled = x * lax.rsqrt(y + 1e-05) * gain_ref[:, cut[p]]
            result[:, cut[p]] = (scaled + base_ref[:, cut[p]]).astype(BF16)
            stores.append(pltpu.make_async_copy(result.at[:, place[p]], out.at[:, place[p]], out_sems.at[p]))
            stores[-1].start()
    for copy in stores:
        copy.wait()


def call(kernel, **kwargs):
    params = pltpu.CompilerParams(vmem_limit_bytes=48 * 1024 * 1024)
    return pl.pallas_call(kernel, interpret=INTERPRET, compiler_params=params, **kwargs)


def shards(q, k, v, raw, rates, logs, memory, boost, gain, shift):
    n = q.shape[0]
    owners = lax.axis_size("ctx")
    columns = memory.shape[1]
    short = (columns + 15) // 16 * 8
    groups = PAIRS // GROUP
    hbm = pl.BlockSpec(memory_space=pltpu.HBM)
    vmem = pl.BlockSpec(memory_space=pltpu.VMEM)
    plane = jax.ShapeDtypeStruct((n, WIDTH), F32)
    tokens = pltpu.VMEM((n, WIDTH), BF16)
    floats = pltpu.VMEM((n, WIDTH), F32)
    sems = pltpu.SemaphoreType.DMA

    slots, w, u = call(
        functools.partial(local_kernel, owners=owners, columns=columns),
        in_specs=[hbm] * 5,
        out_specs=[hbm] * 3,
        out_shape=[jax.ShapeDtypeStruct((owners, CH + short, PAIR), F32), plane, plane],
        scratch_shapes=[tokens] * 5
        + [
            pltpu.VMEM((owners, CH + short, PAIR), F32),
            floats,
            floats,
            pltpu.VMEM((WIDTH, PAIR), F32),
            sems((groups, 5)),
            sems((groups, 3)),
        ],
    )(k, v, raw, rates, logs)
    slots = lax.all_to_all(slots, "ctx", 0, 0)

    read, local, base = call(
        read_kernel,
        in_specs=[hbm] * 8 + [vmem] * 2,
        out_specs=[hbm] * 3,
        out_shape=[plane] * 3,
        scratch_shapes=[tokens] * 6 + [floats] * 5 + [sems((groups, 8)), sems((groups, 3))],
    )(q, k, v, raw, rates, logs, w, u, boost.reshape(1, WIDTH), shift.reshape(1, WIDTH))

    place = lax.axis_index("ctx")
    own = lax.broadcasted_iota(jnp.int32, (2 * short, PAIR), 0)
    half = lax.broadcasted_iota(jnp.int32, (2 * short, PAIR), 1) // CH
    mask = ((place * columns + own) // CH % 2 == half) & (own < columns)
    entry = jnp.pad(memory.T, ((0, 2 * short - columns), (0, 0)))
    starts, final = call(
        scan_kernel,
        in_specs=[vmem, vmem, vmem, hbm],
        out_specs=[hbm, vmem],
        out_shape=[
            jax.ShapeDtypeStruct((owners, short, PAIR), F32),
            jax.ShapeDtypeStruct((2 * short, PAIR), F32),
        ],
        scratch_shapes=[pltpu.VMEM((owners, short, PAIR), F32), sems((4,))],
    )(slots, jnp.concatenate([entry, entry], axis=1), mask.astype(F32), base)
    starts = lax.all_to_all(starts, "ctx", 0, 0)
    exit_state = final[:columns, :CH].T

    out = call(
        functools.partial(final_kernel, columns=columns),
        in_specs=[vmem, hbm, hbm, hbm, vmem],
        out_specs=hbm,
        out_shape=jax.ShapeDtypeStruct((n, WIDTH), BF16),
        scratch_shapes=[floats] * 3
        + [pltpu.VMEM((WIDTH, PAIR), F32), tokens, sems((groups, 3)), sems((PAIRS,))],
    )(starts, read, local, base, gain.reshape(1, WIDTH))
    return out, exit_state


def solution(mesh):
    rows_spec = P(("dp", "ctx"), None)
    return jax.shard_map(
        shards,
        mesh=mesh,
        in_specs=(rows_spec,) * 6 + (P("dp", "ctx"), P(), P(), P()),
        out_specs=(rows_spec, P("dp", "ctx")),
        check_vma=False,
    )
```

time: 76.1 us -> 72.4 us (0.951)
  local copies, waits for them, and re-layouts: 15.2 us -> 13.7 us
  waiting for transfers between devices: 21.8 us -> 20.6 us
  Pallas kernels: 21.1 us -> 20.1 us
    all_to_all x1, waiting for transfers between devices: 20.3 us -> 11 us  [shards(): slots = lax.all_to_all(slots, 'ctx', 0, 0)]
    all_to_all x1, waiting for transfers between devices: 1.49 us -> 9.65 us  [shards(): starts = lax.all_to_all(starts, 'ctx', 0, 0)]
    unnamed x50 -> x48, local copies, waits for them, and re-layouts: 14.6 us -> 13.1 us
    pallas_call x4, Pallas kernels: 21.1 us -> 20.1 us  [the longest x1 9.37 us: shards(): call(functools.partial(local_kernel, owners=owners, columns=columns), in_...]
  transfers between devices with their start and end apart: 2 -> 2, of which waited for: 2 -> 2; matrix products, arithmetic and copies ran while one was open for 1% -> 1% of each run, Pallas kernels for 4% -> 5%
where the time goes in v1:
time: 72.4 us; the launch traced here: 71.8 us
  waiting for transfers between devices  20.6 us (28%)
  Pallas kernels  20.1 us (28%)
  starting transfers between devices  16.1 us (22%)
  local copies, waits for them, and re-layouts  13.7 us (19%)
  between operations  1.03 us (1%)
    unnamed x48, local copies, waits for them, and re-layouts  13.1 us
    all_to_all x1, waiting for transfers between devices, shards(): slots = lax.all_to_all(slots, 'ctx', 0, 0)  11 us
    all_to_all x1, starting transfers between devices, shards(): slots = lax.all_to_all(slots, 'ctx', 0, 0)  10.6 us
    all_to_all x1, waiting for transfers between devices, shards(): starts = lax.all_to_all(starts, 'ctx', 0, 0)  9.65 us
    pallas_call x1, Pallas kernels, shards(): call(functools.partial(local_kernel, owners=owners, columns=columns), in_...  9.37 us
    all_to_all x1, starting transfers between devices, shards(): starts = lax.all_to_all(starts, 'ctx', 0, 0)  5.51 us
    pallas_call x1, Pallas kernels, shards(): call(scan_kernel, in_specs=[vmem, vmem, vmem, hbm], out_specs=[hbm, vmem]...  4.81 us
    pallas_call x1, Pallas kernels, shards(): call(read_kernel, in_specs=[hbm] * 8 + [vmem] * 2, out_specs=[hbm] * 3, o...  3.57 us
  transfers between devices with their start and end apart: 2, of which 2 were waited for; matrix products, arithmetic and copies ran while one was open for 1% of the time, Pallas kernels for 5%

profile of v1, /device:TPU:1, one launch (start us, length us, event | category | flops | bytes accessed | tf_op | source)
XLA Modules:
  0.0 71.8 jit_solution(6989886891557590140)
XLA Ops:
  0.6 0.0 copy-start
  0.6 1.0 %copy-done = bf16[128,1280]{1,0:T(8,128)(2,1)S(1)} copy-done((bf16[128,1280]{1,0:T(8,128)(2,1)S(1)}, bf16[128,1280]{1,0:T(8,128)(2,1)}, u32[]{:S(2)}) %copy-start) | copy-done | bytes 327704
  1.6 0.0 copy-start.2
  1.6 1.0 %copy-done.2 = bf16[128,1280]{1,0:T(8,128)(2,1)S(1)} copy-done((bf16[128,1280]{1,0:T(8,128)(2,1)S(1)}, bf16[128,1280]{1,0:T(8,128)(2,1)}, u32[]{:S(2)}) %copy-start.2) | copy-done | bytes 327704
  2.6 0.0 copy-start.4
  2.6 1.0 %copy-done.4 = bf16[128,1280]{1,0:T(8,128)(2,1)S(1)} copy-done((bf16[128,1280]{1,0:T(8,128)(2,1)S(1)}, bf16[128,1280]{1,0:T(8,128)(2,1)}, u32[]{:S(2)}) %copy-start.4) | copy-done | bytes 327704
  3.6 0.0 copy-start.6
  3.6 1.0 %copy-done.6 = bf16[128,1280]{1,0:T(8,128)(2,1)S(1)} copy-done((bf16[128,1280]{1,0:T(8,128)(2,1)S(1)}, bf16[128,1280]{1,0:T(8,128)(2,1)}, u32[]{:S(2)}) %copy-start.6) | copy-done | bytes 327704
  4.5 0.0 copy-start.8
  4.5 1.0 %copy-done.8 = bf16[128,1280]{1,0:T(8,128)(2,1)S(1)} copy-done((bf16[128,1280]{1,0:T(8,128)(2,1)S(1)}, bf16[128,1280]{1,0:T(8,128)(2,1)}, u32[]{:S(2)}) %copy-start.8) | copy-done | bytes 327704
  5.5 9.4 %shard_map.113 = (f32[32,88,128]{2,1,0:T(8,128)}, f32[128,1280]{1,0:T(8,128)S(1)}, f32[128,1280]{1,0:T(8,128)S(1)}) custom-call(bf16[128,1280]{1,0:T(8,128)(2,1)S(1)} %copy-done, bf16[128,1280]{1,0:T(8,128)(2,1)S(1)} %copy-done.2, bf16[128,1280]{1,0:T(8,128)(2,1)S(1)} %copy-done.4, bf16[128,1280]{1,0:T(8,128)(2,1)S(1)} %copy-done.6, ...), custom_call_target="tpu_custom_call" | custom-call | tf_op jit(solution)/shard_map/pallas_call | solution.py:384
  14.9 0.0 copy-start.14
  14.9 0.8 %copy-done.14 = f32[128,1280]{1,0:T(8,128)} copy-done((f32[128,1280]{1,0:T(8,128)}, f32[128,1280]{1,0:T(8,128)S(1)}, u32[]{:S(2)}) %copy-start.14) | copy-done | bytes 655384
  15.7 0.0 copy-start.16
  15.7 0.8 %copy-done.16 = f32[128,1280]{1,0:T(8,128)} copy-done((f32[128,1280]{1,0:T(8,128)}, f32[128,1280]{1,0:T(8,128)S(1)}, u32[]{:S(2)}) %copy-start.16) | copy-done | bytes 655384
  16.6 0.0 copy-start.3
  16.6 0.0 copy-start.5
  16.6 0.0 copy-start.7
  16.6 10.6 %all-to-all-start = ((f32[32,88,128]{2,1,0:T(8,128)}), f32[32,88,128]{2,1,0:T(8,128)S(1)}, u32[]{:S(2)}, u32[]{:S(2)}) async-start(f32[32,88,128]{2,1,0:T(8,128)} %get-tuple-element.10), calls=%async_computation | async-start | bytes 2883584 | tf_op jit(solution)/shard_map/all_to_all | solution.py:399
  27.2 0.0 copy-done.21
  27.3 0.0 copy-done.22
  27.3 0.0 copy-done.20
  27.3 0.0 copy-done.1
  27.3 0.0 copy-done.3
  27.3 0.0 copy-done.5
  27.3 0.0 copy-done.7
  27.4 0.0 copy-start.9
  27.4 1.0 %copy-done.9 = bf16[128,1280]{1,0:T(8,128)(2,1)S(1)} copy-done((bf16[128,1280]{1,0:T(8,128)(2,1)S(1)}, bf16[128,1280]{1,0:T(8,128)(2,1)}, u32[]{:S(2)}) %copy-start.9) | copy-done | bytes 327704
  28.3 1.1 %copy-done.15 = f32[128,1280]{1,0:T(8,128)S(1)} copy-done((f32[128,1280]{1,0:T(8,128)S(1)}, f32[128,1280]{1,0:T(8,128)}, u32[]{:S(2)}) %copy-start.15) | copy-done | bytes 655384
  29.4 1.1 %copy-done.17 = f32[128,1280]{1,0:T(8,128)S(1)} copy-done((f32[128,1280]{1,0:T(8,128)S(1)}, f32[128,1280]{1,0:T(8,128)}, u32[]{:S(2)}) %copy-start.17) | copy-done | bytes 655384
  30.5 1.0 %copy-done.19 = bf16[128,1280]{1,0:T(8,128)(2,1)S(1)} copy-done((bf16[128,1280]{1,0:T(8,128)(2,1)S(1)}, bf16[128,1280]{1,0:T(8,128)(2,1)}, u32[]{:S(2)}) %copy-start.19) | copy-done | bytes 327704
  31.5 3.6 %shard_map.114 = (f32[128,1280]{1,0:T(8,128)S(1)}, f32[128,1280]{1,0:T(8,128)S(1)}, f32[128,1280]{1,0:T(8,128)S(1)}) custom-call(bf16[128,1280]{1,0:T(8,128)(2,1)S(1)} %copy-done.19, bf16[128,1280]{1,0:T(8,128)(2,1)S(1)} %copy-done.1, bf16[128,1280]{1,0:T(8,128)(2,1)S(1)} %copy-done.3, bf16[128,1280]{1,0:T(8,128)(2,1)S(1)} %copy-done.5, ...), custom_call_target="tpu_custom_call" | custom-call | tf_op jit(solution)/shard_map/pallas_call | solution.py:401
  35.0 0.0 copy-start.10
  35.1 0.8 %copy-done.10 = f32[128,1280]{1,0:T(8,128)} copy-done((f32[128,1280]{1,0:T(8,128)}, f32[128,1280]{1,0:T(8,128)S(1)}, u32[]{:S(2)}) %copy-start.10) | copy-done | bytes 655384
  35.9 0.8 %copy-done.12 = f32[128,1280]{1,0:T(8,128)} copy-done((f32[128,1280]{1,0:T(8,128)}, f32[128,1280]{1,0:T(8,128)S(1)}, u32[]{:S(2)}) %copy-start.12) | copy-done | bytes 655384
  36.8 0.1 pad_maximum_fusion.entry_ref
  36.9 0.1 fusion.3.mask_ref
  37.0 11.0 %all-to-all-done.slots_ref = f32[32,88,128]{2,1,0:T(8,128)S(1)} async-done(((f32[32,88,128]{2,1,0:T(8,128)}), f32[32,88,128]{2,1,0:T(8,128)S(1)}, u32[]{:S(2)}, u32[]{:S(2)}) %all-to-all-start) | async-done | bytes 1441824 | tf_op jit(solution)/shard_map/all_to_all | solution.py:399
  48.0 4.8 %shard_map.115 = (f32[32,24,128]{2,1,0:T(8,128)S(1)}, f32[48,128]{1,0:T(8,128)S(1)}) custom-call(f32[32,88,128]{2,1,0:T(8,128)S(1)} %all-to-all-done.slots_ref, f32[48,128]{1,0:T(8,128)S(1)} %pad_maximum_fusion.entry_ref, f32[48,128]{1,0:T(8,128)S(1)} %fusion.3.mask_ref, f32[128,1280]{1,0:T(8,128)S(1)} %get-tuple-element.13.after_ref.base_in), custom_call_target="tpu_custom_call" | custom-call | tf_op jit(solution)/shard_map/pallas_call | solution.py:414
  52.8 0.0 copy-start.18
  52.8 0.7 %copy-done.18 = f32[32,24,128]{2,1,0:T(8,128)} copy-done((f32[32,24,128]{2,1,0:T(8,128)}, f32[32,24,128]{2,1,0:T(8,128)S(1)}, u32[]{:S(2)}) %copy-start.18) | copy-done | bytes 393240
  53.5 5.5 %all-to-all-start.1 = ((f32[32,24,128]{2,1,0:T(8,128)}), f32[32,24,128]{2,1,0:T(8,128)S(1)}, u32[]{:S(2)}, u32[]{:S(2)}) async-start(f32[32,24,128]{2,1,0:T(8,128)} %copy-done.18), calls=%async_computation.1 | async-start | bytes 786432 | tf_op jit(solution)/shard_map/all_to_all | solution.py:424
  59.0 0.0 copy-done.23
  59.0 0.6 slice_bitcast_fusion
  59.7 9.7 %all-to-all-done.1.starts_ref = f32[32,24,128]{2,1,0:T(8,128)S(1)} async-done(((f32[32,24,128]{2,1,0:T(8,128)}), f32[32,24,128]{2,1,0:T(8,128)S(1)}, u32[]{:S(2)}, u32[]{:S(2)}) %all-to-all-start.1) | async-done | bytes 393248 | tf_op jit(solution)/shard_map/all_to_all | solution.py:424
  69.3 0.0 copy-done.11
  69.3 0.0 copy-done.13
  69.3 2.3 %shard_map.116 = bf16[128,1280]{1,0:T(8,128)(2,1)} custom-call(f32[32,24,128]{2,1,0:T(8,128)S(1)} %all-to-all-done.1.starts_ref, f32[128,1280]{1,0:T(8,128)S(1)} %copy-done.11, f32[128,1280]{1,0:T(8,128)S(1)} %copy-done.13, f32[128,1280]{1,0:T(8,128)S(1)} %get-tuple-element.13.after_ref.base_in, f32[1,1280]{1,0:T(1,128)S(1)} %reshape.15.gain_ref), custom_call_target="tpu_custom_call" | custom-call | tf_op jit(solution)/shard_map/pallas_call | solution.py:427
  (19 shorter events, 0.1 us)
Async XLA Ops:
  0.6 1.0 %copy-start = (bf16[128,1280]{1,0:T(8,128)(2,1)S(1)}, bf16[128,1280]{1,0:T(8,128)(2,1)}, u32[]{:S(2)}) copy-start(bf16[128,1280]{1,0:T(8,128)(2,1)} %refs_1_.3) | copy-start | bytes 983044
  1.6 1.0 %copy-start.2 = (bf16[128,1280]{1,0:T(8,128)(2,1)S(1)}, bf16[128,1280]{1,0:T(8,128)(2,1)}, u32[]{:S(2)}) copy-start(bf16[128,1280]{1,0:T(8,128)(2,1)} %refs_2_.3) | copy-start | bytes 983044
  2.6 1.0 %copy-start.4 = (bf16[128,1280]{1,0:T(8,128)(2,1)S(1)}, bf16[128,1280]{1,0:T(8,128)(2,1)}, u32[]{:S(2)}) copy-start(bf16[128,1280]{1,0:T(8,128)(2,1)} %refs_3_.3) | copy-start | bytes 983044
  3.6 1.0 %copy-start.6 = (bf16[128,1280]{1,0:T(8,128)(2,1)S(1)}, bf16[128,1280]{1,0:T(8,128)(2,1)}, u32[]{:S(2)}) copy-start(bf16[128,1280]{1,0:T(8,128)(2,1)} %refs_4_.3) | copy-start | bytes 983044
  4.5 1.0 %copy-start.8 = (bf16[128,1280]{1,0:T(8,128)(2,1)S(1)}, bf16[128,1280]{1,0:T(8,128)(2,1)}, u32[]{:S(2)}) copy-start(bf16[128,1280]{1,0:T(8,128)(2,1)} %refs_5_.1) | copy-start | bytes 983044
  14.9 0.8 %copy-start.14 = (f32[128,1280]{1,0:T(8,128)}, f32[128,1280]{1,0:T(8,128)S(1)}, u32[]{:S(2)}) copy-start(f32[128,1280]{1,0:T(8,128)S(1)} %get-tuple-element.11.refs_6_) | copy-start | bytes 1966084
  15.7 0.8 %copy-start.16 = (f32[128,1280]{1,0:T(8,128)}, f32[128,1280]{1,0:T(8,128)S(1)}, u32[]{:S(2)}) copy-start(f32[128,1280]{1,0:T(8,128)S(1)} %get-tuple-element.12.refs_7_) | copy-start | bytes 1966084
  16.6 10.7 %copy-start.21 = (f32[1280]{0:T(1024)S(1)}, f32[1280]{0:T(1024)}, u32[]{:S(2)}) copy-start(f32[1280]{0:T(1024)} %param.17) | copy-start | bytes 15364
  16.6 10.7 %copy-start.22 = (f32[1280]{0:T(1024)S(1)}, f32[1280]{0:T(1024)}, u32[]{:S(2)}) copy-start(f32[1280]{0:T(1024)} %param.19) | copy-start | bytes 15364
  16.6 10.7 %copy-start.20 = (f32[64,40]{0,1:T(8,128)S(1)}, f32[64,40]{0,1:T(8,128)}, u32[]{:S(2)}) copy-start(f32[64,40]{0,1:T(8,128)} %param.16) | copy-start | bytes 30724
  16.6 10.8 %copy-start.1 = (bf16[128,1280]{1,0:T(8,128)(2,1)S(1)}, bf16[128,1280]{1,0:T(8,128)(2,1)}, u32[]{:S(2)}) copy-start(bf16[128,1280]{1,0:T(8,128)(2,1)} %refs_1_.3) | copy-start | bytes 983044
  16.6 10.8 %copy-start.3 = (bf16[128,1280]{1,0:T(8,128)(2,1)S(1)}, bf16[128,1280]{1,0:T(8,128)(2,1)}, u32[]{:S(2)}) copy-start(bf16[128,1280]{1,0:T(8,128)(2,1)} %refs_2_.3) | copy-start | bytes 983044
  16.6 10.8 %copy-start.5 = (bf16[128,1280]{1,0:T(8,128)(2,1)S(1)}, bf16[128,1280]{1,0:T(8,128)(2,1)}, u32[]{:S(2)}) copy-start(bf16[128,1280]{1,0:T(8,128)(2,1)} %refs_3_.3) | copy-start | bytes 983044
  16.6 10.8 %copy-start.7 = (bf16[128,1280]{1,0:T(8,128)(2,1)S(1)}, bf16[128,1280]{1,0:T(8,128)(2,1)}, u32[]{:S(2)}) copy-start(bf16[128,1280]{1,0:T(8,128)(2,1)} %refs_4_.3) | copy-start | bytes 983044
  16.6 31.3 %all-to-all-start = ((f32[32,88,128]{2,1,0:T(8,128)}), f32[32,88,128]{2,1,0:T(8,128)S(1)}, u32[]{:S(2)}, u32[]{:S(2)}) async-start(f32[32,88,128]{2,1,0:T(8,128)} %get-tuple-element.10), calls=%async_computation | async-start | bytes 2883584 | tf_op jit(solution)/shard_map/all_to_all | solution.py:399
  27.4 1.0 %copy-start.9 = (bf16[128,1280]{1,0:T(8,128)(2,1)S(1)}, bf16[128,1280]{1,0:T(8,128)(2,1)}, u32[]{:S(2)}) copy-start(bf16[128,1280]{1,0:T(8,128)(2,1)} %refs_5_.1) | copy-start | bytes 983044
  28.3 1.1 %copy-start.15 = (f32[128,1280]{1,0:T(8,128)S(1)}, f32[128,1280]{1,0:T(8,128)}, u32[]{:S(2)}) copy-start(f32[128,1280]{1,0:T(8,128)} %copy-done.14) | copy-start | bytes 1966084
  29.4 1.1 %copy-start.17 = (f32[128,1280]{1,0:T(8,128)S(1)}, f32[128,1280]{1,0:T(8,128)}, u32[]{:S(2)}) copy-start(f32[128,1280]{1,0:T(8,128)} %copy-done.16) | copy-start | bytes 1966084
  30.5 1.0 %copy-start.19 = (bf16[128,1280]{1,0:T(8,128)(2,1)S(1)}, bf16[128,1280]{1,0:T(8,128)(2,1)}, u32[]{:S(2)}) copy-start(bf16[128,1280]{1,0:T(8,128)(2,1)} %refs_0_.3) | copy-start | bytes 983044
  35.0 0.8 %copy-start.10 = (f32[128,1280]{1,0:T(8,128)}, f32[128,1280]{1,0:T(8,128)S(1)}, u32[]{:S(2)}) copy-start(f32[128,1280]{1,0:T(8,128)S(1)} %get-tuple-element.15.read_in) | copy-start | bytes 1966084
  35.9 0.8 %copy-start.12 = (f32[128,1280]{1,0:T(8,128)}, f32[128,1280]{1,0:T(8,128)S(1)}, u32[]{:S(2)}) copy-start(f32[128,1280]{1,0:T(8,128)S(1)} %get-tuple-element.16.local_in) | copy-start | bytes 1966084
  47.9 11.1 %copy-start.23 = (f32[1280]{0:T(1024)S(1)}, f32[1280]{0:T(1024)}, u32[]{:S(2)}) copy-start(f32[1280]{0:T(1024)} %param.18) | copy-start | bytes 15364
  47.9 21.4 %copy-start.11 = (f32[128,1280]{1,0:T(8,128)S(1)}, f32[128,1280]{1,0:T(8,128)}, u32[]{:S(2)}) copy-start(f32[128,1280]{1,0:T(8,128)} %copy-done.10) | copy-start | bytes 1966084
  47.9 21.4 %copy-start.13 = (f32[128,1280]{1,0:T(8,128)S(1)}, f32[128,1280]{1,0:T(8,128)}, u32[]{:S(2)}) copy-start(f32[128,1280]{1,0:T(8,128)} %copy-done.12) | copy-start | bytes 1966084
  52.8 0.7 %copy-start.18 = (f32[32,24,128]{2,1,0:T(8,128)}, f32[32,24,128]{2,1,0:T(8,128)S(1)}, u32[]{:S(2)}) copy-start(f32[32,24,128]{2,1,0:T(8,128)S(1)} %get-tuple-element.14) | copy-start | bytes 1179652
  53.5 15.8 %all-to-all-start.1 = ((f32[32,24,128]{2,1,0:T(8,128)}), f32[32,24,128]{2,1,0:T(8,128)S(1)}, u32[]{:S(2)}, u32[]{:S(2)}) async-start(f32[32,24,128]{2,1,0:T(8,128)} %copy-done.18), calls=%async_computation.1 | async-start | bytes 786432 | tf_op jit(solution)/shard_map/all_to_all | solution.py:424

commit v2 on v1

--- a/solution.py
+++ b/solution.py
@@ -138,10 +138,10 @@
     return halves
 
 
-def local_kernel(*refs, owners, columns):
-    inputs, (slots_out, w_out, u_out) = refs[:5], refs[5:8]
+def local_kernel(*refs):
+    inputs, (pieces_out, w_out, u_out) = refs[:5], refs[5:8]
     buffers = refs[8:13]
-    slots, w_all, u_all, ends, in_sems, out_sems = refs[13:]
+    pieces, w_all, u_all, in_sems, out_sems = refs[13:]
     n, width = w_all.shape
     block = GROUP * PAIR
     groups = width // block
@@ -160,10 +160,8 @@
     ones = block_ones()
     tril = tril_ones(n)
     strict = iota((n, n), 0) > iota((n, n), 1)
-    own = (iota((PAIR, PAIR), 0) < CH) == low_half(PAIR)
-    short = (columns + 15) // 16 * 8
     row, lane = iota((CH, PAIR), 0), iota((CH, PAIR), 1)
-    moves, stores, owner = [], [], 0
+    stores = []
     pairs = range(GROUP)
     heads = range(2 * GROUP)
     for g in range(groups):
@@ -199,28 +197,16 @@
             end_k = key[p] * scale
             moved = square(split(end_b.T), split(w))
             diagonal = jnp.where(row == lane % CH, scale, 0.0)
-            moves.append(jnp.where(low_half(CH), moved[:CH], moved[CH:]) + diagonal)
+            pieces[0, g * GROUP + p] = jnp.where(low_half(CH), moved[:CH], moved[CH:]) + diagonal
             content = v_ref[:, cut[p]].astype(F32).T.astype(BF16)
             by_key = mxu(content, lanes(*split(end_k)))
             fresh = square(split(u.T), split(end_b)) + by_key[:, :PAIR] + by_key[:, PAIR:]
-            fresh = jnp.where(own, fresh, 0.0)
-            ends[cut[p], :] = fresh + pltpu.roll(fresh, CH, 1)
-
-        begin = owner
-        while owner < owners and (owner + 1) * columns <= (g + 1) * block:
-            at = owner * columns
-            first, last = at // CH, (at + columns - 1) // CH
-            slot = moves[first // 2]
-            if first // 2 != last // 2:
-                slot = jnp.where(low_half(CH), moves[last // 2], slot)
-            slots[owner, :CH, :] = slot
-            tail = rows(ends[at + short : at + columns, :], jnp.zeros((2 * short - columns, PAIR), F32))
-            slots[owner, CH:, :] = jnp.where(low_half(short), ends[at : at + short, :], tail)
-            owner += 1
+            pieces[1, g * GROUP + p] = jnp.where(low_half(CH), fresh[:CH], fresh[CH:])
+
         here = pl.ds(g * block, block)
-        ready = pl.ds(begin, owner - begin)
+        ready = pl.ds(g * GROUP, GROUP)
         stores += [
-            pltpu.make_async_copy(slots.at[ready], slots_out.at[ready], out_sems.at[g, 0]),
+            pltpu.make_async_copy(pieces.at[:, ready], pieces_out.at[:, ready], out_sems.at[g, 0]),
             pltpu.make_async_copy(w_all.at[:, here], w_out.at[:, here], out_sems.at[g, 1]),
             pltpu.make_async_copy(u_all.at[:, here], u_out.at[:, here], out_sems.at[g, 2]),
         ]
@@ -230,11 +216,51 @@
         copy.wait()
 
 
+def diagonal_blocks(x):
+    own = (iota((PAIR, PAIR), 0) < CH) == low_half(PAIR)
+    return jnp.where(own, rows(x, x), 0.0)
+
+
+def square_nt(a, b):
+    out = mxu(lanes(*a), rows(lanes(b[0], b[0]), lanes(b[1], b[1])), NT)
+    return out[:, :PAIR] + out[:, PAIR:]
+
+
+def compose_kernel(mine_ref, other_ref, late_ref, slots_ref, moves, ends, *, columns):
+    late = late_ref[...] > 0.5
+    low = low_half(CH)
+    short = (columns + 15) // 16 * 8
+    for p in range(PAIRS):
+        mine, other = mine_ref[0, p], other_ref[0, p]
+        first, second = jnp.where(late, other, mine), jnp.where(late, mine, other)
+        moves[p] = square(split(second), split(diagonal_blocks(first)))
+        mine, other = mine_ref[1, p], other_ref[1, p]
+        first, end = jnp.where(late, other, mine), jnp.where(late, mine, other)
+        end = end + square_nt(split(first), split(diagonal_blocks(second)))
+        turned = pltpu.roll(end, CH, 1)
+        ends[p * PAIR : p * PAIR + CH, :] = jnp.where(low, end, turned)
+        ends[p * PAIR + CH : (p + 1) * PAIR, :] = jnp.where(low, turned, end)
+
+    def packed(owner):
+        at = owner * columns
+        first, last = at // CH, (at + columns - 1) // CH
+        slot = moves[first // 2]
+        if first // 2 != last // 2:
+            slot = jnp.where(low, moves[last // 2], slot)
+        tail = rows(ends[at + short : at + columns, :], jnp.zeros((2 * short - columns, PAIR), F32))
+        return slot, jnp.where(low_half(short), ends[at : at + short, :], tail)
+
+    for chip in range(slots_ref.shape[0]):
+        (move_a, end_a), (move_b, end_b) = packed(2 * chip), packed(2 * chip + 1)
+        slots_ref[chip, :CH, :] = jnp.where(late, move_b, move_a)
+        slots_ref[chip, CH:, :] = jnp.where(late, end_b, end_a)
+
+
 def read_kernel(*refs):
-    inputs, (boost_ref, shift_ref) = refs[:8], refs[8:10]
-    outputs = refs[10:13]
-    buffers = refs[13:21]
-    results, in_sems, out_sems = refs[21:24], refs[24], refs[25]
+    inputs, (boost_ref, shift_ref, other_ref, late_ref) = refs[:8], refs[8:12]
+    outputs = refs[12:15]
+    buffers = refs[15:23]
+    results, in_sems, out_sems = refs[23:26], refs[26], refs[27]
     n, width = results[0].shape
     block = GROUP * PAIR
     groups = width // block
@@ -256,6 +282,7 @@
     ones = block_ones()
     tril = tril_ones(n)
     weak = iota((n, n), 0) >= iota((n, n), 1)
+    late = late_ref[...] > 0.5
     pairs = range(GROUP)
     stores = []
     for g in range(groups):
@@ -280,8 +307,13 @@
                 direct = exact_right(split(jnp.where(weak, part[:, n:], 0.0)), v)
                 reads.append(both[:, :PAIR])
                 locals_.append(both[:, PAIR:] + direct)
-            read_ref[:, c] = read[p] + jnp.where(low, *reads)
-            local_ref[:, c] = jnp.where(low, *locals_)
+            seen = read[p] + jnp.where(low, *reads)
+            here = jnp.where(low, *locals_)
+            parts = split(seen)
+            move, end = other_ref[0, g * GROUP + p], other_ref[1, g * GROUP + p]
+            read_ref[:, c] = jnp.where(late, square(parts, split(diagonal_blocks(move))), seen)
+            passed = here + square_nt(parts, split(diagonal_blocks(end)))
+            local_ref[:, c] = jnp.where(late, passed, here)
             product = q_ref[:, c].astype(F32) * k_ref[:, c].astype(F32) * boost_ref[:, c]
             base_ref[:, c] = head_sum(product, ones) * v.astype(F32) + shift_ref[:, c]
         stores += moved(results, outputs, out_sems, g)
@@ -293,16 +325,16 @@
 
 def scan_kernel(slots_ref, entry_ref, mask_ref, after_ref, starts_out, exit_ref, starts, sems):
     del after_ref
-    count, short = starts.shape[:2]
+    count, short = slots_ref.shape[0], starts.shape[1]
     low = low_half(short)
     mask = mask_ref[...]
     state = entry_ref[...]
     chunk = count // sems.shape[0]
     stores = []
     for d in range(count):
-        starts[d] = jnp.where(low, state[:short], state[short:])
+        starts[2 * d] = starts[2 * d + 1] = jnp.where(low, state[:short], state[short:])
         if d % chunk == chunk - 1:
-            part = pl.ds(d + 1 - chunk, chunk)
+            part = pl.ds(2 * (d + 1 - chunk), 2 * chunk)
             stores.append(pltpu.make_async_copy(starts.at[part], starts_out.at[part], sems.at[d // chunk]))
             stores[-1].start()
         hi, lo = split(slots_ref[d, :CH, :])
@@ -381,32 +413,34 @@
     floats = pltpu.VMEM((n, WIDTH), F32)
     sems = pltpu.SemaphoreType.DMA
 
-    slots, w, u = call(
-        functools.partial(local_kernel, owners=owners, columns=columns),
+    pieces = (2, PAIRS, CH, PAIR)
+    mine, w, u = call(
+        local_kernel,
         in_specs=[hbm] * 5,
         out_specs=[hbm] * 3,
-        out_shape=[jax.ShapeDtypeStruct((owners, CH + short, PAIR), F32), plane, plane],
+        out_shape=[jax.ShapeDtypeStruct(pieces, F32), plane, plane],
         scratch_shapes=[tokens] * 5
-        + [
-            pltpu.VMEM((owners, CH + short, PAIR), F32),
-            floats,
-            floats,
-            pltpu.VMEM((WIDTH, PAIR), F32),
-            sems((groups, 5)),
-            sems((groups, 3)),
-        ],
+        + [pltpu.VMEM(pieces, F32), floats, floats, sems((groups, 5)), sems((groups, 3))],
     )(k, v, raw, rates, logs)
-    slots = lax.all_to_all(slots, "ctx", 0, 0)
+    other = lax.ppermute(mine, "ctx", [(i, i ^ 1) for i in range(owners)])
+    place = lax.axis_index("ctx")
+    late = jnp.broadcast_to((place % 2).astype(F32), (1, PAIR))
+    slots = call(
+        functools.partial(compose_kernel, columns=columns),
+        out_shape=jax.ShapeDtypeStruct((owners // 2, CH + short, PAIR), F32),
+        scratch_shapes=[pltpu.VMEM((PAIRS, CH, PAIR), F32), pltpu.VMEM((WIDTH, PAIR), F32)],
+    )(mine, other, late)
+    same_core = [list(range(core, owners, 2)) for core in range(2)]
+    slots = lax.all_to_all(slots, "ctx", 0, 0, axis_index_groups=same_core)
 
     read, local, base = call(
         read_kernel,
-        in_specs=[hbm] * 8 + [vmem] * 2,
+        in_specs=[hbm] * 8 + [vmem] * 4,
         out_specs=[hbm] * 3,
         out_shape=[plane] * 3,
         scratch_shapes=[tokens] * 6 + [floats] * 5 + [sems((groups, 8)), sems((groups, 3))],
-    )(q, k, v, raw, rates, logs, w, u, boost.reshape(1, WIDTH), shift.reshape(1, WIDTH))
-
-    place = lax.axis_index("ctx")
+    )(q, k, v, raw, rates, logs, w, u, boost.reshape(1, WIDTH), shift.reshape(1, WIDTH), other, late)
+
     own = lax.broadcasted_iota(jnp.int32, (2 * short, PAIR), 0)
     half = lax.broadcasted_iota(jnp.int32, (2 * short, PAIR), 1) // CH
     mask = ((place * columns + own) // CH % 2 == half) & (own < columns)

time: 72.4 us -> 67.1 us (0.927)
  waiting for transfers between devices: 20.6 us -> 12.5 us
  starting transfers between devices: 16.1 us -> 19 us
    all_to_all x1, waiting for transfers between devices: 11 us -> 1.23 us  [shards(): slots = lax.all_to_all(slots, 'ctx', 0, 0, axis_index_groups=same_core)]
    ppermute x0 -> x1, starting transfers between devices: none -> 8.77 us  [shards(): other = lax.ppermute(mine, 'ctx', [(i, i ^ 1) for i in range(owners)])]
    all_to_all x1, starting transfers between devices: 10.6 us -> 3.93 us  [shards(): slots = lax.all_to_all(slots, 'ctx', 0, 0, axis_index_groups=same_core)]
    pallas_call x1, Pallas kernels: 4.81 us -> 2.58 us  [shards(): call(scan_kernel, in_specs=[vmem, vmem, vmem, hbm], out_specs=[hbm, vmem]...]
    pallas_call x2 -> x3, Pallas kernels: 12.9 us -> 15 us  [the longest x1 8.48 us: shards(): call(local_kernel, in_specs=[hbm] * 5, out_specs=[hbm] * 3, out_shape=[ja...]
    ppermute x0 -> x1, waiting for transfers between devices: none -> 1.69 us  [shards(): other = lax.ppermute(mine, 'ctx', [(i, i ^ 1) for i in range(owners)])]
    all_to_all x1, starting transfers between devices: 5.51 us -> 6.31 us  [shards(): starts = lax.all_to_all(starts, 'ctx', 0, 0)]
    unnamed x48 -> x46, local copies, waits for them, and re-layouts: 13.1 us -> 13.1 us
  transfers between devices with their start and end apart: 2 -> 3, of which waited for: 2 -> 3; matrix products, arithmetic and copies ran while one was open for 1% -> 1% of each run, Pallas kernels for 5% -> 7%
where the time goes in v2:
time: 67.1 us; the launch traced here: 66.3 us
  Pallas kernels  19.9 us (30%)
  starting transfers between devices  19 us (28%)
  local copies, waits for them, and re-layouts  13.7 us (20%)
  waiting for transfers between devices  12.5 us (19%)
  between operations  1.05 us (2%)
    unnamed x46, local copies, waits for them, and re-layouts  13.1 us
    all_to_all x1, waiting for transfers between devices, shards(): starts = lax.all_to_all(starts, 'ctx', 0, 0)  9.54 us
    ppermute x1, starting transfers between devices, shards(): other = lax.ppermute(mine, 'ctx', [(i, i ^ 1) for i in range(owners)])  8.77 us
    pallas_call x1, Pallas kernels, shards(): call(local_kernel, in_specs=[hbm] * 5, out_specs=[hbm] * 3, out_shape=[ja...  8.48 us
    all_to_all x1, starting transfers between devices, shards(): starts = lax.all_to_all(starts, 'ctx', 0, 0)  6.31 us
    pallas_call x1, Pallas kernels, shards(): call(read_kernel, in_specs=[hbm] * 8 + [vmem] * 4, out_specs=[hbm] * 3, o...  4.82 us
    all_to_all x1, starting transfers between devices, shards(): slots = lax.all_to_all(slots, 'ctx', 0, 0, axis_index_groups=same_core)  3.93 us
    pallas_call x1, Pallas kernels, shards(): call(scan_kernel, in_specs=[vmem, vmem, vmem, hbm], out_specs=[hbm, vmem]...  2.58 us
  transfers between devices with their start and end apart: 3, of which 3 were waited for; matrix products, arithmetic and copies ran while one was open for 1% of the time, Pallas kernels for 7%

profile of v2, /device:TPU:1, one launch (start us, length us, event | category | flops | bytes accessed | tf_op | source)
XLA Modules:
  0.0 66.3 jit_solution(11883501063881747792)
XLA Ops:
  0.6 0.0 copy-start
  0.6 1.0 %copy-done = bf16[128,1280]{1,0:T(8,128)(2,1)S(1)} copy-done((bf16[128,1280]{1,0:T(8,128)(2,1)S(1)}, bf16[128,1280]{1,0:T(8,128)(2,1)}, u32[]{:S(2)}) %copy-start) | copy-done | bytes 327704
  1.6 0.0 copy-start.2
  1.6 1.0 %copy-done.2 = bf16[128,1280]{1,0:T(8,128)(2,1)S(1)} copy-done((bf16[128,1280]{1,0:T(8,128)(2,1)S(1)}, bf16[128,1280]{1,0:T(8,128)(2,1)}, u32[]{:S(2)}) %copy-start.2) | copy-done | bytes 327704
  2.6 0.0 copy-start.4
  2.6 1.0 %copy-done.4 = bf16[128,1280]{1,0:T(8,128)(2,1)S(1)} copy-done((bf16[128,1280]{1,0:T(8,128)(2,1)S(1)}, bf16[128,1280]{1,0:T(8,128)(2,1)}, u32[]{:S(2)}) %copy-start.4) | copy-done | bytes 327704
  3.6 1.0 %copy-done.6 = bf16[128,1280]{1,0:T(8,128)(2,1)S(1)} copy-done((bf16[128,1280]{1,0:T(8,128)(2,1)S(1)}, bf16[128,1280]{1,0:T(8,128)(2,1)}, u32[]{:S(2)}) %copy-start.6) | copy-done | bytes 327704
  4.5 1.0 %copy-done.8 = bf16[128,1280]{1,0:T(8,128)(2,1)S(1)} copy-done((bf16[128,1280]{1,0:T(8,128)(2,1)S(1)}, bf16[128,1280]{1,0:T(8,128)(2,1)}, u32[]{:S(2)}) %copy-start.8) | copy-done | bytes 327704
  5.5 8.5 %shard_map.113 = (f32[2,10,64,128]{3,2,1,0:T(8,128)S(1)}, f32[128,1280]{1,0:T(8,128)S(1)}, f32[128,1280]{1,0:T(8,128)S(1)}) custom-call(bf16[128,1280]{1,0:T(8,128)(2,1)S(1)} %copy-done, bf16[128,1280]{1,0:T(8,128)(2,1)S(1)} %copy-done.2, bf16[128,1280]{1,0:T(8,128)(2,1)S(1)} %copy-done.4, bf16[128,1280]{1,0:T(8,128)(2,1)S(1)} %copy-done.6, ...), custom_call_target="tpu_custom_call" | custom-call | tf_op jit(solution)/shard_map/pallas_call | solution.py:417
  14.0 0.0 copy-start.14
  14.0 0.9 %copy-done.14 = f32[128,1280]{1,0:T(8,128)} copy-done((f32[128,1280]{1,0:T(8,128)}, f32[128,1280]{1,0:T(8,128)S(1)}, u32[]{:S(2)}) %copy-start.14) | copy-done | bytes 655384
  14.9 0.8 %copy-done.16 = f32[128,1280]{1,0:T(8,128)} copy-done((f32[128,1280]{1,0:T(8,128)}, f32[128,1280]{1,0:T(8,128)S(1)}, u32[]{:S(2)}) %copy-start.16) | copy-done | bytes 655384
  15.7 8.8 %collective-permute-start = (f32[2,10,64,128]{3,2,1,0:T(8,128)S(1)}, f32[2,10,64,128]{3,2,1,0:T(8,128)S(1)}, u32[]{:S(2)}, u32[]{:S(2)}) collective-permute-start(f32[2,10,64,128]{3,2,1,0:T(8,128)S(1)} %get-tuple-element.10.mine_ref), channel_id=1, source_target_pairs={{0,1},{1,0},{2,3},{3,2},{4,5},{5,4},{6,7},{7,6},{8,9},{9,8},{10,11... | collective-permute-start | bytes 1966088 | tf_op jit(solution)/shard_map/ppermute | solution.py:425
  24.5 1.7 %collective-permute-done.other_ref.refs_10_ = f32[2,10,64,128]{3,2,1,0:T(8,128)S(1)} collective-permute-done((f32[2,10,64,128]{3,2,1,0:T(8,128)S(1)}, f32[2,10,64,128]{3,2,1,0:T(8,128)S(1)}, u32[]{:S(2)}, u32[]{:S(2)}) %collective-permute-start) | collective-permute-done | bytes 655392 | tf_op jit(solution)/shard_map/ppermute | solution.py:425
  26.2 1.7 %shard_map.114 = f32[16,88,128]{2,1,0:T(8,128)} custom-call(f32[2,10,64,128]{3,2,1,0:T(8,128)S(1)} %get-tuple-element.10.mine_ref, f32[2,10,64,128]{3,2,1,0:T(8,128)S(1)} %collective-permute-done.other_ref.refs_10_, f32[1,128]{1,0:T(1,128)S(1)} %broadcast_in_dim.3.late_ref.refs_11_), custom_call_target="tpu_custom_call" | custom-call | tf_op jit(solution)/shard_map/pallas_call | solution.py:428
  27.9 0.0 copy-start.5
  27.9 0.0 copy-start.7
  27.9 3.9 %all-to-all-start = ((f32[16,88,128]{2,1,0:T(8,128)}), f32[16,88,128]{2,1,0:T(8,128)S(1)}, u32[]{:S(2)}, u32[]{:S(2)}) async-start(f32[16,88,128]{2,1,0:T(8,128)} %shard_map.114), calls=%async_computation | async-start | bytes 1441792 | tf_op jit(solution)/shard_map/all_to_all | solution.py:434
  31.9 0.0 copy-start.19
  31.9 0.0 copy-done.20
  31.9 0.0 copy-done.21
  31.9 0.7 copy-done.19
  32.6 0.1 pad_maximum_fusion.entry_ref
  32.7 0.1 fusion.3.mask_ref
  32.8 0.0 copy-done.1
  32.8 0.0 copy-done.3
  32.8 0.0 copy-done.5
  32.9 0.0 copy-done.7
  32.9 0.0 copy-start.9
  32.9 1.0 %copy-done.9 = bf16[128,1280]{1,0:T(8,128)(2,1)S(1)} copy-done((bf16[128,1280]{1,0:T(8,128)(2,1)S(1)}, bf16[128,1280]{1,0:T(8,128)(2,1)}, u32[]{:S(2)}) %copy-start.9) | copy-done | bytes 327704
  33.8 1.1 %copy-done.15 = f32[128,1280]{1,0:T(8,128)S(1)} copy-done((f32[128,1280]{1,0:T(8,128)S(1)}, f32[128,1280]{1,0:T(8,128)}, u32[]{:S(2)}) %copy-start.15) | copy-done | bytes 655384
  34.9 1.1 %copy-done.17 = f32[128,1280]{1,0:T(8,128)S(1)} copy-done((f32[128,1280]{1,0:T(8,128)S(1)}, f32[128,1280]{1,0:T(8,128)}, u32[]{:S(2)}) %copy-start.17) | copy-done | bytes 655384
  36.0 1.0 %copy-done.18 = bf16[128,1280]{1,0:T(8,128)(2,1)S(1)} copy-done((bf16[128,1280]{1,0:T(8,128)(2,1)S(1)}, bf16[128,1280]{1,0:T(8,128)(2,1)}, u32[]{:S(2)}) %copy-start.18) | copy-done | bytes 327704
  37.0 4.8 %shard_map.115 = (f32[128,1280]{1,0:T(8,128)S(1)}, f32[128,1280]{1,0:T(8,128)S(1)}, f32[128,1280]{1,0:T(8,128)S(1)}) custom-call(bf16[128,1280]{1,0:T(8,128)(2,1)S(1)} %copy-done.18, bf16[128,1280]{1,0:T(8,128)(2,1)S(1)} %copy-done.1, bf16[128,1280]{1,0:T(8,128)(2,1)S(1)} %copy-done.3, bf16[128,1280]{1,0:T(8,128)(2,1)S(1)} %copy-done.5, ...), custom_call_target="tpu_custom_call" | custom-call | tf_op jit(solution)/shard_map/pallas_call | solution.py:436
  41.8 0.0 copy-start.10
  41.8 0.9 %copy-done.10 = f32[128,1280]{1,0:T(8,128)} copy-done((f32[128,1280]{1,0:T(8,128)}, f32[128,1280]{1,0:T(8,128)S(1)}, u32[]{:S(2)}) %copy-start.10) | copy-done | bytes 655384
  42.7 0.8 %copy-done.12 = f32[128,1280]{1,0:T(8,128)} copy-done((f32[128,1280]{1,0:T(8,128)}, f32[128,1280]{1,0:T(8,128)S(1)}, u32[]{:S(2)}) %copy-start.12) | copy-done | bytes 655384
  43.5 1.2 %all-to-all-done.slots_ref = f32[16,88,128]{2,1,0:T(8,128)S(1)} async-done(((f32[16,88,128]{2,1,0:T(8,128)}), f32[16,88,128]{2,1,0:T(8,128)S(1)}, u32[]{:S(2)}, u32[]{:S(2)}) %all-to-all-start) | async-done | bytes 720928 | tf_op jit(solution)/shard_map/all_to_all | solution.py:434
  44.8 2.6 %shard_map.116 = (f32[32,24,128]{2,1,0:T(8,128)}, f32[48,128]{1,0:T(8,128)S(1)}) custom-call(f32[16,88,128]{2,1,0:T(8,128)S(1)} %all-to-all-done.slots_ref, f32[48,128]{1,0:T(8,128)S(1)} %pad_maximum_fusion.entry_ref, f32[48,128]{1,0:T(8,128)S(1)} %fusion.3.mask_ref, f32[128,1280]{1,0:T(8,128)S(1)} %get-tuple-element.13.after_ref.base_in), custom_call_target="tpu_custom_call" | custom-call | tf_op jit(solution)/shard_map/pallas_call | solution.py:448
  47.3 0.0 copy-start.11
  47.3 0.0 copy-start.22
  47.4 6.3 %all-to-all-start.1 = ((f32[32,24,128]{2,1,0:T(8,128)}), f32[32,24,128]{2,1,0:T(8,128)S(1)}, u32[]{:S(2)}, u32[]{:S(2)}) async-start(f32[32,24,128]{2,1,0:T(8,128)} %get-tuple-element.14), calls=%async_computation.1 | async-start | bytes 786432 | tf_op jit(solution)/shard_map/all_to_all | solution.py:458
  53.7 0.0 copy-done.22
  53.7 0.6 slice_bitcast_fusion
  54.3 9.5 %all-to-all-done.1.starts_ref = f32[32,24,128]{2,1,0:T(8,128)S(1)} async-done(((f32[32,24,128]{2,1,0:T(8,128)}), f32[32,24,128]{2,1,0:T(8,128)S(1)}, u32[]{:S(2)}, u32[]{:S(2)}) %all-to-all-start.1) | async-done | bytes 393248 | tf_op jit(solution)/shard_map/all_to_all | solution.py:458
  63.9 0.0 copy-done.13
  63.9 0.0 copy-done.11
  63.9 2.3 %shard_map.117 = bf16[128,1280]{1,0:T(8,128)(2,1)} custom-call(f32[32,24,128]{2,1,0:T(8,128)S(1)} %all-to-all-done.1.starts_ref, f32[128,1280]{1,0:T(8,128)S(1)} %copy-done.11, f32[128,1280]{1,0:T(8,128)S(1)} %copy-done.13, f32[128,1280]{1,0:T(8,128)S(1)} %get-tuple-element.13.after_ref.base_in, f32[1,1280]{1,0:T(1,128)S(1)} %reshape.15.gain_ref), custom_call_target="tpu_custom_call" | custom-call | tf_op jit(solution)/shard_map/pallas_call | solution.py:461
  (21 shorter events, 0.1 us)
Async XLA Ops:
  0.6 1.0 %copy-start = (bf16[128,1280]{1,0:T(8,128)(2,1)S(1)}, bf16[128,1280]{1,0:T(8,128)(2,1)}, u32[]{:S(2)}) copy-start(bf16[128,1280]{1,0:T(8,128)(2,1)} %refs_1_.3) | copy-start | bytes 983044
  1.6 1.0 %copy-start.2 = (bf16[128,1280]{1,0:T(8,128)(2,1)S(1)}, bf16[128,1280]{1,0:T(8,128)(2,1)}, u32[]{:S(2)}) copy-start(bf16[128,1280]{1,0:T(8,128)(2,1)} %refs_2_.3) | copy-start | bytes 983044
  2.6 1.0 %copy-start.4 = (bf16[128,1280]{1,0:T(8,128)(2,1)S(1)}, bf16[128,1280]{1,0:T(8,128)(2,1)}, u32[]{:S(2)}) copy-start(bf16[128,1280]{1,0:T(8,128)(2,1)} %refs_3_.3) | copy-start | bytes 983044
  3.6 1.0 %copy-start.6 = (bf16[128,1280]{1,0:T(8,128)(2,1)S(1)}, bf16[128,1280]{1,0:T(8,128)(2,1)}, u32[]{:S(2)}) copy-start(bf16[128,1280]{1,0:T(8,128)(2,1)} %refs_4_.3) | copy-start | bytes 983044
  4.5 1.0 %copy-start.8 = (bf16[128,1280]{1,0:T(8,128)(2,1)S(1)}, bf16[128,1280]{1,0:T(8,128)(2,1)}, u32[]{:S(2)}) copy-start(bf16[128,1280]{1,0:T(8,128)(2,1)} %refs_5_.1) | copy-start | bytes 983044
  14.0 0.9 %copy-start.14 = (f32[128,1280]{1,0:T(8,128)}, f32[128,1280]{1,0:T(8,128)S(1)}, u32[]{:S(2)}) copy-start(f32[128,1280]{1,0:T(8,128)S(1)} %get-tuple-element.11.refs_6_) | copy-start | bytes 1966084
  14.9 0.8 %copy-start.16 = (f32[128,1280]{1,0:T(8,128)}, f32[128,1280]{1,0:T(8,128)S(1)}, u32[]{:S(2)}) copy-start(f32[128,1280]{1,0:T(8,128)S(1)} %get-tuple-element.12.refs_7_) | copy-start | bytes 1966084
  15.7 10.5 %collective-permute-start = (f32[2,10,64,128]{3,2,1,0:T(8,128)S(1)}, f32[2,10,64,128]{3,2,1,0:T(8,128)S(1)}, u32[]{:S(2)}, u32[]{:S(2)}) collective-permute-start(f32[2,10,64,128]{3,2,1,0:T(8,128)S(1)} %get-tuple-element.10.mine_ref), channel_id=1, source_target_pairs={{0,1},{1,0},{2,3},{3,2},{4,5},{5,4},{6,7},{7,6},{8,9},{9,8},{10,11... | collective-permute-start | bytes 1966088 | tf_op jit(solution)/shard_map/ppermute | solution.py:425
  27.9 4.0 %copy-start.20 = (f32[1280]{0:T(1024)S(1)}, f32[1280]{0:T(1024)}, u32[]{:S(2)}) copy-start(f32[1280]{0:T(1024)} %param.17) | copy-start | bytes 15364
  27.9 4.0 %copy-start.21 = (f32[1280]{0:T(1024)S(1)}, f32[1280]{0:T(1024)}, u32[]{:S(2)}) copy-start(f32[1280]{0:T(1024)} %param.19) | copy-start | bytes 15364
  27.9 4.9 %copy-start.1 = (bf16[128,1280]{1,0:T(8,128)(2,1)S(1)}, bf16[128,1280]{1,0:T(8,128)(2,1)}, u32[]{:S(2)}) copy-start(bf16[128,1280]{1,0:T(8,128)(2,1)} %refs_1_.3) | copy-start | bytes 983044
  27.9 4.9 %copy-start.3 = (bf16[128,1280]{1,0:T(8,128)(2,1)S(1)}, bf16[128,1280]{1,0:T(8,128)(2,1)}, u32[]{:S(2)}) copy-start(bf16[128,1280]{1,0:T(8,128)(2,1)} %refs_2_.3) | copy-start | bytes 983044
  27.9 4.9 %copy-start.5 = (bf16[128,1280]{1,0:T(8,128)(2,1)S(1)}, bf16[128,1280]{1,0:T(8,128)(2,1)}, u32[]{:S(2)}) copy-start(bf16[128,1280]{1,0:T(8,128)(2,1)} %refs_3_.3) | copy-start | bytes 983044
  27.9 4.9 %copy-start.7 = (bf16[128,1280]{1,0:T(8,128)(2,1)S(1)}, bf16[128,1280]{1,0:T(8,128)(2,1)}, u32[]{:S(2)}) copy-start(bf16[128,1280]{1,0:T(8,128)(2,1)} %refs_4_.3) | copy-start | bytes 983044
  27.9 16.8 %all-to-all-start = ((f32[16,88,128]{2,1,0:T(8,128)}), f32[16,88,128]{2,1,0:T(8,128)S(1)}, u32[]{:S(2)}, u32[]{:S(2)}) async-start(f32[16,88,128]{2,1,0:T(8,128)} %shard_map.114), calls=%async_computation | async-start | bytes 1441792 | tf_op jit(solution)/shard_map/all_to_all | solution.py:434
  31.9 0.7 %copy-start.19 = (f32[64,40]{0,1:T(8,128)S(1)}, f32[64,40]{0,1:T(8,128)}, u32[]{:S(2)}) copy-start(f32[64,40]{0,1:T(8,128)} %param.16) | copy-start | bytes 30724
  32.9 1.0 %copy-start.9 = (bf16[128,1280]{1,0:T(8,128)(2,1)S(1)}, bf16[128,1280]{1,0:T(8,128)(2,1)}, u32[]{:S(2)}) copy-start(bf16[128,1280]{1,0:T(8,128)(2,1)} %refs_5_.1) | copy-start | bytes 983044
  33.8 1.1 %copy-start.15 = (f32[128,1280]{1,0:T(8,128)S(1)}, f32[128,1280]{1,0:T(8,128)}, u32[]{:S(2)}) copy-start(f32[128,1280]{1,0:T(8,128)} %copy-done.14) | copy-start | bytes 1966084
  34.9 1.1 %copy-start.17 = (f32[128,1280]{1,0:T(8,128)S(1)}, f32[128,1280]{1,0:T(8,128)}, u32[]{:S(2)}) copy-start(f32[128,1280]{1,0:T(8,128)} %copy-done.16) | copy-start | bytes 1966084
  36.0 1.0 %copy-start.18 = (bf16[128,1280]{1,0:T(8,128)(2,1)S(1)}, bf16[128,1280]{1,0:T(8,128)(2,1)}, u32[]{:S(2)}) copy-start(bf16[128,1280]{1,0:T(8,128)(2,1)} %refs_0_.3) | copy-start | bytes 983044
  41.8 0.9 %copy-start.10 = (f32[128,1280]{1,0:T(8,128)}, f32[128,1280]{1,0:T(8,128)S(1)}, u32[]{:S(2)}) copy-start(f32[128,1280]{1,0:T(8,128)S(1)} %get-tuple-element.15.read_in) | copy-start | bytes 1966084
  42.7 0.8 %copy-start.12 = (f32[128,1280]{1,0:T(8,128)}, f32[128,1280]{1,0:T(8,128)S(1)}, u32[]{:S(2)}) copy-start(f32[128,1280]{1,0:T(8,128)S(1)} %get-tuple-element.16.local_in) | copy-start | bytes 1966084
  44.7 19.1 %copy-start.13 = (f32[128,1280]{1,0:T(8,128)S(1)}, f32[128,1280]{1,0:T(8,128)}, u32[]{:S(2)}) copy-start(f32[128,1280]{1,0:T(8,128)} %copy-done.12) | copy-start | bytes 1966084
  47.3 16.5 %copy-start.11 = (f32[128,1280]{1,0:T(8,128)S(1)}, f32[128,1280]{1,0:T(8,128)}, u32[]{:S(2)}) copy-start(f32[128,1280]{1,0:T(8,128)} %copy-done.10) | copy-start | bytes 1966084
  47.3 6.3 %copy-start.22 = (f32[1280]{0:T(1024)S(1)}, f32[1280]{0:T(1024)}, u32[]{:S(2)}) copy-start(f32[1280]{0:T(1024)} %param.18) | copy-start | bytes 15364
  47.4 16.5 %all-to-all-start.1 = ((f32[32,24,128]{2,1,0:T(8,128)}), f32[32,24,128]{2,1,0:T(8,128)S(1)}, u32[]{:S(2)}, u32[]{:S(2)}) async-start(f32[32,24,128]{2,1,0:T(8,128)} %get-tuple-element.14), calls=%async_computation.1 | async-start | bytes 786432 | tf_op jit(solution)/shard_map/all_to_all | solution.py:458

commit v3 on v2

--- a/solution.py
+++ b/solution.py
@@ -43,6 +43,12 @@
     return out[:, :PAIR] + out[:, PAIR:]
 
 
+def stacked(a, b):
+    n = a[0].shape[0]
+    out = mxu(rows(*a), lanes(*b))
+    return out[:n, :PAIR] + out[:n, PAIR:] + out[n:, :PAIR]
+
+
 def wide(a, b):
     return mxu(lanes(*a), rows(b[0], b[0])) + mxu(a[0], b[1])
 
@@ -106,8 +112,8 @@
     while size < slab:
         joins = (apart >= size) & (apart < 2 * size)
         halves = [split(x) for x in solver]
-        mid = [square(split(jnp.where(joins, x, 0.0)), spread(t)) for x, t in zip(small, halves)]
-        solver = [x + square(t, spread(split(m))) for x, t, m in zip(solver, halves, mid)]
+        mid = [stacked(split(jnp.where(joins, x, 0.0)), spread(t)) for x, t in zip(small, halves)]
+        solver = [x + stacked(t, spread(split(m))) for x, t, m in zip(solver, halves, mid)]
         size *= 2
     halves = [spread(split(x)) for x in solver]
     solver = [rows(*[x] * count) * same for x in solver]
@@ -124,10 +130,10 @@
         apart = odd(iota((n, n), 0) ^ iota((n, n), 1))
         joins = (apart >= size) & (apart < 2 * size)
         gap = jnp.zeros((size, n), BF16)
-        mid = [square(split(jnp.where(joins, odd(x), 0.0)), t) for x, t in zip(inner, halves)]
+        mid = [stacked(split(jnp.where(joins, odd(x), 0.0)), t) for x, t in zip(inner, halves)]
         mid = [tuple(joined(lambda i: gap, m) for m in split(x)) for x in mid]
         later = [
-            odd(x) + square((odd(t[0]), odd(t[1])), m) for x, t, m in zip(solver, halves, mid)
+            odd(x) + stacked((odd(t[0]), odd(t[1])), m) for x, t, m in zip(solver, halves, mid)
         ]
         halves = [
             tuple(joined(lambda i: old[i : i + size], new) for old, new in zip(t, split(x)))
@@ -407,8 +413,10 @@
     short = (columns + 15) // 16 * 8
     groups = PAIRS // GROUP
     hbm = pl.BlockSpec(memory_space=pltpu.HBM)
+    held = functools.partial(pltpu.with_memory_space_constraint, memory_space=pltpu.HBM)
     vmem = pl.BlockSpec(memory_space=pltpu.VMEM)
-    plane = jax.ShapeDtypeStruct((n, WIDTH), F32)
+    plane = pltpu.HBM((n, WIDTH), F32)
+    arrays = [held(x) for x in (q, k, v, raw, rates, logs)]
     tokens = pltpu.VMEM((n, WIDTH), BF16)
     floats = pltpu.VMEM((n, WIDTH), F32)
     sems = pltpu.SemaphoreType.DMA
@@ -421,7 +429,7 @@
         out_shape=[jax.ShapeDtypeStruct(pieces, F32), plane, plane],
         scratch_shapes=[tokens] * 5
         + [pltpu.VMEM(pieces, F32), floats, floats, sems((groups, 5)), sems((groups, 3))],
-    )(k, v, raw, rates, logs)
+    )(*arrays[1:])
     other = lax.ppermute(mine, "ctx", [(i, i ^ 1) for i in range(owners)])
     place = lax.axis_index("ctx")
     late = jnp.broadcast_to((place % 2).astype(F32), (1, PAIR))
@@ -439,7 +447,7 @@
         out_specs=[hbm] * 3,
         out_shape=[plane] * 3,
         scratch_shapes=[tokens] * 6 + [floats] * 5 + [sems((groups, 8)), sems((groups, 3))],
-    )(q, k, v, raw, rates, logs, w, u, boost.reshape(1, WIDTH), shift.reshape(1, WIDTH), other, late)
+    )(*arrays, held(w), held(u), boost.reshape(1, WIDTH), shift.reshape(1, WIDTH), other, late)
 
     own = lax.broadcasted_iota(jnp.int32, (2 * short, PAIR), 0)
     half = lax.broadcasted_iota(jnp.int32, (2 * short, PAIR), 1) // CH
@@ -450,11 +458,11 @@
         in_specs=[vmem, vmem, vmem, hbm],
         out_specs=[hbm, vmem],
         out_shape=[
-            jax.ShapeDtypeStruct((owners, short, PAIR), F32),
+            pltpu.HBM((owners, short, PAIR), F32),
             jax.ShapeDtypeStruct((2 * short, PAIR), F32),
         ],
         scratch_shapes=[pltpu.VMEM((owners, short, PAIR), F32), sems((4,))],
-    )(slots, jnp.concatenate([entry, entry], axis=1), mask.astype(F32), base)
+    )(slots, jnp.concatenate([entry, entry], axis=1), mask.astype(F32), held(base))
     starts = lax.all_to_all(starts, "ctx", 0, 0)
     exit_state = final[:columns, :CH].T
 
@@ -462,10 +470,10 @@
         functools.partial(final_kernel, columns=columns),
         in_specs=[vmem, hbm, hbm, hbm, vmem],
         out_specs=hbm,
-        out_shape=jax.ShapeDtypeStruct((n, WIDTH), BF16),
+        out_shape=pltpu.HBM((n, WIDTH), BF16),
         scratch_shapes=[floats] * 3
         + [pltpu.VMEM((WIDTH, PAIR), F32), tokens, sems((groups, 3)), sems((PAIRS,))],
-    )(starts, read, local, base, gain.reshape(1, WIDTH))
+    )(starts, held(read), held(local), held(base), gain.reshape(1, WIDTH))
     return out, exit_state
 
 

time: 67.1 us -> 61.2 us (0.912)
  local copies, waits for them, and re-layouts: 13.7 us -> 1.31 us
  Pallas kernels: 19.9 us -> 24.1 us
  waiting for transfers between devices: 12.5 us -> 16.4 us
  starting transfers between devices: 19 us -> 17.7 us
    unnamed x46 -> x8, local copies, waits for them, and re-layouts: 13.1 us -> 0.68 us
    all_to_all x1, waiting for transfers between devices: 1.23 us -> 5.09 us  [shards(): slots = lax.all_to_all(slots, 'ctx', 0, 0, axis_index_groups=same_core)]
    pallas_call x1, Pallas kernels: 4.82 us -> 6.83 us  [shards(): call(read_kernel, in_specs=[hbm] * 8 + [vmem] * 4, out_specs=[hbm] * 3, o...]
    all_to_all x1, starting transfers between devices: 6.31 us -> 5.04 us  [shards(): starts = lax.all_to_all(starts, 'ctx', 0, 0)]
    pallas_call x1, Pallas kernels: 8.48 us -> 9.64 us  [shards(): call(local_kernel, in_specs=[hbm] * 5, out_specs=[hbm] * 3, out_shape=[ja...]
    pallas_call x1, Pallas kernels: 2.33 us -> 3.28 us  [shards(): call(functools.partial(final_kernel, columns=columns), in_specs=[vmem, hb...]
  transfers between devices with their start and end apart: 3 -> 3, of which waited for: 3 -> 3; matrix products, arithmetic and copies ran while one was open for 1% -> 1% of each run, Pallas kernels for 7% -> 11%
where the time goes in v3:
time: 61.2 us; the launch traced here: 60.7 us
  Pallas kernels  24.1 us (39%)
  starting transfers between devices  17.7 us (29%)
  waiting for transfers between devices  16.4 us (27%)
  local copies, waits for them, and re-layouts  1.31 us (2%)
  between operations  0.94 us (2%)
    all_to_all x1, waiting for transfers between devices, shards(): starts = lax.all_to_all(starts, 'ctx', 0, 0)  9.65 us
    pallas_call x1, Pallas kernels, shards(): call(local_kernel, in_specs=[hbm] * 5, out_specs=[hbm] * 3, out_shape=[ja...  9.64 us
    ppermute x1, starting transfers between devices, shards(): other = lax.ppermute(mine, 'ctx', [(i, i ^ 1) for i in range(owners)])  8.79 us
    pallas_call x1, Pallas kernels, shards(): call(read_kernel, in_specs=[hbm] * 8 + [vmem] * 4, out_specs=[hbm] * 3, o...  6.83 us
    all_to_all x1, waiting for transfers between devices, shards(): slots = lax.all_to_all(slots, 'ctx', 0, 0, axis_index_groups=same_core)  5.09 us
    all_to_all x1, starting transfers between devices, shards(): starts = lax.all_to_all(starts, 'ctx', 0, 0)  5.04 us
    all_to_all x1, starting transfers between devices, shards(): slots = lax.all_to_all(slots, 'ctx', 0, 0, axis_index_groups=same_core)  3.91 us
    pallas_call x1, Pallas kernels, shards(): call(functools.partial(final_kernel, columns=columns), in_specs=[vmem, hb...  3.28 us
  transfers between devices with their start and end apart: 3, of which 3 were waited for; matrix products, arithmetic and copies ran while one was open for 1% of the time, Pallas kernels for 11%

profile of v3, /device:TPU:1, one launch (start us, length us, event | category | flops | bytes accessed | tf_op | source)
XLA Modules:
  0.0 60.7 jit_solution(2956965129882428675)
XLA Ops:
  0.6 9.6 %shard_map.113 = (f32[2,10,64,128]{3,2,1,0:T(8,128)S(1)}, f32[128,1280]{1,0:T(8,128)}, f32[128,1280]{1,0:T(8,128)}) custom-call(bf16[128,1280]{1,0:T(8,128)(2,1)} %refs_1_.3, bf16[128,1280]{1,0:T(8,128)(2,1)} %refs_2_.3, bf16[128,1280]{1,0:T(8,128)(2,1)} %refs_3_.3, bf16[128,1280]{1,0:T(8,128)(2,1)} %refs_4_.3, bf16[128,1280]{1,0:T(8,128)(2,1)} %refs_5_.1), custom_call_target="tpu_custom_call" | custom-call | tf_op jit(solution)/shard_map/pallas_call | solution.py:425
  10.3 8.8 %collective-permute-start = (f32[2,10,64,128]{3,2,1,0:T(8,128)S(1)}, f32[2,10,64,128]{3,2,1,0:T(8,128)S(1)}, u32[]{:S(2)}, u32[]{:S(2)}) collective-permute-start(f32[2,10,64,128]{3,2,1,0:T(8,128)S(1)} %get-tuple-element.10.mine_ref), channel_id=1, source_target_pairs={{0,1},{1,0},{2,3},{3,2},{4,5},{5,4},{6,7},{7,6},{8,9},{9,8},{10,11... | collective-permute-start | bytes 1966088 | tf_op jit(solution)/shard_map/ppermute | solution.py:433
  19.1 1.7 %collective-permute-done.other_ref.refs_10_ = f32[2,10,64,128]{3,2,1,0:T(8,128)S(1)} collective-permute-done((f32[2,10,64,128]{3,2,1,0:T(8,128)S(1)}, f32[2,10,64,128]{3,2,1,0:T(8,128)S(1)}, u32[]{:S(2)}, u32[]{:S(2)}) %collective-permute-start) | collective-permute-done | bytes 655392 | tf_op jit(solution)/shard_map/ppermute | solution.py:433
  20.8 1.7 %shard_map.114 = f32[16,88,128]{2,1,0:T(8,128)} custom-call(f32[2,10,64,128]{3,2,1,0:T(8,128)S(1)} %get-tuple-element.10.mine_ref, f32[2,10,64,128]{3,2,1,0:T(8,128)S(1)} %collective-permute-done.other_ref.refs_10_, f32[1,128]{1,0:T(1,128)S(1)} %broadcast_in_dim.3.late_ref.refs_11_), custom_call_target="tpu_custom_call" | custom-call | tf_op jit(solution)/shard_map/pallas_call | solution.py:436
  22.5 0.0 copy-start.1
  22.5 0.0 copy-start.2
  22.5 3.9 %all-to-all-start = ((f32[16,88,128]{2,1,0:T(8,128)}), f32[16,88,128]{2,1,0:T(8,128)S(1)}, u32[]{:S(2)}, u32[]{:S(2)}) async-start(f32[16,88,128]{2,1,0:T(8,128)} %shard_map.114), calls=%async_computation | async-start | bytes 1441792 | tf_op jit(solution)/shard_map/all_to_all | solution.py:442
  26.4 0.0 copy-start
  26.5 0.0 copy-done.1
  26.5 0.0 copy-done.2
  26.5 0.7 %copy-done = f32[64,40]{0,1:T(8,128)S(1)} copy-done((f32[64,40]{0,1:T(8,128)S(1)}, f32[64,40]{0,1:T(8,128)}, u32[]{:S(2)}) %copy-start) | copy-done | bytes 10264
  27.2 0.1 pad_maximum_fusion.entry_ref
  27.3 0.1 fusion.3.mask_ref
  27.4 6.8 %shard_map.115 = (f32[128,1280]{1,0:T(8,128)}, f32[128,1280]{1,0:T(8,128)}, f32[128,1280]{1,0:T(8,128)}) custom-call(bf16[128,1280]{1,0:T(8,128)(2,1)} %refs_0_.3, bf16[128,1280]{1,0:T(8,128)(2,1)} %refs_1_.3, bf16[128,1280]{1,0:T(8,128)(2,1)} %refs_2_.3, bf16[128,1280]{1,0:T(8,128)(2,1)} %refs_3_.3, bf16[128,1280]{1,0:T(8,128)(2,1)} %refs_4_.3, ...), custom_call_target="tpu_custom_call" | custom-call | tf_op jit(solution)/shard_map/pallas_call | solution.py:444
  34.2 5.1 %all-to-all-done.slots_ref = f32[16,88,128]{2,1,0:T(8,128)S(1)} async-done(((f32[16,88,128]{2,1,0:T(8,128)}), f32[16,88,128]{2,1,0:T(8,128)S(1)}, u32[]{:S(2)}, u32[]{:S(2)}) %all-to-all-start) | async-done | bytes 720928 | tf_op jit(solution)/shard_map/all_to_all | solution.py:442
  39.3 2.6 %shard_map.116 = (f32[32,24,128]{2,1,0:T(8,128)}, f32[48,128]{1,0:T(8,128)S(1)}) custom-call(f32[16,88,128]{2,1,0:T(8,128)S(1)} %all-to-all-done.slots_ref, f32[48,128]{1,0:T(8,128)S(1)} %pad_maximum_fusion.entry_ref, f32[48,128]{1,0:T(8,128)S(1)} %fusion.3.mask_ref, f32[128,1280]{1,0:T(8,128)} %get-tuple-element.13.after_ref.base_in), custom_call_target="tpu_custom_call" | custom-call | tf_op jit(solution)/shard_map/pallas_call | solution.py:456
  41.9 0.0 copy-start.3
  41.9 5.0 %all-to-all-start.1 = ((f32[32,24,128]{2,1,0:T(8,128)}), f32[32,24,128]{2,1,0:T(8,128)S(1)}, u32[]{:S(2)}, u32[]{:S(2)}) async-start(f32[32,24,128]{2,1,0:T(8,128)} %get-tuple-element.14), calls=%async_computation.1 | async-start | bytes 786432 | tf_op jit(solution)/shard_map/all_to_all | solution.py:466
  47.0 0.0 copy-done.3
  47.0 0.6 %slice_bitcast_fusion = f32[64,40]{0,1:T(8,128)} fusion(f32[48,128]{1,0:T(8,128)S(1)} %get-tuple-element.17), kind=kLoop, calls=%fused_computation.10 | loop fusion | bytes 20480 | tf_op jit(solution)/shard_map/transpose | solution.py:467
  47.6 9.7 %all-to-all-done.1.starts_ref = f32[32,24,128]{2,1,0:T(8,128)S(1)} async-done(((f32[32,24,128]{2,1,0:T(8,128)}), f32[32,24,128]{2,1,0:T(8,128)S(1)}, u32[]{:S(2)}, u32[]{:S(2)}) %all-to-all-start.1) | async-done | bytes 393248 | tf_op jit(solution)/shard_map/all_to_all | solution.py:466
  57.3 3.3 %shard_map.117 = bf16[128,1280]{1,0:T(8,128)(2,1)} custom-call(f32[32,24,128]{2,1,0:T(8,128)S(1)} %all-to-all-done.1.starts_ref, f32[128,1280]{1,0:T(8,128)} %get-tuple-element.15.read_in, f32[128,1280]{1,0:T(8,128)} %get-tuple-element.16.local_in, f32[128,1280]{1,0:T(8,128)} %get-tuple-element.13.after_ref.base_in, f32[1,1280]{1,0:T(1,128)S(1)} %reshape.15.gain_ref), custom_call_target="tpu_custom_call" | custom-call | tf_op jit(solution)/shard_map/pallas_call | solution.py:469
  (9 shorter events, 0.1 us)
Async XLA Ops:
  10.3 10.5 %collective-permute-start = (f32[2,10,64,128]{3,2,1,0:T(8,128)S(1)}, f32[2,10,64,128]{3,2,1,0:T(8,128)S(1)}, u32[]{:S(2)}, u32[]{:S(2)}) collective-permute-start(f32[2,10,64,128]{3,2,1,0:T(8,128)S(1)} %get-tuple-element.10.mine_ref), channel_id=1, source_target_pairs={{0,1},{1,0},{2,3},{3,2},{4,5},{5,4},{6,7},{7,6},{8,9},{9,8},{10,11... | collective-permute-start | bytes 1966088 | tf_op jit(solution)/shard_map/ppermute | solution.py:433
  22.5 4.0 %copy-start.1 = (f32[1280]{0:T(1024)S(1)}, f32[1280]{0:T(1024)}, u32[]{:S(2)}) copy-start(f32[1280]{0:T(1024)} %param.17) | copy-start | bytes 15364
  22.5 4.0 %copy-start.2 = (f32[1280]{0:T(1024)S(1)}, f32[1280]{0:T(1024)}, u32[]{:S(2)}) copy-start(f32[1280]{0:T(1024)} %param.19) | copy-start | bytes 15364
  22.5 16.8 %all-to-all-start = ((f32[16,88,128]{2,1,0:T(8,128)}), f32[16,88,128]{2,1,0:T(8,128)S(1)}, u32[]{:S(2)}, u32[]{:S(2)}) async-start(f32[16,88,128]{2,1,0:T(8,128)} %shard_map.114), calls=%async_computation | async-start | bytes 1441792 | tf_op jit(solution)/shard_map/all_to_all | solution.py:442
  26.4 0.7 %copy-start = (f32[64,40]{0,1:T(8,128)S(1)}, f32[64,40]{0,1:T(8,128)}, u32[]{:S(2)}) copy-start(f32[64,40]{0,1:T(8,128)} %param.16) | copy-start | bytes 30724
  41.9 5.1 %copy-start.3 = (f32[1280]{0:T(1024)S(1)}, f32[1280]{0:T(1024)}, u32[]{:S(2)}) copy-start(f32[1280]{0:T(1024)} %param.18) | copy-start | bytes 15364
  41.9 15.3 %all-to-all-start.1 = ((f32[32,24,128]{2,1,0:T(8,128)}), f32[32,24,128]{2,1,0:T(8,128)S(1)}, u32[]{:S(2)}, u32[]{:S(2)}) async-start(f32[32,24,128]{2,1,0:T(8,128)} %get-tuple-element.14), calls=%async_computation.1 | async-start | bytes 786432 | tf_op jit(solution)/shard_map/all_to_all | solution.py:466

commit v4 on v2

--- a/solution.py
+++ b/solution.py
@@ -143,75 +143,74 @@
     buffers = refs[8:13]
     pieces, w_all, u_all, in_sems, out_sems = refs[13:]
     n, width = w_all.shape
-    block = GROUP * PAIR
-    groups = width // block
-    loads = [
-        [
-            pltpu.make_async_copy(src.at[:, pl.ds(g * block, block)], dst.at[:, pl.ds(g * block, block)], in_sems.at[g, i])
-            for i, (src, dst) in enumerate(zip(inputs, buffers))
-        ]
-        for g in range(groups)
-    ]
-    for group in loads:
-        for copy in group:
-            copy.start()
+    order = (4, 3, 2, 0, 1)
+    loads = [pltpu.make_async_copy(inputs[i], buffers[i], in_sems.at[i]) for i in range(5)]
+    for i in order:
+        loads[i].start()
     k_ref, v_ref, raw_ref, rate_ref, log_ref = buffers
+    pairs = range(width // PAIR)
+    heads = range(2 * len(pairs))
+    cut = [slice(p * PAIR, (p + 1) * PAIR) for p in pairs]
     low = low_half(n)
     ones = block_ones()
     tril = tril_ones(n)
     strict = iota((n, n), 0) > iota((n, n), 1)
     row, lane = iota((CH, PAIR), 0), iota((CH, PAIR), 1)
+
+    loads[4].wait()
+    cumul = [decays(log_ref[:, c], tril) for c in cut]
+    fall = [jnp.exp(-x) for x in cumul]
+    rise = [jnp.exp(x - log_ref[:, c].astype(F32)) for x, c in zip(cumul, cut)]
+    loads[2].wait()
+    unit = [units(raw_ref[:, c], ones) for c in cut]
+    alpha = [-x * y for x, y in zip(unit, rise)]
+    loads[3].wait()
+    beta = [rate_ref[:, c].astype(F32) * x * y for c, x, y in zip(cut, unit, fall)]
+    loads[0].wait()
+    key = [k_ref[:, c].astype(F32) * x for c, x in zip(cut, fall)]
+    gram = [grams(alpha[p], rows(beta[p], key[p]), low) for p in pairs]
+    inner, cross = [], []
+    for h in heads:
+        part = gram[h // 2][(h % 2) * n : (h % 2 + 1) * n]
+        inner.append(jnp.where(strict, part[:, :n], 0.0))
+        cross.append(jnp.where(strict, part[:, n:], 0.0))
+    loads[1].wait()
+    akv = [exact_right(split(cross[h]), v_ref[:, cut[h // 2]]) for h in heads]
+    akv = [pltpu.roll(jnp.where(low, akv[2 * p], akv[2 * p + 1]), CH, 1) for p in pairs]
+    right = []
+    for p in pairs:
+        right += [split(jnp.where(low, alpha[p], akv[p])), split(jnp.where(low, akv[p], alpha[p]))]
+    solver = inverse(inner)
+    solved = [square(solver[h], right[h]) for h in heads]
+    w = [jnp.where(low, solved[2 * p], solved[2 * p + 1]) for p in pairs]
+    u = [pltpu.roll(jnp.where(low, solved[2 * p + 1], solved[2 * p]), CH, 1) for p in pairs]
     stores = []
-    pairs = range(GROUP)
-    heads = range(2 * GROUP)
-    for g in range(groups):
-        for copy in loads[g]:
-            copy.wait()
-        cut = [slice(g * block + p * PAIR, g * block + (p + 1) * PAIR) for p in pairs]
-        cumul = [decays(log_ref[:, c], tril) for c in cut]
-        unit = [units(raw_ref[:, c], ones) for c in cut]
-        alpha = [-unit[p] * jnp.exp(cumul[p] - log_ref[:, cut[p]].astype(F32)) for p in pairs]
-        fall = [jnp.exp(-cumul[p]) for p in pairs]
-        beta = [rate_ref[:, cut[p]].astype(F32) * unit[p] * fall[p] for p in pairs]
-        key = [k_ref[:, cut[p]].astype(F32) * fall[p] for p in pairs]
-        gram = [grams(alpha[p], rows(beta[p], key[p]), low) for p in pairs]
-
-        inner, cross = [], []
-        for h in heads:
-            part = gram[h // 2][(h % 2) * n : (h % 2 + 1) * n]
-            inner.append(jnp.where(strict, part[:, :n], 0.0))
-            cross.append(jnp.where(strict, part[:, n:], 0.0))
-        akv = [exact_right(split(cross[h]), v_ref[:, cut[h // 2]]) for h in heads]
-        akv = [jnp.where(low, akv[2 * p], akv[2 * p + 1]) for p in pairs]
-        right = [split(lanes(alpha[p], akv[p])) for p in pairs]
-        solver = inverse(inner)
-        solved = [wide(solver[h], right[h // 2]) for h in heads]
-        for p in pairs:
-            first, second = solved[2 * p], solved[2 * p + 1]
-            w = jnp.where(low, first[:, :PAIR], second[:, :PAIR])
-            u = jnp.where(low, first[:, PAIR:], second[:, PAIR:])
-            w_all[:, cut[p]] = w
-            u_all[:, cut[p]] = u
-            scale = jnp.exp(cumul[p][n - 1 :, :])
-            end_b = beta[p] * scale
-            end_k = key[p] * scale
-            moved = square(split(end_b.T), split(w))
-            diagonal = jnp.where(row == lane % CH, scale, 0.0)
-            pieces[0, g * GROUP + p] = jnp.where(low_half(CH), moved[:CH], moved[CH:]) + diagonal
-            content = v_ref[:, cut[p]].astype(F32).T.astype(BF16)
-            by_key = mxu(content, lanes(*split(end_k)))
-            fresh = square(split(u.T), split(end_b)) + by_key[:, :PAIR] + by_key[:, PAIR:]
-            pieces[1, g * GROUP + p] = jnp.where(low_half(CH), fresh[:CH], fresh[CH:])
-
-        here = pl.ds(g * block, block)
-        ready = pl.ds(g * GROUP, GROUP)
-        stores += [
-            pltpu.make_async_copy(pieces.at[:, ready], pieces_out.at[:, ready], out_sems.at[g, 0]),
-            pltpu.make_async_copy(w_all.at[:, here], w_out.at[:, here], out_sems.at[g, 1]),
-            pltpu.make_async_copy(u_all.at[:, here], u_out.at[:, here], out_sems.at[g, 2]),
-        ]
-        for copy in stores[-3:]:
-            copy.start()
+
+    def store(slot, src, dst):
+        stores.append(pltpu.make_async_copy(src, dst, out_sems.at[slot]))
+        stores[-1].start()
+
+    for p in pairs:
+        w_all[:, cut[p]] = w[p]
+        u_all[:, cut[p]] = u[p]
+        here = pl.ds(p * PAIR, PAIR)
+        store(4 * p, w_all.at[:, here], w_out.at[:, here])
+        store(4 * p + 1, u_all.at[:, here], u_out.at[:, here])
+    scale = [jnp.exp(x[n - 1 :, :]) for x in cumul]
+    end_b = [x * y for x, y in zip(beta, scale)]
+    moved = [square(split(x.T), split(y)) for x, y in zip(end_b, w)]
+    for p in pairs:
+        diagonal = jnp.where(row == lane % CH, scale[p], 0.0)
+        pieces[0, p] = jnp.where(low_half(CH), moved[p][:CH], moved[p][CH:]) + diagonal
+        store(4 * p + 2, pieces.at[0, p], pieces_out.at[0, p])
+    by_key = [
+        mxu(v_ref[:, c].astype(F32).T.astype(BF16), lanes(*split(x * y))) for c, x, y in zip(cut, key, scale)
+    ]
+    fresh = [square(split(x.T), split(y)) for x, y in zip(u, end_b)]
+    for p in pairs:
+        end = fresh[p] + by_key[p][:, :PAIR] + by_key[p][:, PAIR:]
+        pieces[1, p] = jnp.where(low_half(CH), end[:CH], end[CH:])
+        store(4 * p + 3, pieces.at[1, p], pieces_out.at[1, p])
     for copy in stores:
         copy.wait()
 
@@ -230,13 +229,15 @@
     late = late_ref[...] > 0.5
     low = low_half(CH)
     short = (columns + 15) // 16 * 8
-    for p in range(PAIRS):
-        mine, other = mine_ref[0, p], other_ref[0, p]
-        first, second = jnp.where(late, other, mine), jnp.where(late, mine, other)
-        moves[p] = square(split(second), split(diagonal_blocks(first)))
-        mine, other = mine_ref[1, p], other_ref[1, p]
-        first, end = jnp.where(late, other, mine), jnp.where(late, mine, other)
-        end = end + square_nt(split(first), split(diagonal_blocks(second)))
+    pairs = range(PAIRS)
+    first = [jnp.where(late, other_ref[0, p], mine_ref[0, p]) for p in pairs]
+    second = [jnp.where(late, mine_ref[0, p], other_ref[0, p]) for p in pairs]
+    moved = [square(split(y), split(diagonal_blocks(x))) for x, y in zip(first, second)]
+    first = [jnp.where(late, other_ref[1, p], mine_ref[1, p]) for p in pairs]
+    carried = [square_nt(split(x), split(diagonal_blocks(y))) for x, y in zip(first, second)]
+    for p in pairs:
+        moves[p] = moved[p]
+        end = carried[p] + jnp.where(late, mine_ref[1, p], other_ref[1, p])
         turned = pltpu.roll(end, CH, 1)
         ends[p * PAIR : p * PAIR + CH, :] = jnp.where(low, end, turned)
         ends[p * PAIR + CH : (p + 1) * PAIR, :] = jnp.where(low, turned, end)
@@ -328,40 +329,48 @@
     count, short = slots_ref.shape[0], starts.shape[1]
     low = low_half(short)
     mask = mask_ref[...]
-    state = entry_ref[...]
-    chunk = count // sems.shape[0]
-    stores = []
-    for d in range(count):
-        starts[2 * d] = starts[2 * d + 1] = jnp.where(low, state[:short], state[short:])
-        if d % chunk == chunk - 1:
-            part = pl.ds(2 * (d + 1 - chunk), 2 * chunk)
-            stores.append(pltpu.make_async_copy(starts.at[part], starts_out.at[part], sems.at[d // chunk]))
-            stores[-1].start()
-        hi, lo = split(slots_ref[d, :CH, :])
-        weights = rows(lanes(hi, hi), lanes(hi, hi), lanes(lo, lo), lanes(lo, lo))
+
+    def weights(move):
+        hi, lo = move
+        return rows(lanes(hi, hi), lanes(hi, hi), lanes(lo, lo), lanes(lo, lo))
+
+    def advance(state, move, fresh):
+        out = mxu(lanes(*split(state * mask)), move, NT)
+        return out[:, :PAIR] + out[:, PAIR:] + fresh
+
+    def unpacked(d):
         end = slots_ref[d, CH:, :]
         turned = pltpu.roll(end, CH, 1)
-        fresh = rows(jnp.where(low, end, turned), jnp.where(low, turned, end))
-        out = mxu(lanes(*split(state * mask)), weights, NT)
-        state = out[:, :PAIR] + out[:, PAIR:] + fresh
-    exit_ref[...] = state
+        return rows(jnp.where(low, end, turned), jnp.where(low, turned, end))
+
+    parts = [split(slots_ref[d, :CH, :]) for d in range(count)]
+    moves = [weights(x) for x in parts]
+    fresh = [unpacked(d) for d in range(count)]
+    both = [
+        weights(split(square(parts[d + 1], split(diagonal_blocks(slots_ref[d, :CH, :])))))
+        for d in range(0, count, 2)
+    ]
+    joint = [advance(fresh[d], moves[d + 1], fresh[d + 1]) for d in range(0, count, 2)]
+    states = [entry_ref[...]]
+    for d in range(count // 2):
+        states.append(advance(states[d], both[d], joint[d]))
+    stores = []
+    for d in range(count // 2):
+        middle = advance(states[d], moves[2 * d], fresh[2 * d])
+        for i, x in enumerate((states[d], middle)):
+            at = 4 * d + 2 * i
+            starts[at] = starts[at + 1] = jnp.where(low, x[:short], x[short:])
+        part = pl.ds(4 * d, 4)
+        stores.append(pltpu.make_async_copy(starts.at[part], starts_out.at[part], sems.at[d]))
+        stores[-1].start()
+    exit_ref[...] = states[-1]
     for copy in stores:
         copy.wait()
 
 
-def final_kernel(starts_ref, read_in, local_in, base_in, gain_ref, out, *scratch, columns):
-    buffers, (begins, result, in_sems, out_sems) = scratch[:3], scratch[3:]
-    read_ref, local_ref, base_ref = buffers
+def final_kernel(starts_ref, read_ref, local_ref, base_ref, gain_ref, out, begins, result, out_sems, *, columns):
     cut = [slice(p * PAIR, (p + 1) * PAIR) for p in range(PAIRS)]
     place = [pl.ds(p * PAIR, PAIR) for p in range(PAIRS)]
-    block = GROUP * PAIR
-    loads = []
-    for g in range(WIDTH // block):
-        here = pl.ds(g * block, block)
-        for i, (src, dst) in enumerate(zip((read_in, local_in, base_in), buffers)):
-            loads.append(pltpu.make_async_copy(src.at[:, here], dst.at[:, here], in_sems.at[g, i]))
-    for copy in loads:
-        copy.start()
     short = starts_ref.shape[1]
     low = low_half(short)
     for owner in range(starts_ref.shape[0]):
@@ -375,8 +384,6 @@
     right = [split(jnp.where(own, begins[c, :], 0.0)) for c in cut]
     stores = []
     for g in range(PAIRS // GROUP):
-        for copy in loads[3 * g : 3 * g + 3]:
-            copy.wait()
         pairs = range(g * GROUP, (g + 1) * GROUP)
         left = [split(read_ref[:, cut[p]]) for p in pairs]
         carried = [
@@ -407,8 +414,10 @@
     short = (columns + 15) // 16 * 8
     groups = PAIRS // GROUP
     hbm = pl.BlockSpec(memory_space=pltpu.HBM)
+    held = functools.partial(pltpu.with_memory_space_constraint, memory_space=pltpu.HBM)
     vmem = pl.BlockSpec(memory_space=pltpu.VMEM)
-    plane = jax.ShapeDtypeStruct((n, WIDTH), F32)
+    plane = pltpu.HBM((n, WIDTH), F32)
+    arrays = [held(x) for x in (q, k, v, raw, rates, logs)]
     tokens = pltpu.VMEM((n, WIDTH), BF16)
     floats = pltpu.VMEM((n, WIDTH), F32)
     sems = pltpu.SemaphoreType.DMA
@@ -420,8 +429,8 @@
         out_specs=[hbm] * 3,
         out_shape=[jax.ShapeDtypeStruct(pieces, F32), plane, plane],
         scratch_shapes=[tokens] * 5
-        + [pltpu.VMEM(pieces, F32), floats, floats, sems((groups, 5)), sems((groups, 3))],
-    )(k, v, raw, rates, logs)
+        + [pltpu.VMEM(pieces, F32), floats, floats, sems((5,)), sems((4 * PAIRS,))],
+    )(*arrays[1:])
     other = lax.ppermute(mine, "ctx", [(i, i ^ 1) for i in range(owners)])
     place = lax.axis_index("ctx")
     late = jnp.broadcast_to((place % 2).astype(F32), (1, PAIR))
@@ -437,9 +446,9 @@
         read_kernel,
         in_specs=[hbm] * 8 + [vmem] * 4,
         out_specs=[hbm] * 3,
-        out_shape=[plane] * 3,
+        out_shape=[jax.ShapeDtypeStruct((n, WIDTH), F32)] * 3,
         scratch_shapes=[tokens] * 6 + [floats] * 5 + [sems((groups, 8)), sems((groups, 3))],
-    )(q, k, v, raw, rates, logs, w, u, boost.reshape(1, WIDTH), shift.reshape(1, WIDTH), other, late)
+    )(*arrays, held(w), held(u), boost.reshape(1, WIDTH), shift.reshape(1, WIDTH), other, late)
 
     own = lax.broadcasted_iota(jnp.int32, (2 * short, PAIR), 0)
     half = lax.broadcasted_iota(jnp.int32, (2 * short, PAIR), 1) // CH
@@ -450,21 +459,20 @@
         in_specs=[vmem, vmem, vmem, hbm],
         out_specs=[hbm, vmem],
         out_shape=[
-            jax.ShapeDtypeStruct((owners, short, PAIR), F32),
+            pltpu.HBM((owners, short, PAIR), F32),
             jax.ShapeDtypeStruct((2 * short, PAIR), F32),
         ],
-        scratch_shapes=[pltpu.VMEM((owners, short, PAIR), F32), sems((4,))],
+        scratch_shapes=[pltpu.VMEM((owners, short, PAIR), F32), sems((owners // 4,))],
     )(slots, jnp.concatenate([entry, entry], axis=1), mask.astype(F32), base)
     starts = lax.all_to_all(starts, "ctx", 0, 0)
     exit_state = final[:columns, :CH].T
 
     out = call(
         functools.partial(final_kernel, columns=columns),
-        in_specs=[vmem, hbm, hbm, hbm, vmem],
+        in_specs=[vmem] * 5,
         out_specs=hbm,
-        out_shape=jax.ShapeDtypeStruct((n, WIDTH), BF16),
-        scratch_shapes=[floats] * 3
-        + [pltpu.VMEM((WIDTH, PAIR), F32), tokens, sems((groups, 3)), sems((PAIRS,))],
+        out_shape=pltpu.HBM((n, WIDTH), BF16),
+        scratch_shapes=[pltpu.VMEM((WIDTH, PAIR), F32), tokens, sems((PAIRS,))],
     )(starts, read, local, base, gain.reshape(1, WIDTH))
     return out, exit_state
 

time: 67.1 us -> 60.6 us (0.903)
  local copies, waits for them, and re-layouts: 13.7 us -> 1.31 us
  waiting for transfers between devices: 12.5 us -> 17.3 us
  Pallas kernels: 19.9 us -> 22.7 us
  starting transfers between devices: 19 us -> 17.8 us
    unnamed x46 -> x8, local copies, waits for them, and re-layouts: 13.1 us -> 0.68 us
    all_to_all x1, waiting for transfers between devices: 1.23 us -> 5.92 us  [shards(): slots = lax.all_to_all(slots, 'ctx', 0, 0, axis_index_groups=same_core)]
    pallas_call x1, Pallas kernels: 8.48 us -> 10.6 us  [shards(): call(local_kernel, in_specs=[hbm] * 5, out_specs=[hbm] * 3, out_shape=[ja...]
    all_to_all x1, starting transfers between devices: 6.31 us -> 5.05 us  [shards(): starts = lax.all_to_all(starts, 'ctx', 0, 0)]
    pallas_call x1, Pallas kernels: 4.82 us -> 5.99 us  [shards(): call(read_kernel, in_specs=[hbm] * 8 + [vmem] * 4, out_specs=[hbm] * 3, o...]
  transfers between devices with their start and end apart: 3 -> 3, of which waited for: 3 -> 3; matrix products, arithmetic and copies ran while one was open for 1% -> 1% of each run, Pallas kernels for 7% -> 10%
where the time goes in v4:
time: 60.6 us; the launch traced here: 60.2 us
  Pallas kernels  22.7 us (37%)
  starting transfers between devices  17.8 us (29%)
  waiting for transfers between devices  17.3 us (29%)
  local copies, waits for them, and re-layouts  1.31 us (2%)
  between operations  0.94 us (2%)
    pallas_call x1, Pallas kernels, shards(): call(local_kernel, in_specs=[hbm] * 5, out_specs=[hbm] * 3, out_shape=[ja...  10.6 us
    all_to_all x1, waiting for transfers between devices, shards(): starts = lax.all_to_all(starts, 'ctx', 0, 0)  9.65 us
    ppermute x1, starting transfers between devices, shards(): other = lax.ppermute(mine, 'ctx', [(i, i ^ 1) for i in range(owners)])  8.81 us
    pallas_call x1, Pallas kernels, shards(): call(read_kernel, in_specs=[hbm] * 8 + [vmem] * 4, out_specs=[hbm] * 3, o...  5.99 us
    all_to_all x1, waiting for transfers between devices, shards(): slots = lax.all_to_all(slots, 'ctx', 0, 0, axis_index_groups=same_core)  5.92 us
    all_to_all x1, starting transfers between devices, shards(): starts = lax.all_to_all(starts, 'ctx', 0, 0)  5.05 us
    all_to_all x1, starting transfers between devices, shards(): slots = lax.all_to_all(slots, 'ctx', 0, 0, axis_index_groups=same_core)  3.91 us
    pallas_call x1, Pallas kernels, shards(): call(scan_kernel, in_specs=[vmem, vmem, vmem, hbm], out_specs=[hbm, vmem]...  2.53 us
  transfers between devices with their start and end apart: 3, of which 3 were waited for; matrix products, arithmetic and copies ran while one was open for 1% of the time, Pallas kernels for 10%

profile of v4, /device:TPU:1, one launch (start us, length us, event | category | flops | bytes accessed | tf_op | source)
XLA Modules:
  0.0 60.2 jit_solution(2679768179264835975)
XLA Ops:
  0.6 10.6 %shard_map.113 = (f32[2,10,64,128]{3,2,1,0:T(8,128)S(1)}, f32[128,1280]{1,0:T(8,128)}, f32[128,1280]{1,0:T(8,128)}) custom-call(bf16[128,1280]{1,0:T(8,128)(2,1)} %refs_1_.3, bf16[128,1280]{1,0:T(8,128)(2,1)} %refs_2_.3, bf16[128,1280]{1,0:T(8,128)(2,1)} %refs_3_.3, bf16[128,1280]{1,0:T(8,128)(2,1)} %refs_4_.3, bf16[128,1280]{1,0:T(8,128)(2,1)} %refs_5_.1), custom_call_target="tpu_custom_call" | custom-call | tf_op jit(solution)/shard_map/pallas_call | solution.py:426
  11.2 8.8 %collective-permute-start = (f32[2,10,64,128]{3,2,1,0:T(8,128)S(1)}, f32[2,10,64,128]{3,2,1,0:T(8,128)S(1)}, u32[]{:S(2)}, u32[]{:S(2)}) collective-permute-start(f32[2,10,64,128]{3,2,1,0:T(8,128)S(1)} %get-tuple-element.10.mine_ref), channel_id=1, source_target_pairs={{0,1},{1,0},{2,3},{3,2},{4,5},{5,4},{6,7},{7,6},{8,9},{9,8},{10,11... | collective-permute-start | bytes 1966088 | tf_op jit(solution)/shard_map/ppermute | solution.py:434
  20.0 1.7 %collective-permute-done.other_ref.refs_10_ = f32[2,10,64,128]{3,2,1,0:T(8,128)S(1)} collective-permute-done((f32[2,10,64,128]{3,2,1,0:T(8,128)S(1)}, f32[2,10,64,128]{3,2,1,0:T(8,128)S(1)}, u32[]{:S(2)}, u32[]{:S(2)}) %collective-permute-start) | collective-permute-done | bytes 655392 | tf_op jit(solution)/shard_map/ppermute | solution.py:434
  21.7 1.7 %shard_map.114 = f32[16,88,128]{2,1,0:T(8,128)} custom-call(f32[2,10,64,128]{3,2,1,0:T(8,128)S(1)} %get-tuple-element.10.mine_ref, f32[2,10,64,128]{3,2,1,0:T(8,128)S(1)} %collective-permute-done.other_ref.refs_10_, f32[1,128]{1,0:T(1,128)S(1)} %broadcast_in_dim.3.late_ref.refs_11_), custom_call_target="tpu_custom_call" | custom-call | tf_op jit(solution)/shard_map/pallas_call | solution.py:437
  23.5 0.0 copy-start.1
  23.5 0.0 copy-start.2
  23.5 3.9 %all-to-all-start = ((f32[16,88,128]{2,1,0:T(8,128)}), f32[16,88,128]{2,1,0:T(8,128)S(1)}, u32[]{:S(2)}, u32[]{:S(2)}) async-start(f32[16,88,128]{2,1,0:T(8,128)} %shard_map.114), calls=%async_computation | async-start | bytes 1441792 | tf_op jit(solution)/shard_map/all_to_all | solution.py:443
  27.4 0.0 copy-start
  27.4 0.0 copy-done.1
  27.4 0.0 copy-done.2
  27.5 0.7 %copy-done = f32[64,40]{0,1:T(8,128)S(1)} copy-done((f32[64,40]{0,1:T(8,128)S(1)}, f32[64,40]{0,1:T(8,128)}, u32[]{:S(2)}) %copy-start) | copy-done | bytes 10264
  28.2 0.1 pad_maximum_fusion.entry_ref
  28.2 0.1 fusion.3.mask_ref
  28.3 6.0 %shard_map.115 = (f32[128,1280]{1,0:T(8,128)S(1)}, f32[128,1280]{1,0:T(8,128)S(1)}, f32[128,1280]{1,0:T(8,128)S(1)}) custom-call(bf16[128,1280]{1,0:T(8,128)(2,1)} %refs_0_.3, bf16[128,1280]{1,0:T(8,128)(2,1)} %refs_1_.3, bf16[128,1280]{1,0:T(8,128)(2,1)} %refs_2_.3, bf16[128,1280]{1,0:T(8,128)(2,1)} %refs_3_.3, bf16[128,1280]{1,0:T(8,128)(2,1)} %refs_4_.3, ...), custom_call_target="tpu_custom_call" | custom-call | tf_op jit(solution)/shard_map/pallas_call | solution.py:445
  34.3 5.9 %all-to-all-done.slots_ref = f32[16,88,128]{2,1,0:T(8,128)S(1)} async-done(((f32[16,88,128]{2,1,0:T(8,128)}), f32[16,88,128]{2,1,0:T(8,128)S(1)}, u32[]{:S(2)}, u32[]{:S(2)}) %all-to-all-start) | async-done | bytes 720928 | tf_op jit(solution)/shard_map/all_to_all | solution.py:443
  40.3 2.5 %shard_map.116 = (f32[32,24,128]{2,1,0:T(8,128)}, f32[48,128]{1,0:T(8,128)S(1)}) custom-call(f32[16,88,128]{2,1,0:T(8,128)S(1)} %all-to-all-done.slots_ref, f32[48,128]{1,0:T(8,128)S(1)} %pad_maximum_fusion.entry_ref, f32[48,128]{1,0:T(8,128)S(1)} %fusion.3.mask_ref, f32[128,1280]{1,0:T(8,128)S(1)} %get-tuple-element.13.after_ref.base_ref), custom_call_target="tpu_custom_call" | custom-call | tf_op jit(solution)/shard_map/pallas_call | solution.py:457
  42.8 0.0 copy-start.3
  42.8 5.0 %all-to-all-start.1 = ((f32[32,24,128]{2,1,0:T(8,128)}), f32[32,24,128]{2,1,0:T(8,128)S(1)}, u32[]{:S(2)}, u32[]{:S(2)}) async-start(f32[32,24,128]{2,1,0:T(8,128)} %get-tuple-element.14), calls=%async_computation.1 | async-start | bytes 786432 | tf_op jit(solution)/shard_map/all_to_all | solution.py:467
  47.9 0.0 copy-done.3
  47.9 0.6 %slice_bitcast_fusion = f32[64,40]{0,1:T(8,128)} fusion(f32[48,128]{1,0:T(8,128)S(1)} %get-tuple-element.17), kind=kLoop, calls=%fused_computation.10 | loop fusion | bytes 20480 | tf_op jit(solution)/shard_map/transpose | solution.py:468
  48.5 9.7 %all-to-all-done.1.starts_ref = f32[32,24,128]{2,1,0:T(8,128)S(1)} async-done(((f32[32,24,128]{2,1,0:T(8,128)}), f32[32,24,128]{2,1,0:T(8,128)S(1)}, u32[]{:S(2)}, u32[]{:S(2)}) %all-to-all-start.1) | async-done | bytes 393248 | tf_op jit(solution)/shard_map/all_to_all | solution.py:467
  58.1 1.9 %shard_map.117 = bf16[128,1280]{1,0:T(8,128)(2,1)} custom-call(f32[32,24,128]{2,1,0:T(8,128)S(1)} %all-to-all-done.1.starts_ref, f32[128,1280]{1,0:T(8,128)S(1)} %get-tuple-element.15.read_ref, f32[128,1280]{1,0:T(8,128)S(1)} %get-tuple-element.16.local_ref, f32[128,1280]{1,0:T(8,128)S(1)} %get-tuple-element.13.after_ref.base_ref, ...), custom_call_target="tpu_custom_call" | custom-call | tf_op jit(solution)/shard_map/pallas_call | solution.py:470
  (9 shorter events, 0.1 us)
Async XLA Ops:
  11.2 10.5 %collective-permute-start = (f32[2,10,64,128]{3,2,1,0:T(8,128)S(1)}, f32[2,10,64,128]{3,2,1,0:T(8,128)S(1)}, u32[]{:S(2)}, u32[]{:S(2)}) collective-permute-start(f32[2,10,64,128]{3,2,1,0:T(8,128)S(1)} %get-tuple-element.10.mine_ref), channel_id=1, source_target_pairs={{0,1},{1,0},{2,3},{3,2},{4,5},{5,4},{6,7},{7,6},{8,9},{9,8},{10,11... | collective-permute-start | bytes 1966088 | tf_op jit(solution)/shard_map/ppermute | solution.py:434
  23.5 4.0 %copy-start.1 = (f32[1280]{0:T(1024)S(1)}, f32[1280]{0:T(1024)}, u32[]{:S(2)}) copy-start(f32[1280]{0:T(1024)} %param.17) | copy-start | bytes 15364
  23.5 4.0 %copy-start.2 = (f32[1280]{0:T(1024)S(1)}, f32[1280]{0:T(1024)}, u32[]{:S(2)}) copy-start(f32[1280]{0:T(1024)} %param.19) | copy-start | bytes 15364
  23.5 16.8 %all-to-all-start = ((f32[16,88,128]{2,1,0:T(8,128)}), f32[16,88,128]{2,1,0:T(8,128)S(1)}, u32[]{:S(2)}, u32[]{:S(2)}) async-start(f32[16,88,128]{2,1,0:T(8,128)} %shard_map.114), calls=%async_computation | async-start | bytes 1441792 | tf_op jit(solution)/shard_map/all_to_all | solution.py:443
  27.4 0.7 %copy-start = (f32[64,40]{0,1:T(8,128)S(1)}, f32[64,40]{0,1:T(8,128)}, u32[]{:S(2)}) copy-start(f32[64,40]{0,1:T(8,128)} %param.16) | copy-start | bytes 30724
  42.8 5.1 %copy-start.3 = (f32[1280]{0:T(1024)S(1)}, f32[1280]{0:T(1024)}, u32[]{:S(2)}) copy-start(f32[1280]{0:T(1024)} %param.18) | copy-start | bytes 15364
  42.8 15.3 %all-to-all-start.1 = ((f32[32,24,128]{2,1,0:T(8,128)}), f32[32,24,128]{2,1,0:T(8,128)S(1)}, u32[]{:S(2)}, u32[]{:S(2)}) async-start(f32[32,24,128]{2,1,0:T(8,128)} %get-tuple-element.14), calls=%async_computation.1 | async-start | bytes 786432 | tf_op jit(solution)/shard_map/all_to_all | solution.py:467

commit v5 on v4

--- a/solution.py
+++ b/solution.py
@@ -82,18 +82,40 @@
 
 
 def grams(left, right, low):
-    zero = jnp.zeros_like(left)
-    stacked = split(rows(jnp.where(low, left, zero), jnp.where(low, zero, left)))
+    first = jnp.where(low, 1.0, 0.0).astype(BF16)
+    second = jnp.where(low, 0.0, 1.0).astype(BF16)
+    hi, lo = (rows(x * first, x * second) for x in split(left))
     b = split(right)
-    return mxu(lanes(*stacked), lanes(b[0], b[0]), NT) + mxu(stacked[0], b[1], NT)
+    return mxu(lanes(hi, lo), lanes(b[0], b[0]), NT) + mxu(hi, b[1], NT)
+
+
+def small_inverse(small):
+    slab, n = small[0].shape
+    parts = lanes(*split(rows(*small)))
+    source, target = iota((n, n), 0), iota((n, n), 1)
+
+    def pick(s):
+        return jnp.where(source == target // slab * slab + s, 1.0, 0.0).astype(BF16)
+
+    columns = []
+    for s in range(0, slab, 2):
+        both = lanes(pick(s), pick(s + 1))
+        out = mxu(parts, rows(both, both))
+        columns += [out[:, :n], out[:, n:]]
+    unit = jnp.where(iota((slab, n), 0) == iota((slab, n), 1) % slab, 1.0, 0.0)
+    solver = [unit] * len(small)
+    for s in range(slab - 1):
+        solver = [
+            x + columns[s][h * slab : (h + 1) * slab] * x[s : s + 1, :] for h, x in enumerate(solver)
+        ]
+    return solver
 
 
 def inverse(inner):
     n = inner[0].shape[0]
     slab = 16
     count = n // slab
-    row, lane = iota((slab, n), 0), iota((slab, n), 1)
-    apart = row ^ (lane % slab)
+    lane = iota((slab, n), 1)
     same = jnp.where(iota((n, n), 0) // slab == iota((n, n), 1) // slab, 1.0, 0.0)
     same_short = same.astype(BF16)
 
@@ -101,14 +123,8 @@
         return tuple(rows(*[x] * count) * same_short for x in pair)
 
     small = [sum(jnp.where(lane // slab == i, x[i * slab : (i + 1) * slab], 0.0) for i in range(count)) for x in inner]
-    solver = [jnp.where(apart == 0, 1.0, 0.0) + jnp.where(apart == 1, x, 0.0) for x in small]
-    size = 2
-    while size < slab:
-        joins = (apart >= size) & (apart < 2 * size)
-        halves = [split(x) for x in solver]
-        mid = [square(split(jnp.where(joins, x, 0.0)), spread(t)) for x, t in zip(small, halves)]
-        solver = [x + square(t, spread(split(m))) for x, t, m in zip(solver, halves, mid)]
-        size *= 2
+    solver = small_inverse(small)
+    size = slab
     halves = [spread(split(x)) for x in solver]
     solver = [rows(*[x] * count) * same for x in solver]
 
@@ -144,73 +160,85 @@
     pieces, w_all, u_all, in_sems, out_sems = refs[13:]
     n, width = w_all.shape
     order = (4, 3, 2, 0, 1)
-    loads = [pltpu.make_async_copy(inputs[i], buffers[i], in_sems.at[i]) for i in range(5)]
-    for i in order:
-        loads[i].start()
+    block = GROUP * PAIR
+    groups = width // block
+    loads = []
+    for g in range(groups):
+        here = pl.ds(g * block, block)
+        loads.append(
+            [
+                pltpu.make_async_copy(inputs[i].at[:, here], buffers[i].at[:, here], in_sems.at[g, i])
+                for i in range(5)
+            ]
+        )
+        for i in order:
+            loads[g][i].start()
     k_ref, v_ref, raw_ref, rate_ref, log_ref = buffers
-    pairs = range(width // PAIR)
-    heads = range(2 * len(pairs))
-    cut = [slice(p * PAIR, (p + 1) * PAIR) for p in pairs]
+    pairs = range(GROUP)
+    heads = range(2 * GROUP)
     low = low_half(n)
     ones = block_ones()
     tril = tril_ones(n)
     strict = iota((n, n), 0) > iota((n, n), 1)
     row, lane = iota((CH, PAIR), 0), iota((CH, PAIR), 1)
 
-    loads[4].wait()
-    cumul = [decays(log_ref[:, c], tril) for c in cut]
-    fall = [jnp.exp(-x) for x in cumul]
-    rise = [jnp.exp(x - log_ref[:, c].astype(F32)) for x, c in zip(cumul, cut)]
-    loads[2].wait()
-    unit = [units(raw_ref[:, c], ones) for c in cut]
-    alpha = [-x * y for x, y in zip(unit, rise)]
-    loads[3].wait()
-    beta = [rate_ref[:, c].astype(F32) * x * y for c, x, y in zip(cut, unit, fall)]
-    loads[0].wait()
-    key = [k_ref[:, c].astype(F32) * x for c, x in zip(cut, fall)]
-    gram = [grams(alpha[p], rows(beta[p], key[p]), low) for p in pairs]
-    inner, cross = [], []
-    for h in heads:
-        part = gram[h // 2][(h % 2) * n : (h % 2 + 1) * n]
-        inner.append(jnp.where(strict, part[:, :n], 0.0))
-        cross.append(jnp.where(strict, part[:, n:], 0.0))
-    loads[1].wait()
-    akv = [exact_right(split(cross[h]), v_ref[:, cut[h // 2]]) for h in heads]
-    akv = [pltpu.roll(jnp.where(low, akv[2 * p], akv[2 * p + 1]), CH, 1) for p in pairs]
-    right = []
-    for p in pairs:
-        right += [split(jnp.where(low, alpha[p], akv[p])), split(jnp.where(low, akv[p], alpha[p]))]
-    solver = inverse(inner)
-    solved = [square(solver[h], right[h]) for h in heads]
-    w = [jnp.where(low, solved[2 * p], solved[2 * p + 1]) for p in pairs]
-    u = [pltpu.roll(jnp.where(low, solved[2 * p + 1], solved[2 * p]), CH, 1) for p in pairs]
     stores = []
 
     def store(slot, src, dst):
         stores.append(pltpu.make_async_copy(src, dst, out_sems.at[slot]))
         stores[-1].start()
 
-    for p in pairs:
-        w_all[:, cut[p]] = w[p]
-        u_all[:, cut[p]] = u[p]
-        here = pl.ds(p * PAIR, PAIR)
-        store(4 * p, w_all.at[:, here], w_out.at[:, here])
-        store(4 * p + 1, u_all.at[:, here], u_out.at[:, here])
-    scale = [jnp.exp(x[n - 1 :, :]) for x in cumul]
-    end_b = [x * y for x, y in zip(beta, scale)]
-    moved = [square(split(x.T), split(y)) for x, y in zip(end_b, w)]
-    for p in pairs:
-        diagonal = jnp.where(row == lane % CH, scale[p], 0.0)
-        pieces[0, p] = jnp.where(low_half(CH), moved[p][:CH], moved[p][CH:]) + diagonal
-        store(4 * p + 2, pieces.at[0, p], pieces_out.at[0, p])
-    by_key = [
-        mxu(v_ref[:, c].astype(F32).T.astype(BF16), lanes(*split(x * y))) for c, x, y in zip(cut, key, scale)
-    ]
-    fresh = [square(split(x.T), split(y)) for x, y in zip(u, end_b)]
-    for p in pairs:
-        end = fresh[p] + by_key[p][:, :PAIR] + by_key[p][:, PAIR:]
-        pieces[1, p] = jnp.where(low_half(CH), end[:CH], end[CH:])
-        store(4 * p + 3, pieces.at[1, p], pieces_out.at[1, p])
+    for g in range(groups):
+        first = g * GROUP
+        cut = [slice((first + p) * PAIR, (first + p + 1) * PAIR) for p in pairs]
+        loads[g][4].wait()
+        cumul = [decays(log_ref[:, c], tril) for c in cut]
+        fall = [jnp.exp(-x) for x in cumul]
+        rise = [jnp.exp(x - log_ref[:, c].astype(F32)) for x, c in zip(cumul, cut)]
+        loads[g][2].wait()
+        unit = [units(raw_ref[:, c], ones) for c in cut]
+        alpha = [-x * y for x, y in zip(unit, rise)]
+        loads[g][3].wait()
+        beta = [rate_ref[:, c].astype(F32) * x * y for c, x, y in zip(cut, unit, fall)]
+        loads[g][0].wait()
+        key = [k_ref[:, c].astype(F32) * x for c, x in zip(cut, fall)]
+        gram = [grams(alpha[p], rows(beta[p], key[p]), low) for p in pairs]
+        inner, cross = [], []
+        for h in heads:
+            part = gram[h // 2][(h % 2) * n : (h % 2 + 1) * n]
+            inner.append(jnp.where(strict, part[:, :n], 0.0))
+            cross.append(jnp.where(strict, part[:, n:], 0.0))
+        loads[g][1].wait()
+        akv = [exact_right(split(cross[h]), v_ref[:, cut[h // 2]]) for h in heads]
+        akv = [pltpu.roll(jnp.where(low, akv[2 * p], akv[2 * p + 1]), CH, 1) for p in pairs]
+        right = []
+        for p in pairs:
+            right += [split(jnp.where(low, alpha[p], akv[p])), split(jnp.where(low, akv[p], alpha[p]))]
+        solver = inverse(inner)
+        solved = [square(solver[h], right[h]) for h in heads]
+        w = [jnp.where(low, solved[2 * p], solved[2 * p + 1]) for p in pairs]
+        u = [pltpu.roll(jnp.where(low, solved[2 * p + 1], solved[2 * p]), CH, 1) for p in pairs]
+        for p in pairs:
+            w_all[:, cut[p]] = w[p]
+            u_all[:, cut[p]] = u[p]
+            here = pl.ds((first + p) * PAIR, PAIR)
+            store(4 * (first + p), w_all.at[:, here], w_out.at[:, here])
+            store(4 * (first + p) + 1, u_all.at[:, here], u_out.at[:, here])
+        scale = [jnp.exp(x[n - 1 :, :]) for x in cumul]
+        end_b = [x * y for x, y in zip(beta, scale)]
+        moved = [square(split(x.T), split(y)) for x, y in zip(end_b, w)]
+        for p in pairs:
+            diagonal = jnp.where(row == lane % CH, scale[p], 0.0)
+            pieces[0, first + p] = jnp.where(low_half(CH), moved[p][:CH], moved[p][CH:]) + diagonal
+            store(4 * (first + p) + 2, pieces.at[0, first + p], pieces_out.at[0, first + p])
+        by_key = [
+            mxu(v_ref[:, c].astype(F32).T.astype(BF16), lanes(*split(x * y))) for c, x, y in zip(cut, key, scale)
+        ]
+        fresh = [square(split(x.T), split(y)) for x, y in zip(u, end_b)]
+        for p in pairs:
+            end = fresh[p] + by_key[p][:, :PAIR] + by_key[p][:, PAIR:]
+            pieces[1, first + p] = jnp.where(low_half(CH), end[:CH], end[CH:])
+            store(4 * (first + p) + 3, pieces.at[1, first + p], pieces_out.at[1, first + p])
     for copy in stores:
         copy.wait()
 
@@ -330,24 +358,21 @@
     low = low_half(short)
     mask = mask_ref[...]
 
-    def weights(move):
-        hi, lo = move
-        return rows(lanes(hi, hi), lanes(hi, hi), lanes(lo, lo), lanes(lo, lo))
-
     def advance(state, move, fresh):
-        out = mxu(lanes(*split(state * mask)), move, NT)
-        return out[:, :PAIR] + out[:, PAIR:] + fresh
+        hi, lo = split(state * mask)
+        out = mxu(rows(hi, lo), rows(*move), NT)
+        out = out[: 2 * short] + out[2 * short :]
+        return out + pltpu.roll(out, CH, 1) + fresh
 
     def unpacked(d):
         end = slots_ref[d, CH:, :]
         turned = pltpu.roll(end, CH, 1)
         return rows(jnp.where(low, end, turned), jnp.where(low, turned, end))
 
-    parts = [split(slots_ref[d, :CH, :]) for d in range(count)]
-    moves = [weights(x) for x in parts]
+    moves = [split(slots_ref[d, :CH, :]) for d in range(count)]
     fresh = [unpacked(d) for d in range(count)]
     both = [
-        weights(split(square(parts[d + 1], split(diagonal_blocks(slots_ref[d, :CH, :])))))
+        split(square(moves[d + 1], split(diagonal_blocks(slots_ref[d, :CH, :]))))
         for d in range(0, count, 2)
     ]
     joint = [advance(fresh[d], moves[d + 1], fresh[d + 1]) for d in range(0, count, 2)]
@@ -429,7 +454,7 @@
         out_specs=[hbm] * 3,
         out_shape=[jax.ShapeDtypeStruct(pieces, F32), plane, plane],
         scratch_shapes=[tokens] * 5
-        + [pltpu.VMEM(pieces, F32), floats, floats, sems((5,)), sems((4 * PAIRS,))],
+        + [pltpu.VMEM(pieces, F32), floats, floats, sems((groups, 5)), sems((4 * PAIRS,))],
     )(*arrays[1:])
     other = lax.ppermute(mine, "ctx", [(i, i ^ 1) for i in range(owners)])
     place = lax.axis_index("ctx")

time: 60.6 us -> 60.5 us (level)
  no operation moved by 1% of the time
where the time goes in v5:
time: 60.5 us; the launch traced here: 60 us
  Pallas kernels  22.6 us (37%)
  starting transfers between devices  17.7 us (29%)
  waiting for transfers between devices  17.3 us (29%)
  local copies, waits for them, and re-layouts  1.31 us (2%)
  between operations  0.94 us (2%)
    pallas_call x1, Pallas kernels, shards(): call(local_kernel, in_specs=[hbm] * 5, out_specs=[hbm] * 3, out_shape=[ja...  10.3 us
    all_to_all x1, waiting for transfers between devices, shards(): starts = lax.all_to_all(starts, 'ctx', 0, 0)  9.65 us
    ppermute x1, starting transfers between devices, shards(): other = lax.ppermute(mine, 'ctx', [(i, i ^ 1) for i in range(owners)])  8.79 us
    pallas_call x1, Pallas kernels, shards(): call(read_kernel, in_specs=[hbm] * 8 + [vmem] * 4, out_specs=[hbm] * 3, o...  6 us
    all_to_all x1, waiting for transfers between devices, shards(): slots = lax.all_to_all(slots, 'ctx', 0, 0, axis_index_groups=same_core)  5.91 us
    all_to_all x1, starting transfers between devices, shards(): starts = lax.all_to_all(starts, 'ctx', 0, 0)  5.04 us
    all_to_all x1, starting transfers between devices, shards(): slots = lax.all_to_all(slots, 'ctx', 0, 0, axis_index_groups=same_core)  3.91 us
    pallas_call x1, Pallas kernels, shards(): call(scan_kernel, in_specs=[vmem, vmem, vmem, hbm], out_specs=[hbm, vmem]...  2.73 us
  transfers between devices with their start and end apart: 3, of which 3 were waited for; matrix products, arithmetic and copies ran while one was open for 1% of the time, Pallas kernels for 10%

profile of v5, /device:TPU:1, one launch (start us, length us, event | category | flops | bytes accessed | tf_op | source)
XLA Modules:
  0.0 60.0 jit_solution(16520064042336627088)
XLA Ops:
  0.6 10.3 %shard_map.113 = (f32[2,10,64,128]{3,2,1,0:T(8,128)S(1)}, f32[128,1280]{1,0:T(8,128)}, f32[128,1280]{1,0:T(8,128)}) custom-call(bf16[128,1280]{1,0:T(8,128)(2,1)} %refs_1_.3, bf16[128,1280]{1,0:T(8,128)(2,1)} %refs_2_.3, bf16[128,1280]{1,0:T(8,128)(2,1)} %refs_3_.3, bf16[128,1280]{1,0:T(8,128)(2,1)} %refs_4_.3, bf16[128,1280]{1,0:T(8,128)(2,1)} %refs_5_.1), custom_call_target="tpu_custom_call" | custom-call | tf_op jit(solution)/shard_map/pallas_call | solution.py:451
  10.9 8.8 %collective-permute-start = (f32[2,10,64,128]{3,2,1,0:T(8,128)S(1)}, f32[2,10,64,128]{3,2,1,0:T(8,128)S(1)}, u32[]{:S(2)}, u32[]{:S(2)}) collective-permute-start(f32[2,10,64,128]{3,2,1,0:T(8,128)S(1)} %get-tuple-element.10.mine_ref), channel_id=1, source_target_pairs={{0,1},{1,0},{2,3},{3,2},{4,5},{5,4},{6,7},{7,6},{8,9},{9,8},{10,11... | collective-permute-start | bytes 1966088 | tf_op jit(solution)/shard_map/ppermute | solution.py:459
  19.7 1.7 %collective-permute-done.other_ref.refs_10_ = f32[2,10,64,128]{3,2,1,0:T(8,128)S(1)} collective-permute-done((f32[2,10,64,128]{3,2,1,0:T(8,128)S(1)}, f32[2,10,64,128]{3,2,1,0:T(8,128)S(1)}, u32[]{:S(2)}, u32[]{:S(2)}) %collective-permute-start) | collective-permute-done | bytes 655392 | tf_op jit(solution)/shard_map/ppermute | solution.py:459
  21.4 1.7 %shard_map.114 = f32[16,88,128]{2,1,0:T(8,128)} custom-call(f32[2,10,64,128]{3,2,1,0:T(8,128)S(1)} %get-tuple-element.10.mine_ref, f32[2,10,64,128]{3,2,1,0:T(8,128)S(1)} %collective-permute-done.other_ref.refs_10_, f32[1,128]{1,0:T(1,128)S(1)} %broadcast_in_dim.3.late_ref.refs_11_), custom_call_target="tpu_custom_call" | custom-call | tf_op jit(solution)/shard_map/pallas_call | solution.py:462
  23.1 0.0 copy-start.1
  23.1 0.0 copy-start.2
  23.1 3.9 %all-to-all-start = ((f32[16,88,128]{2,1,0:T(8,128)}), f32[16,88,128]{2,1,0:T(8,128)S(1)}, u32[]{:S(2)}, u32[]{:S(2)}) async-start(f32[16,88,128]{2,1,0:T(8,128)} %shard_map.114), calls=%async_computation | async-start | bytes 1441792 | tf_op jit(solution)/shard_map/all_to_all | solution.py:468
  27.0 0.0 copy-start
  27.1 0.0 copy-done.1
  27.1 0.0 copy-done.2
  27.1 0.7 %copy-done = f32[64,40]{0,1:T(8,128)S(1)} copy-done((f32[64,40]{0,1:T(8,128)S(1)}, f32[64,40]{0,1:T(8,128)}, u32[]{:S(2)}) %copy-start) | copy-done | bytes 10264
  27.8 0.1 pad_maximum_fusion.entry_ref
  27.9 0.1 fusion.3.mask_ref
  28.0 6.0 %shard_map.115 = (f32[128,1280]{1,0:T(8,128)S(1)}, f32[128,1280]{1,0:T(8,128)S(1)}, f32[128,1280]{1,0:T(8,128)S(1)}) custom-call(bf16[128,1280]{1,0:T(8,128)(2,1)} %refs_0_.3, bf16[128,1280]{1,0:T(8,128)(2,1)} %refs_1_.3, bf16[128,1280]{1,0:T(8,128)(2,1)} %refs_2_.3, bf16[128,1280]{1,0:T(8,128)(2,1)} %refs_3_.3, bf16[128,1280]{1,0:T(8,128)(2,1)} %refs_4_.3, ...), custom_call_target="tpu_custom_call" | custom-call | tf_op jit(solution)/shard_map/pallas_call | solution.py:470
  34.0 5.9 %all-to-all-done.slots_ref = f32[16,88,128]{2,1,0:T(8,128)S(1)} async-done(((f32[16,88,128]{2,1,0:T(8,128)}), f32[16,88,128]{2,1,0:T(8,128)S(1)}, u32[]{:S(2)}, u32[]{:S(2)}) %all-to-all-start) | async-done | bytes 720928 | tf_op jit(solution)/shard_map/all_to_all | solution.py:468
  39.9 2.7 %shard_map.116 = (f32[32,24,128]{2,1,0:T(8,128)}, f32[48,128]{1,0:T(8,128)S(1)}) custom-call(f32[16,88,128]{2,1,0:T(8,128)S(1)} %all-to-all-done.slots_ref, f32[48,128]{1,0:T(8,128)S(1)} %pad_maximum_fusion.entry_ref, f32[48,128]{1,0:T(8,128)S(1)} %fusion.3.mask_ref, f32[128,1280]{1,0:T(8,128)S(1)} %get-tuple-element.13.after_ref.base_ref), custom_call_target="tpu_custom_call" | custom-call | tf_op jit(solution)/shard_map/pallas_call | solution.py:482
  42.7 0.0 copy-start.3
  42.7 5.0 %all-to-all-start.1 = ((f32[32,24,128]{2,1,0:T(8,128)}), f32[32,24,128]{2,1,0:T(8,128)S(1)}, u32[]{:S(2)}, u32[]{:S(2)}) async-start(f32[32,24,128]{2,1,0:T(8,128)} %get-tuple-element.14), calls=%async_computation.1 | async-start | bytes 786432 | tf_op jit(solution)/shard_map/all_to_all | solution.py:492
  47.7 0.0 copy-done.3
  47.8 0.6 %slice_bitcast_fusion = f32[64,40]{0,1:T(8,128)} fusion(f32[48,128]{1,0:T(8,128)S(1)} %get-tuple-element.17), kind=kLoop, calls=%fused_computation.10 | loop fusion | bytes 20480 | tf_op jit(solution)/shard_map/transpose | solution.py:493
  48.4 9.7 %all-to-all-done.1.starts_ref = f32[32,24,128]{2,1,0:T(8,128)S(1)} async-done(((f32[32,24,128]{2,1,0:T(8,128)}), f32[32,24,128]{2,1,0:T(8,128)S(1)}, u32[]{:S(2)}, u32[]{:S(2)}) %all-to-all-start.1) | async-done | bytes 393248 | tf_op jit(solution)/shard_map/all_to_all | solution.py:492
  58.0 1.9 %shard_map.117 = bf16[128,1280]{1,0:T(8,128)(2,1)} custom-call(f32[32,24,128]{2,1,0:T(8,128)S(1)} %all-to-all-done.1.starts_ref, f32[128,1280]{1,0:T(8,128)S(1)} %get-tuple-element.15.read_ref, f32[128,1280]{1,0:T(8,128)S(1)} %get-tuple-element.16.local_ref, f32[128,1280]{1,0:T(8,128)S(1)} %get-tuple-element.13.after_ref.base_ref, ...), custom_call_target="tpu_custom_call" | custom-call | tf_op jit(solution)/shard_map/pallas_call | solution.py:495
  (9 shorter events, 0.1 us)
Async XLA Ops:
  10.9 10.5 %collective-permute-start = (f32[2,10,64,128]{3,2,1,0:T(8,128)S(1)}, f32[2,10,64,128]{3,2,1,0:T(8,128)S(1)}, u32[]{:S(2)}, u32[]{:S(2)}) collective-permute-start(f32[2,10,64,128]{3,2,1,0:T(8,128)S(1)} %get-tuple-element.10.mine_ref), channel_id=1, source_target_pairs={{0,1},{1,0},{2,3},{3,2},{4,5},{5,4},{6,7},{7,6},{8,9},{9,8},{10,11... | collective-permute-start | bytes 1966088 | tf_op jit(solution)/shard_map/ppermute | solution.py:459
  23.1 4.0 %copy-start.1 = (f32[1280]{0:T(1024)S(1)}, f32[1280]{0:T(1024)}, u32[]{:S(2)}) copy-start(f32[1280]{0:T(1024)} %param.17) | copy-start | bytes 15364
  23.1 4.0 %copy-start.2 = (f32[1280]{0:T(1024)S(1)}, f32[1280]{0:T(1024)}, u32[]{:S(2)}) copy-start(f32[1280]{0:T(1024)} %param.19) | copy-start | bytes 15364
  23.1 16.8 %all-to-all-start = ((f32[16,88,128]{2,1,0:T(8,128)}), f32[16,88,128]{2,1,0:T(8,128)S(1)}, u32[]{:S(2)}, u32[]{:S(2)}) async-start(f32[16,88,128]{2,1,0:T(8,128)} %shard_map.114), calls=%async_computation | async-start | bytes 1441792 | tf_op jit(solution)/shard_map/all_to_all | solution.py:468
  27.0 0.7 %copy-start = (f32[64,40]{0,1:T(8,128)S(1)}, f32[64,40]{0,1:T(8,128)}, u32[]{:S(2)}) copy-start(f32[64,40]{0,1:T(8,128)} %param.16) | copy-start | bytes 30724
  42.7 5.1 %copy-start.3 = (f32[1280]{0:T(1024)S(1)}, f32[1280]{0:T(1024)}, u32[]{:S(2)}) copy-start(f32[1280]{0:T(1024)} %param.18) | copy-start | bytes 15364
  42.7 15.3 %all-to-all-start.1 = ((f32[32,24,128]{2,1,0:T(8,128)}), f32[32,24,128]{2,1,0:T(8,128)S(1)}, u32[]{:S(2)}, u32[]{:S(2)}) async-start(f32[32,24,128]{2,1,0:T(8,128)} %get-tuple-element.14), calls=%async_computation.1 | async-start | bytes 786432 | tf_op jit(solution)/shard_map/all_to_all | solution.py:492

commit v6 on v2

--- a/solution.py
+++ b/solution.py
@@ -82,10 +82,11 @@
 
 
 def grams(left, right, low):
-    zero = jnp.zeros_like(left)
-    stacked = split(rows(jnp.where(low, left, zero), jnp.where(low, zero, left)))
+    first = jnp.where(low, 1.0, 0.0).astype(BF16)
+    second = jnp.where(low, 0.0, 1.0).astype(BF16)
+    hi, lo = (rows(x * first, x * second) for x in split(left))
     b = split(right)
-    return mxu(lanes(*stacked), lanes(b[0], b[0]), NT) + mxu(stacked[0], b[1], NT)
+    return mxu(lanes(hi, lo), lanes(b[0], b[0]), NT) + mxu(hi, b[1], NT)
 
 
 def inverse(inner):
@@ -139,9 +140,9 @@
 
 
 def local_kernel(*refs):
-    inputs, (pieces_out, w_out, u_out) = refs[:5], refs[5:8]
+    inputs, (pieces, w_out, u_out) = refs[:5], refs[5:8]
     buffers = refs[8:13]
-    pieces, w_all, u_all, in_sems, out_sems = refs[13:]
+    w_all, u_all, in_sems, out_sems = refs[13:]
     n, width = w_all.shape
     block = GROUP * PAIR
     groups = width // block
@@ -153,8 +154,8 @@
         for g in range(groups)
     ]
     for group in loads:
-        for copy in group:
-            copy.start()
+        for i in (4, 2, 3, 0, 1):
+            group[i].start()
     k_ref, v_ref, raw_ref, rate_ref, log_ref = buffers
     low = low_half(n)
     ones = block_ones()
@@ -165,14 +166,17 @@
     pairs = range(GROUP)
     heads = range(2 * GROUP)
     for g in range(groups):
-        for copy in loads[g]:
-            copy.wait()
         cut = [slice(g * block + p * PAIR, g * block + (p + 1) * PAIR) for p in pairs]
+        loads[g][4].wait()
         cumul = [decays(log_ref[:, c], tril) for c in cut]
+        rise = [jnp.exp(cumul[p] - log_ref[:, cut[p]].astype(F32)) for p in pairs]
+        fall = [jnp.exp(-cumul[p]) for p in pairs]
+        loads[g][2].wait()
         unit = [units(raw_ref[:, c], ones) for c in cut]
-        alpha = [-unit[p] * jnp.exp(cumul[p] - log_ref[:, cut[p]].astype(F32)) for p in pairs]
-        fall = [jnp.exp(-cumul[p]) for p in pairs]
+        alpha = [-unit[p] * x for p, x in zip(pairs, rise)]
+        loads[g][3].wait()
         beta = [rate_ref[:, cut[p]].astype(F32) * unit[p] * fall[p] for p in pairs]
+        loads[g][0].wait()
         key = [k_ref[:, cut[p]].astype(F32) * fall[p] for p in pairs]
         gram = [grams(alpha[p], rows(beta[p], key[p]), low) for p in pairs]
 
@@ -181,6 +185,7 @@
             part = gram[h // 2][(h % 2) * n : (h % 2 + 1) * n]
             inner.append(jnp.where(strict, part[:, :n], 0.0))
             cross.append(jnp.where(strict, part[:, n:], 0.0))
+        loads[g][1].wait()
         akv = [exact_right(split(cross[h]), v_ref[:, cut[h // 2]]) for h in heads]
         akv = [jnp.where(low, akv[2 * p], akv[2 * p + 1]) for p in pairs]
         right = [split(lanes(alpha[p], akv[p])) for p in pairs]
@@ -192,6 +197,15 @@
             u = jnp.where(low, first[:, PAIR:], second[:, PAIR:])
             w_all[:, cut[p]] = w
             u_all[:, cut[p]] = u
+        here = pl.ds(g * block, block)
+        stores += [
+            pltpu.make_async_copy(w_all.at[:, here], w_out.at[:, here], out_sems.at[g, 0]),
+            pltpu.make_async_copy(u_all.at[:, here], u_out.at[:, here], out_sems.at[g, 1]),
+        ]
+        for copy in stores[-2:]:
+            copy.start()
+        for p in pairs:
+            w, u = w_all[:, cut[p]], u_all[:, cut[p]]
             scale = jnp.exp(cumul[p][n - 1 :, :])
             end_b = beta[p] * scale
             end_k = key[p] * scale
@@ -202,16 +216,6 @@
             by_key = mxu(content, lanes(*split(end_k)))
             fresh = square(split(u.T), split(end_b)) + by_key[:, :PAIR] + by_key[:, PAIR:]
             pieces[1, g * GROUP + p] = jnp.where(low_half(CH), fresh[:CH], fresh[CH:])
-
-        here = pl.ds(g * block, block)
-        ready = pl.ds(g * GROUP, GROUP)
-        stores += [
-            pltpu.make_async_copy(pieces.at[:, ready], pieces_out.at[:, ready], out_sems.at[g, 0]),
-            pltpu.make_async_copy(w_all.at[:, here], w_out.at[:, here], out_sems.at[g, 1]),
-            pltpu.make_async_copy(u_all.at[:, here], u_out.at[:, here], out_sems.at[g, 2]),
-        ]
-        for copy in stores[-3:]:
-            copy.start()
     for copy in stores:
         copy.wait()
 
@@ -230,13 +234,15 @@
     late = late_ref[...] > 0.5
     low = low_half(CH)
     short = (columns + 15) // 16 * 8
-    for p in range(PAIRS):
-        mine, other = mine_ref[0, p], other_ref[0, p]
-        first, second = jnp.where(late, other, mine), jnp.where(late, mine, other)
-        moves[p] = square(split(second), split(diagonal_blocks(first)))
-        mine, other = mine_ref[1, p], other_ref[1, p]
-        first, end = jnp.where(late, other, mine), jnp.where(late, mine, other)
-        end = end + square_nt(split(first), split(diagonal_blocks(second)))
+    pairs = range(PAIRS)
+    first = [jnp.where(late, other_ref[0, p], mine_ref[0, p]) for p in pairs]
+    second = [jnp.where(late, mine_ref[0, p], other_ref[0, p]) for p in pairs]
+    moved = [square(split(y), split(diagonal_blocks(x))) for x, y in zip(first, second)]
+    first = [jnp.where(late, other_ref[1, p], mine_ref[1, p]) for p in pairs]
+    carried = [square_nt(split(x), split(diagonal_blocks(y))) for x, y in zip(first, second)]
+    for p in pairs:
+        moves[p] = moved[p]
+        end = carried[p] + jnp.where(late, mine_ref[1, p], other_ref[1, p])
         turned = pltpu.roll(end, CH, 1)
         ends[p * PAIR : p * PAIR + CH, :] = jnp.where(low, end, turned)
         ends[p * PAIR + CH : (p + 1) * PAIR, :] = jnp.where(low, turned, end)
@@ -328,40 +334,48 @@
     count, short = slots_ref.shape[0], starts.shape[1]
     low = low_half(short)
     mask = mask_ref[...]
-    state = entry_ref[...]
-    chunk = count // sems.shape[0]
-    stores = []
-    for d in range(count):
-        starts[2 * d] = starts[2 * d + 1] = jnp.where(low, state[:short], state[short:])
-        if d % chunk == chunk - 1:
-            part = pl.ds(2 * (d + 1 - chunk), 2 * chunk)
-            stores.append(pltpu.make_async_copy(starts.at[part], starts_out.at[part], sems.at[d // chunk]))
-            stores[-1].start()
-        hi, lo = split(slots_ref[d, :CH, :])
-        weights = rows(lanes(hi, hi), lanes(hi, hi), lanes(lo, lo), lanes(lo, lo))
+
+    def weights(move):
+        hi, lo = move
+        return rows(lanes(hi, hi), lanes(hi, hi), lanes(lo, lo), lanes(lo, lo))
+
+    def advance(state, move, fresh):
+        out = mxu(lanes(*split(state * mask)), move, NT)
+        return out[:, :PAIR] + out[:, PAIR:] + fresh
+
+    def unpacked(d):
         end = slots_ref[d, CH:, :]
         turned = pltpu.roll(end, CH, 1)
-        fresh = rows(jnp.where(low, end, turned), jnp.where(low, turned, end))
-        out = mxu(lanes(*split(state * mask)), weights, NT)
-        state = out[:, :PAIR] + out[:, PAIR:] + fresh
+        return rows(jnp.where(low, end, turned), jnp.where(low, turned, end))
+
+    parts = [split(slots_ref[d, :CH, :]) for d in range(count)]
+    moves = [weights(x) for x in parts]
+    fresh = [unpacked(d) for d in range(count)]
+    both = [
+        weights(split(square(parts[d + 1], split(diagonal_blocks(slots_ref[d, :CH, :])))))
+        for d in range(0, count, 2)
+    ]
+    joint = [advance(fresh[d], moves[d + 1], fresh[d + 1]) for d in range(0, count, 2)]
+    state = entry_ref[...]
+    stores = []
+    for d in range(count // 2):
+        following = advance(state, both[d], joint[d])
+        middle = advance(state, moves[2 * d], fresh[2 * d])
+        for i, x in enumerate((state, middle)):
+            at = 4 * d + 2 * i
+            starts[at] = starts[at + 1] = jnp.where(low, x[:short], x[short:])
+        part = pl.ds(4 * d, 4)
+        stores.append(pltpu.make_async_copy(starts.at[part], starts_out.at[part], sems.at[d]))
+        stores[-1].start()
+        state = following
     exit_ref[...] = state
     for copy in stores:
         copy.wait()
 
 
-def final_kernel(starts_ref, read_in, local_in, base_in, gain_ref, out, *scratch, columns):
-    buffers, (begins, result, in_sems, out_sems) = scratch[:3], scratch[3:]
-    read_ref, local_ref, base_ref = buffers
+def final_kernel(starts_ref, read_ref, local_ref, base_ref, gain_ref, out, begins, result, out_sems, *, columns):
     cut = [slice(p * PAIR, (p + 1) * PAIR) for p in range(PAIRS)]
     place = [pl.ds(p * PAIR, PAIR) for p in range(PAIRS)]
-    block = GROUP * PAIR
-    loads = []
-    for g in range(WIDTH // block):
-        here = pl.ds(g * block, block)
-        for i, (src, dst) in enumerate(zip((read_in, local_in, base_in), buffers)):
-            loads.append(pltpu.make_async_copy(src.at[:, here], dst.at[:, here], in_sems.at[g, i]))
-    for copy in loads:
-        copy.start()
     short = starts_ref.shape[1]
     low = low_half(short)
     for owner in range(starts_ref.shape[0]):
@@ -375,8 +389,6 @@
     right = [split(jnp.where(own, begins[c, :], 0.0)) for c in cut]
     stores = []
     for g in range(PAIRS // GROUP):
-        for copy in loads[3 * g : 3 * g + 3]:
-            copy.wait()
         pairs = range(g * GROUP, (g + 1) * GROUP)
         left = [split(read_ref[:, cut[p]]) for p in pairs]
         carried = [
@@ -407,8 +419,10 @@
     short = (columns + 15) // 16 * 8
     groups = PAIRS // GROUP
     hbm = pl.BlockSpec(memory_space=pltpu.HBM)
+    held = functools.partial(pltpu.with_memory_space_constraint, memory_space=pltpu.HBM)
     vmem = pl.BlockSpec(memory_space=pltpu.VMEM)
-    plane = jax.ShapeDtypeStruct((n, WIDTH), F32)
+    plane = pltpu.HBM((n, WIDTH), F32)
+    arrays = [held(x) for x in (q, k, v, raw, rates, logs)]
     tokens = pltpu.VMEM((n, WIDTH), BF16)
     floats = pltpu.VMEM((n, WIDTH), F32)
     sems = pltpu.SemaphoreType.DMA
@@ -417,11 +431,11 @@
     mine, w, u = call(
         local_kernel,
         in_specs=[hbm] * 5,
-        out_specs=[hbm] * 3,
+        out_specs=[vmem, hbm, hbm],
         out_shape=[jax.ShapeDtypeStruct(pieces, F32), plane, plane],
         scratch_shapes=[tokens] * 5
-        + [pltpu.VMEM(pieces, F32), floats, floats, sems((groups, 5)), sems((groups, 3))],
-    )(k, v, raw, rates, logs)
+        + [floats, floats, sems((groups, 5)), sems((groups, 2))],
+    )(*arrays[1:])
     other = lax.ppermute(mine, "ctx", [(i, i ^ 1) for i in range(owners)])
     place = lax.axis_index("ctx")
     late = jnp.broadcast_to((place % 2).astype(F32), (1, PAIR))
@@ -437,9 +451,9 @@
         read_kernel,
         in_specs=[hbm] * 8 + [vmem] * 4,
         out_specs=[hbm] * 3,
-        out_shape=[plane] * 3,
+        out_shape=[jax.ShapeDtypeStruct((n, WIDTH), F32)] * 3,
         scratch_shapes=[tokens] * 6 + [floats] * 5 + [sems((groups, 8)), sems((groups, 3))],
-    )(q, k, v, raw, rates, logs, w, u, boost.reshape(1, WIDTH), shift.reshape(1, WIDTH), other, late)
+    )(*arrays, held(w), held(u), boost.reshape(1, WIDTH), shift.reshape(1, WIDTH), other, late)
 
     own = lax.broadcasted_iota(jnp.int32, (2 * short, PAIR), 0)
     half = lax.broadcasted_iota(jnp.int32, (2 * short, PAIR), 1) // CH
@@ -450,21 +464,20 @@
         in_specs=[vmem, vmem, vmem, hbm],
         out_specs=[hbm, vmem],
         out_shape=[
-            jax.ShapeDtypeStruct((owners, short, PAIR), F32),
+            pltpu.HBM((owners, short, PAIR), F32),
             jax.ShapeDtypeStruct((2 * short, PAIR), F32),
         ],
-        scratch_shapes=[pltpu.VMEM((owners, short, PAIR), F32), sems((4,))],
+        scratch_shapes=[pltpu.VMEM((owners, short, PAIR), F32), sems((owners // 4,))],
     )(slots, jnp.concatenate([entry, entry], axis=1), mask.astype(F32), base)
     starts = lax.all_to_all(starts, "ctx", 0, 0)
     exit_state = final[:columns, :CH].T
 
     out = call(
         functools.partial(final_kernel, columns=columns),
-        in_specs=[vmem, hbm, hbm, hbm, vmem],
+        in_specs=[vmem] * 5,
         out_specs=hbm,
-        out_shape=jax.ShapeDtypeStruct((n, WIDTH), BF16),
-        scratch_shapes=[floats] * 3
-        + [pltpu.VMEM((WIDTH, PAIR), F32), tokens, sems((groups, 3)), sems((PAIRS,))],
+        out_shape=pltpu.HBM((n, WIDTH), BF16),
+        scratch_shapes=[pltpu.VMEM((WIDTH, PAIR), F32), tokens, sems((PAIRS,))],
     )(starts, read, local, base, gain.reshape(1, WIDTH))
     return out, exit_state
 

time: 67.1 us -> 60.4 us (0.900)
  local copies, waits for them, and re-layouts: 13.7 us -> 1.31 us
  waiting for transfers between devices: 12.5 us -> 17.3 us
  Pallas kernels: 19.9 us -> 22.5 us
  starting transfers between devices: 19 us -> 17.7 us
    unnamed x46 -> x8, local copies, waits for them, and re-layouts: 13.1 us -> 0.68 us
    all_to_all x1, waiting for transfers between devices: 1.23 us -> 5.91 us  [shards(): slots = lax.all_to_all(slots, 'ctx', 0, 0, axis_index_groups=same_core)]
    pallas_call x2, Pallas kernels: 10.8 us -> 12.5 us  [the longest x1 10.6 us: shards(): call(local_kernel, in_specs=[hbm] * 5, out_specs=[vmem, hbm, hbm], out_sh...]
    all_to_all x1, starting transfers between devices: 6.31 us -> 5.04 us  [shards(): starts = lax.all_to_all(starts, 'ctx', 0, 0)]
    pallas_call x1, Pallas kernels: 4.82 us -> 6 us  [shards(): call(read_kernel, in_specs=[hbm] * 8 + [vmem] * 4, out_specs=[hbm] * 3, o...]
  transfers between devices with their start and end apart: 3 -> 3, of which waited for: 3 -> 3; matrix products, arithmetic and copies ran while one was open for 1% -> 1% of each run, Pallas kernels for 7% -> 10%
where the time goes in v6:
time: 60.4 us; the launch traced here: 59.9 us
  Pallas kernels  22.5 us (37%)
  starting transfers between devices  17.7 us (29%)
  waiting for transfers between devices  17.3 us (29%)
  local copies, waits for them, and re-layouts  1.31 us (2%)
  between operations  0.94 us (2%)
    pallas_call x1, Pallas kernels, shards(): call(local_kernel, in_specs=[hbm] * 5, out_specs=[vmem, hbm, hbm], out_sh...  10.6 us
    all_to_all x1, waiting for transfers between devices, shards(): starts = lax.all_to_all(starts, 'ctx', 0, 0)  9.65 us
    ppermute x1, starting transfers between devices, shards(): other = lax.ppermute(mine, 'ctx', [(i, i ^ 1) for i in range(owners)])  8.79 us
    pallas_call x1, Pallas kernels, shards(): call(read_kernel, in_specs=[hbm] * 8 + [vmem] * 4, out_specs=[hbm] * 3, o...  6 us
    all_to_all x1, waiting for transfers between devices, shards(): slots = lax.all_to_all(slots, 'ctx', 0, 0, axis_index_groups=same_core)  5.91 us
    all_to_all x1, starting transfers between devices, shards(): starts = lax.all_to_all(starts, 'ctx', 0, 0)  5.04 us
    all_to_all x1, starting transfers between devices, shards(): slots = lax.all_to_all(slots, 'ctx', 0, 0, axis_index_groups=same_core)  3.91 us
    pallas_call x1, Pallas kernels, shards(): call(scan_kernel, in_specs=[vmem, vmem, vmem, hbm], out_specs=[hbm, vmem]...  2.25 us
  transfers between devices with their start and end apart: 3, of which 3 were waited for; matrix products, arithmetic and copies ran while one was open for 1% of the time, Pallas kernels for 10%

profile of v6, /device:TPU:1, one launch (start us, length us, event | category | flops | bytes accessed | tf_op | source)
XLA Modules:
  0.0 59.9 jit_solution(111795413634402677)
XLA Ops:
  0.6 10.6 %shard_map.113 = (f32[2,10,64,128]{3,2,1,0:T(8,128)S(1)}, f32[128,1280]{1,0:T(8,128)}, f32[128,1280]{1,0:T(8,128)}) custom-call(bf16[128,1280]{1,0:T(8,128)(2,1)} %refs_1_.3, bf16[128,1280]{1,0:T(8,128)(2,1)} %refs_2_.3, bf16[128,1280]{1,0:T(8,128)(2,1)} %refs_3_.3, bf16[128,1280]{1,0:T(8,128)(2,1)} %refs_4_.3, bf16[128,1280]{1,0:T(8,128)(2,1)} %refs_5_.1), custom_call_target="tpu_custom_call" | custom-call | tf_op jit(solution)/shard_map/pallas_call | solution.py:431
  11.3 8.8 %collective-permute-start = (f32[2,10,64,128]{3,2,1,0:T(8,128)S(1)}, f32[2,10,64,128]{3,2,1,0:T(8,128)S(1)}, u32[]{:S(2)}, u32[]{:S(2)}) collective-permute-start(f32[2,10,64,128]{3,2,1,0:T(8,128)S(1)} %get-tuple-element.10.mine_ref), channel_id=1, source_target_pairs={{0,1},{1,0},{2,3},{3,2},{4,5},{5,4},{6,7},{7,6},{8,9},{9,8},{10,11... | collective-permute-start | bytes 1966088 | tf_op jit(solution)/shard_map/ppermute | solution.py:439
  20.1 1.7 %collective-permute-done.other_ref.refs_10_ = f32[2,10,64,128]{3,2,1,0:T(8,128)S(1)} collective-permute-done((f32[2,10,64,128]{3,2,1,0:T(8,128)S(1)}, f32[2,10,64,128]{3,2,1,0:T(8,128)S(1)}, u32[]{:S(2)}, u32[]{:S(2)}) %collective-permute-start) | collective-permute-done | bytes 655392 | tf_op jit(solution)/shard_map/ppermute | solution.py:439
  21.8 1.7 %shard_map.114 = f32[16,88,128]{2,1,0:T(8,128)} custom-call(f32[2,10,64,128]{3,2,1,0:T(8,128)S(1)} %get-tuple-element.10.mine_ref, f32[2,10,64,128]{3,2,1,0:T(8,128)S(1)} %collective-permute-done.other_ref.refs_10_, f32[1,128]{1,0:T(1,128)S(1)} %broadcast_in_dim.3.late_ref.refs_11_), custom_call_target="tpu_custom_call" | custom-call | tf_op jit(solution)/shard_map/pallas_call | solution.py:442
  23.5 0.0 copy-start.1
  23.5 0.0 copy-start.2
  23.5 3.9 %all-to-all-start = ((f32[16,88,128]{2,1,0:T(8,128)}), f32[16,88,128]{2,1,0:T(8,128)S(1)}, u32[]{:S(2)}, u32[]{:S(2)}) async-start(f32[16,88,128]{2,1,0:T(8,128)} %shard_map.114), calls=%async_computation | async-start | bytes 1441792 | tf_op jit(solution)/shard_map/all_to_all | solution.py:448
  27.4 0.0 copy-start
  27.4 0.0 copy-done.1
  27.5 0.0 copy-done.2
  27.5 0.7 %copy-done = f32[64,40]{0,1:T(8,128)S(1)} copy-done((f32[64,40]{0,1:T(8,128)S(1)}, f32[64,40]{0,1:T(8,128)}, u32[]{:S(2)}) %copy-start) | copy-done | bytes 10264
  28.2 0.1 pad_maximum_fusion.entry_ref
  28.3 0.1 fusion.3.mask_ref
  28.4 6.0 %shard_map.115 = (f32[128,1280]{1,0:T(8,128)S(1)}, f32[128,1280]{1,0:T(8,128)S(1)}, f32[128,1280]{1,0:T(8,128)S(1)}) custom-call(bf16[128,1280]{1,0:T(8,128)(2,1)} %refs_0_.3, bf16[128,1280]{1,0:T(8,128)(2,1)} %refs_1_.3, bf16[128,1280]{1,0:T(8,128)(2,1)} %refs_2_.3, bf16[128,1280]{1,0:T(8,128)(2,1)} %refs_3_.3, bf16[128,1280]{1,0:T(8,128)(2,1)} %refs_4_.3, ...), custom_call_target="tpu_custom_call" | custom-call | tf_op jit(solution)/shard_map/pallas_call | solution.py:450
  34.4 5.9 %all-to-all-done.slots_ref = f32[16,88,128]{2,1,0:T(8,128)S(1)} async-done(((f32[16,88,128]{2,1,0:T(8,128)}), f32[16,88,128]{2,1,0:T(8,128)S(1)}, u32[]{:S(2)}, u32[]{:S(2)}) %all-to-all-start) | async-done | bytes 720928 | tf_op jit(solution)/shard_map/all_to_all | solution.py:448
  40.3 2.3 %shard_map.116 = (f32[32,24,128]{2,1,0:T(8,128)}, f32[48,128]{1,0:T(8,128)S(1)}) custom-call(f32[16,88,128]{2,1,0:T(8,128)S(1)} %all-to-all-done.slots_ref, f32[48,128]{1,0:T(8,128)S(1)} %pad_maximum_fusion.entry_ref, f32[48,128]{1,0:T(8,128)S(1)} %fusion.3.mask_ref, f32[128,1280]{1,0:T(8,128)S(1)} %get-tuple-element.13.after_ref.base_ref), custom_call_target="tpu_custom_call" | custom-call | tf_op jit(solution)/shard_map/pallas_call | solution.py:462
  42.6 0.0 copy-start.3
  42.6 5.0 %all-to-all-start.1 = ((f32[32,24,128]{2,1,0:T(8,128)}), f32[32,24,128]{2,1,0:T(8,128)S(1)}, u32[]{:S(2)}, u32[]{:S(2)}) async-start(f32[32,24,128]{2,1,0:T(8,128)} %get-tuple-element.14), calls=%async_computation.1 | async-start | bytes 786432 | tf_op jit(solution)/shard_map/all_to_all | solution.py:472
  47.6 0.0 copy-done.3
  47.6 0.6 %slice_bitcast_fusion = f32[64,40]{0,1:T(8,128)} fusion(f32[48,128]{1,0:T(8,128)S(1)} %get-tuple-element.17), kind=kLoop, calls=%fused_computation.10 | loop fusion | bytes 20480 | tf_op jit(solution)/shard_map/transpose | solution.py:473
  48.3 9.7 %all-to-all-done.1.starts_ref = f32[32,24,128]{2,1,0:T(8,128)S(1)} async-done(((f32[32,24,128]{2,1,0:T(8,128)}), f32[32,24,128]{2,1,0:T(8,128)S(1)}, u32[]{:S(2)}, u32[]{:S(2)}) %all-to-all-start.1) | async-done | bytes 393248 | tf_op jit(solution)/shard_map/all_to_all | solution.py:472
  57.9 1.9 %shard_map.117 = bf16[128,1280]{1,0:T(8,128)(2,1)} custom-call(f32[32,24,128]{2,1,0:T(8,128)S(1)} %all-to-all-done.1.starts_ref, f32[128,1280]{1,0:T(8,128)S(1)} %get-tuple-element.15.read_ref, f32[128,1280]{1,0:T(8,128)S(1)} %get-tuple-element.16.local_ref, f32[128,1280]{1,0:T(8,128)S(1)} %get-tuple-element.13.after_ref.base_ref, ...), custom_call_target="tpu_custom_call" | custom-call | tf_op jit(solution)/shard_map/pallas_call | solution.py:475
  (9 shorter events, 0.1 us)
Async XLA Ops:
  11.3 10.5 %collective-permute-start = (f32[2,10,64,128]{3,2,1,0:T(8,128)S(1)}, f32[2,10,64,128]{3,2,1,0:T(8,128)S(1)}, u32[]{:S(2)}, u32[]{:S(2)}) collective-permute-start(f32[2,10,64,128]{3,2,1,0:T(8,128)S(1)} %get-tuple-element.10.mine_ref), channel_id=1, source_target_pairs={{0,1},{1,0},{2,3},{3,2},{4,5},{5,4},{6,7},{7,6},{8,9},{9,8},{10,11... | collective-permute-start | bytes 1966088 | tf_op jit(solution)/shard_map/ppermute | solution.py:439
  23.5 4.0 %copy-start.1 = (f32[1280]{0:T(1024)S(1)}, f32[1280]{0:T(1024)}, u32[]{:S(2)}) copy-start(f32[1280]{0:T(1024)} %param.17) | copy-start | bytes 15364
  23.5 4.0 %copy-start.2 = (f32[1280]{0:T(1024)S(1)}, f32[1280]{0:T(1024)}, u32[]{:S(2)}) copy-start(f32[1280]{0:T(1024)} %param.19) | copy-start | bytes 15364
  23.5 16.8 %all-to-all-start = ((f32[16,88,128]{2,1,0:T(8,128)}), f32[16,88,128]{2,1,0:T(8,128)S(1)}, u32[]{:S(2)}, u32[]{:S(2)}) async-start(f32[16,88,128]{2,1,0:T(8,128)} %shard_map.114), calls=%async_computation | async-start | bytes 1441792 | tf_op jit(solution)/shard_map/all_to_all | solution.py:448
  27.4 0.7 %copy-start = (f32[64,40]{0,1:T(8,128)S(1)}, f32[64,40]{0,1:T(8,128)}, u32[]{:S(2)}) copy-start(f32[64,40]{0,1:T(8,128)} %param.16) | copy-start | bytes 30724
  42.6 5.1 %copy-start.3 = (f32[1280]{0:T(1024)S(1)}, f32[1280]{0:T(1024)}, u32[]{:S(2)}) copy-start(f32[1280]{0:T(1024)} %param.18) | copy-start | bytes 15364
  42.6 15.3 %all-to-all-start.1 = ((f32[32,24,128]{2,1,0:T(8,128)}), f32[32,24,128]{2,1,0:T(8,128)S(1)}, u32[]{:S(2)}, u32[]{:S(2)}) async-start(f32[32,24,128]{2,1,0:T(8,128)} %get-tuple-element.14), calls=%async_computation.1 | async-start | bytes 786432 | tf_op jit(solution)/shard_map/all_to_all | solution.py:472

commit v7 on v6

--- a/solution.py
+++ b/solution.py
@@ -156,6 +156,9 @@
     for group in loads:
         for i in (4, 2, 3, 0, 1):
             group[i].start()
+    for group in loads:
+        for copy in group:
+            copy.wait()
     k_ref, v_ref, raw_ref, rate_ref, log_ref = buffers
     low = low_half(n)
     ones = block_ones()
@@ -167,16 +170,12 @@
     heads = range(2 * GROUP)
     for g in range(groups):
         cut = [slice(g * block + p * PAIR, g * block + (p + 1) * PAIR) for p in pairs]
-        loads[g][4].wait()
         cumul = [decays(log_ref[:, c], tril) for c in cut]
         rise = [jnp.exp(cumul[p] - log_ref[:, cut[p]].astype(F32)) for p in pairs]
         fall = [jnp.exp(-cumul[p]) for p in pairs]
-        loads[g][2].wait()
         unit = [units(raw_ref[:, c], ones) for c in cut]
         alpha = [-unit[p] * x for p, x in zip(pairs, rise)]
-        loads[g][3].wait()
         beta = [rate_ref[:, cut[p]].astype(F32) * unit[p] * fall[p] for p in pairs]
-        loads[g][0].wait()
         key = [k_ref[:, cut[p]].astype(F32) * fall[p] for p in pairs]
         gram = [grams(alpha[p], rows(beta[p], key[p]), low) for p in pairs]
 
@@ -185,7 +184,6 @@
             part = gram[h // 2][(h % 2) * n : (h % 2 + 1) * n]
             inner.append(jnp.where(strict, part[:, :n], 0.0))
             cross.append(jnp.where(strict, part[:, n:], 0.0))
-        loads[g][1].wait()
         akv = [exact_right(split(cross[h]), v_ref[:, cut[h // 2]]) for h in heads]
         akv = [jnp.where(low, akv[2 * p], akv[2 * p + 1]) for p in pairs]
         right = [split(lanes(alpha[p], akv[p])) for p in pairs]

time: 60.4 us -> 59.1 us (0.978)
  Pallas kernels: 22.5 us -> 21.2 us
    pallas_call x1, Pallas kernels: 10.6 us -> 9.39 us  [shards(): call(local_kernel, in_specs=[hbm] * 5, out_specs=[vmem, hbm, hbm], out_sh...]
where the time goes in v7:
time: 59.1 us; the launch traced here: 58.7 us
  Pallas kernels  21.2 us (36%)
  starting transfers between devices  17.7 us (30%)
  waiting for transfers between devices  17.3 us (29%)
  local copies, waits for them, and re-layouts  1.31 us (2%)
  between operations  0.94 us (2%)
    all_to_all x1, waiting for transfers between devices, shards(): starts = lax.all_to_all(starts, 'ctx', 0, 0)  9.65 us
    pallas_call x1, Pallas kernels, shards(): call(local_kernel, in_specs=[hbm] * 5, out_specs=[vmem, hbm, hbm], out_sh...  9.39 us
    ppermute x1, starting transfers between devices, shards(): other = lax.ppermute(mine, 'ctx', [(i, i ^ 1) for i in range(owners)])  8.78 us
    pallas_call x1, Pallas kernels, shards(): call(read_kernel, in_specs=[hbm] * 8 + [vmem] * 4, out_specs=[hbm] * 3, o...  6 us
    all_to_all x1, waiting for transfers between devices, shards(): slots = lax.all_to_all(slots, 'ctx', 0, 0, axis_index_groups=same_core)  5.91 us
    all_to_all x1, starting transfers between devices, shards(): starts = lax.all_to_all(starts, 'ctx', 0, 0)  5.05 us
    all_to_all x1, starting transfers between devices, shards(): slots = lax.all_to_all(slots, 'ctx', 0, 0, axis_index_groups=same_core)  3.91 us
    pallas_call x1, Pallas kernels, shards(): call(scan_kernel, in_specs=[vmem, vmem, vmem, hbm], out_specs=[hbm, vmem]...  2.25 us
  transfers between devices with their start and end apart: 3, of which 3 were waited for; matrix products, arithmetic and copies ran while one was open for 1% of the time, Pallas kernels for 10%

profile of v7, /device:TPU:1, one launch (start us, length us, event | category | flops | bytes accessed | tf_op | source)
XLA Modules:
  0.0 58.7 jit_solution(18015019351405854977)
XLA Ops:
  0.6 9.4 %shard_map.113 = (f32[2,10,64,128]{3,2,1,0:T(8,128)S(1)}, f32[128,1280]{1,0:T(8,128)}, f32[128,1280]{1,0:T(8,128)}) custom-call(bf16[128,1280]{1,0:T(8,128)(2,1)} %refs_1_.3, bf16[128,1280]{1,0:T(8,128)(2,1)} %refs_2_.3, bf16[128,1280]{1,0:T(8,128)(2,1)} %refs_3_.3, bf16[128,1280]{1,0:T(8,128)(2,1)} %refs_4_.3, bf16[128,1280]{1,0:T(8,128)(2,1)} %refs_5_.1), custom_call_target="tpu_custom_call" | custom-call | tf_op jit(solution)/shard_map/pallas_call | solution.py:429
  10.0 8.8 %collective-permute-start = (f32[2,10,64,128]{3,2,1,0:T(8,128)S(1)}, f32[2,10,64,128]{3,2,1,0:T(8,128)S(1)}, u32[]{:S(2)}, u32[]{:S(2)}) collective-permute-start(f32[2,10,64,128]{3,2,1,0:T(8,128)S(1)} %get-tuple-element.10.mine_ref), channel_id=1, source_target_pairs={{0,1},{1,0},{2,3},{3,2},{4,5},{5,4},{6,7},{7,6},{8,9},{9,8},{10,11... | collective-permute-start | bytes 1966088 | tf_op jit(solution)/shard_map/ppermute | solution.py:437
  18.8 1.7 %collective-permute-done.other_ref.refs_10_ = f32[2,10,64,128]{3,2,1,0:T(8,128)S(1)} collective-permute-done((f32[2,10,64,128]{3,2,1,0:T(8,128)S(1)}, f32[2,10,64,128]{3,2,1,0:T(8,128)S(1)}, u32[]{:S(2)}, u32[]{:S(2)}) %collective-permute-start) | collective-permute-done | bytes 655392 | tf_op jit(solution)/shard_map/ppermute | solution.py:437
  20.5 1.7 %shard_map.114 = f32[16,88,128]{2,1,0:T(8,128)} custom-call(f32[2,10,64,128]{3,2,1,0:T(8,128)S(1)} %get-tuple-element.10.mine_ref, f32[2,10,64,128]{3,2,1,0:T(8,128)S(1)} %collective-permute-done.other_ref.refs_10_, f32[1,128]{1,0:T(1,128)S(1)} %broadcast_in_dim.3.late_ref.refs_11_), custom_call_target="tpu_custom_call" | custom-call | tf_op jit(solution)/shard_map/pallas_call | solution.py:440
  22.2 0.0 copy-start.1
  22.2 0.0 copy-start.2
  22.2 3.9 %all-to-all-start = ((f32[16,88,128]{2,1,0:T(8,128)}), f32[16,88,128]{2,1,0:T(8,128)S(1)}, u32[]{:S(2)}, u32[]{:S(2)}) async-start(f32[16,88,128]{2,1,0:T(8,128)} %shard_map.114), calls=%async_computation | async-start | bytes 1441792 | tf_op jit(solution)/shard_map/all_to_all | solution.py:446
  26.2 0.0 copy-start
  26.2 0.0 copy-done.1
  26.2 0.0 copy-done.2
  26.2 0.7 %copy-done = f32[64,40]{0,1:T(8,128)S(1)} copy-done((f32[64,40]{0,1:T(8,128)S(1)}, f32[64,40]{0,1:T(8,128)}, u32[]{:S(2)}) %copy-start) | copy-done | bytes 10264
  26.9 0.1 pad_maximum_fusion.entry_ref
  27.0 0.1 fusion.3.mask_ref
  27.1 6.0 %shard_map.115 = (f32[128,1280]{1,0:T(8,128)S(1)}, f32[128,1280]{1,0:T(8,128)S(1)}, f32[128,1280]{1,0:T(8,128)S(1)}) custom-call(bf16[128,1280]{1,0:T(8,128)(2,1)} %refs_0_.3, bf16[128,1280]{1,0:T(8,128)(2,1)} %refs_1_.3, bf16[128,1280]{1,0:T(8,128)(2,1)} %refs_2_.3, bf16[128,1280]{1,0:T(8,128)(2,1)} %refs_3_.3, bf16[128,1280]{1,0:T(8,128)(2,1)} %refs_4_.3, ...), custom_call_target="tpu_custom_call" | custom-call | tf_op jit(solution)/shard_map/pallas_call | solution.py:448
  33.1 5.9 %all-to-all-done.slots_ref = f32[16,88,128]{2,1,0:T(8,128)S(1)} async-done(((f32[16,88,128]{2,1,0:T(8,128)}), f32[16,88,128]{2,1,0:T(8,128)S(1)}, u32[]{:S(2)}, u32[]{:S(2)}) %all-to-all-start) | async-done | bytes 720928 | tf_op jit(solution)/shard_map/all_to_all | solution.py:446
  39.0 2.2 %shard_map.116 = (f32[32,24,128]{2,1,0:T(8,128)}, f32[48,128]{1,0:T(8,128)S(1)}) custom-call(f32[16,88,128]{2,1,0:T(8,128)S(1)} %all-to-all-done.slots_ref, f32[48,128]{1,0:T(8,128)S(1)} %pad_maximum_fusion.entry_ref, f32[48,128]{1,0:T(8,128)S(1)} %fusion.3.mask_ref, f32[128,1280]{1,0:T(8,128)S(1)} %get-tuple-element.13.after_ref.base_ref), custom_call_target="tpu_custom_call" | custom-call | tf_op jit(solution)/shard_map/pallas_call | solution.py:460
  41.3 0.0 copy-start.3
  41.3 5.0 %all-to-all-start.1 = ((f32[32,24,128]{2,1,0:T(8,128)}), f32[32,24,128]{2,1,0:T(8,128)S(1)}, u32[]{:S(2)}, u32[]{:S(2)}) async-start(f32[32,24,128]{2,1,0:T(8,128)} %get-tuple-element.14), calls=%async_computation.1 | async-start | bytes 786432 | tf_op jit(solution)/shard_map/all_to_all | solution.py:470
  46.4 0.0 copy-done.3
  46.4 0.6 %slice_bitcast_fusion = f32[64,40]{0,1:T(8,128)} fusion(f32[48,128]{1,0:T(8,128)S(1)} %get-tuple-element.17), kind=kLoop, calls=%fused_computation.10 | loop fusion | bytes 20480 | tf_op jit(solution)/shard_map/transpose | solution.py:471
  47.0 9.7 %all-to-all-done.1.starts_ref = f32[32,24,128]{2,1,0:T(8,128)S(1)} async-done(((f32[32,24,128]{2,1,0:T(8,128)}), f32[32,24,128]{2,1,0:T(8,128)S(1)}, u32[]{:S(2)}, u32[]{:S(2)}) %all-to-all-start.1) | async-done | bytes 393248 | tf_op jit(solution)/shard_map/all_to_all | solution.py:470
  56.7 1.9 %shard_map.117 = bf16[128,1280]{1,0:T(8,128)(2,1)} custom-call(f32[32,24,128]{2,1,0:T(8,128)S(1)} %all-to-all-done.1.starts_ref, f32[128,1280]{1,0:T(8,128)S(1)} %get-tuple-element.15.read_ref, f32[128,1280]{1,0:T(8,128)S(1)} %get-tuple-element.16.local_ref, f32[128,1280]{1,0:T(8,128)S(1)} %get-tuple-element.13.after_ref.base_ref, ...), custom_call_target="tpu_custom_call" | custom-call | tf_op jit(solution)/shard_map/pallas_call | solution.py:473
  (9 shorter events, 0.1 us)
Async XLA Ops:
  10.0 10.5 %collective-permute-start = (f32[2,10,64,128]{3,2,1,0:T(8,128)S(1)}, f32[2,10,64,128]{3,2,1,0:T(8,128)S(1)}, u32[]{:S(2)}, u32[]{:S(2)}) collective-permute-start(f32[2,10,64,128]{3,2,1,0:T(8,128)S(1)} %get-tuple-element.10.mine_ref), channel_id=1, source_target_pairs={{0,1},{1,0},{2,3},{3,2},{4,5},{5,4},{6,7},{7,6},{8,9},{9,8},{10,11... | collective-permute-start | bytes 1966088 | tf_op jit(solution)/shard_map/ppermute | solution.py:437
  22.2 4.0 %copy-start.1 = (f32[1280]{0:T(1024)S(1)}, f32[1280]{0:T(1024)}, u32[]{:S(2)}) copy-start(f32[1280]{0:T(1024)} %param.17) | copy-start | bytes 15364
  22.2 4.0 %copy-start.2 = (f32[1280]{0:T(1024)S(1)}, f32[1280]{0:T(1024)}, u32[]{:S(2)}) copy-start(f32[1280]{0:T(1024)} %param.19) | copy-start | bytes 15364
  22.2 16.8 %all-to-all-start = ((f32[16,88,128]{2,1,0:T(8,128)}), f32[16,88,128]{2,1,0:T(8,128)S(1)}, u32[]{:S(2)}, u32[]{:S(2)}) async-start(f32[16,88,128]{2,1,0:T(8,128)} %shard_map.114), calls=%async_computation | async-start | bytes 1441792 | tf_op jit(solution)/shard_map/all_to_all | solution.py:446
  26.2 0.7 %copy-start = (f32[64,40]{0,1:T(8,128)S(1)}, f32[64,40]{0,1:T(8,128)}, u32[]{:S(2)}) copy-start(f32[64,40]{0,1:T(8,128)} %param.16) | copy-start | bytes 30724
  41.3 5.1 %copy-start.3 = (f32[1280]{0:T(1024)S(1)}, f32[1280]{0:T(1024)}, u32[]{:S(2)}) copy-start(f32[1280]{0:T(1024)} %param.18) | copy-start | bytes 15364
  41.3 15.3 %all-to-all-start.1 = ((f32[32,24,128]{2,1,0:T(8,128)}), f32[32,24,128]{2,1,0:T(8,128)S(1)}, u32[]{:S(2)}, u32[]{:S(2)}) async-start(f32[32,24,128]{2,1,0:T(8,128)} %get-tuple-element.14), calls=%async_computation.1 | async-start | bytes 786432 | tf_op jit(solution)/shard_map/all_to_all | solution.py:470
